TPU v7x, 32 devices: a whole 2x2x4 slice. The times are simulated.
32 devices in a mesh: dp: 8 (over y, x, core), shard: 4 (over z).
Axes of the slice: x: 2, y: 2, z: 4, core: 2. Of those that a mesh axis runs over, the one named last changes fastest.
Arguments:
- inputs: bfloat16 [16, 1024, 768], P('dp', 'shard'), may hold values from -6 to 6
- segments: int32 [16, 1024], P('dp', 'shard'), may hold values from 0 to 11, as said below
- random_key_blocks: int32 [12, 16, 3], replicated, may hold values from 0 to 15, as said below
- adapter_index_table: int32 [16, 6], P('dp'), may hold values from 0 to 7
- frozen_query_key_value_weight: bfloat16 [768, 2304], P('shard'), may hold values from -0.21875 to 0.21875
- frozen_output_weight: bfloat16 [768, 768], P('shard'), may hold values from -0.875 to 0.875
- frozen_up_weight: bfloat16 [768, 3072], P('shard'), may hold values from -0.21875 to 0.21875
- frozen_down_weight: bfloat16 [3072, 768], P('shard'), may hold values from -0.109375 to 0.109375
- attention_norm_gain: float32 [768], replicated, may hold values from 0.5 to 1.5
- feedforward_norm_gain: float32 [768], replicated, may hold values from 0.5 to 1.5
- adapter_down_from_width: bfloat16 [5, 8, 16, 768], replicated, may hold values from -0.21875 to 0.21875
- adapter_down_from_hidden: bfloat16 [8, 16, 3072], replicated, may hold values from -0.109375 to 0.109375
- adapter_up_to_width: bfloat16 [5, 8, 16, 768], replicated, may hold values from -0.75 to 0.75
- adapter_up_to_hidden: bfloat16 [8, 16, 3072], replicated, may hold values from -0.75 to 0.75
- cotangent: bfloat16 [16, 1024, 768], P('dp', 'shard'), may hold values from -6 to 6
Outputs:
- layer_out: bfloat16 [16, 1024, 768], P('dp', 'shard')
- input_grad: float32 [16, 1024, 768], P('dp', 'shard')
- grad_lora_in_d: float32 [5, 8, 16, 768], P(None, None, None, 'shard')
- grad_lora_in_f: float32 [8, 16, 3072], P(None, None, 'shard')
- grad_lora_out_d: float32 [5, 8, 16, 768], P(None, None, None, 'shard')
- grad_lora_out_f: float32 [8, 16, 3072], P(None, None, 'shard')
Inputs may be any that keep to these rules, and one draw needn't show every extreme that they name: `segments`: document numbers start at 0 and never fall along a sequence; among the 2 sequences of each index of dp one holds a single document. `random_key_blocks`: for each head and query block i the three numbers differ and none is below 2 or within one of i.
All inputs are finite; a program needn't handle non-finite values.
Results may differ from a plain program's by a relative error of at most 0.02.
Values may be sent and summed in bfloat16 or wider, within the bound.
No kernel may reach another device: no remote copies, remote signals or barrier semaphores. Data moves between devices by JAX's collectives and lax.ppermute only.
A program may use at most 448 MiB of HBM per device.

v0:
```python
import functools

import jax
import jax.numpy as jnp
from jax import lax
from jax.experimental import pallas as pl
from jax.experimental.pallas import tpu as pltpu
from jax.sharding import PartitionSpec as P

H = 12
HD = 64
BLOCK = 64
GLOBALS = 2
RANDOMS = 3


EPSILON = 1e-06
NEGATIVE = -1e30


def norm_rows(hidden, gain_vector):
    average = jnp.mean(hidden, axis=-1, keepdims=True)
    centred = hidden - average
    spread = jnp.mean(centred * centred, axis=-1, keepdims=True)
    return centred * lax.rsqrt(spread + EPSILON) * gain_vector


def gelu_exact(values):
    return jax.nn.gelu(values, approximate=False)


def dense_forward(inputs, weight):
    return jnp.einsum("sti,io->sto", inputs, weight, preferred_element_type=jnp.float32)


def dense_backward(grad_low, weight):
    return jnp.einsum("sto,io->sti", grad_low, weight, preferred_element_type=jnp.float32)


def adapt(inputs, down_rows, up_rows):
    rank_part = jnp.einsum(
        "sti,sri->str", inputs, down_rows, preferred_element_type=jnp.float32
    ).astype(jnp.bfloat16)
    return (
        rank_part,
        jnp.einsum("str,sro->sto", rank_part, up_rows, preferred_element_type=jnp.float32),
    )


def adapt_back(inputs, down_rows, up_rows, rank_part, grad_low):
    grad_up = jnp.einsum("str,sto->sro", rank_part, grad_low, preferred_element_type=jnp.float32)
    rank_grad = jnp.einsum(
        "sto,sro->str", grad_low, up_rows, preferred_element_type=jnp.float32
    ).astype(jnp.bfloat16)
    grad_down = jnp.einsum("str,sti->sri", rank_grad, inputs, preferred_element_type=jnp.float32)
    grad_inputs = jnp.einsum(
        "str,sri->sti", rank_grad, down_rows, preferred_element_type=jnp.float32
    )
    return (grad_down, grad_up, grad_inputs)


def table_sum(per_sequence, chosen, table_size):
    matches = (chosen[:, None] == jnp.arange(table_size, dtype=jnp.int32)[None, :]).astype(
        jnp.float32
    )
    return jnp.sum(matches[:, :, None, None] * per_sequence[:, None], axis=0)


def sparse_scores(query_heads, key_picked, permit, scaling):
    scores = (
        jnp.einsum(
            "shbqd,shbkd->shbqk", query_heads, key_picked, preferred_element_type=jnp.float32
        )
        * scaling
    )
    return jnp.where(permit, scores, NEGATIVE)


def global_scores(query_rows, key_rows, seg_query, seg_keys, scaling):
    scores = (
        jnp.einsum("hqd,hkd->hqk", query_rows, key_rows, preferred_element_type=jnp.float32)
        * scaling
    )
    return jnp.where((seg_query[:, None] == seg_keys[None, :])[None], scores, NEGATIVE)


def global_forward(query_rows, key_rows, value_rows, seg_query, seg_keys, scaling):
    scores = global_scores(query_rows, key_rows, seg_query, seg_keys, scaling)
    top_score = jnp.max(scores, axis=-1, keepdims=True)
    weights = jnp.exp(scores - top_score)
    totals = jnp.sum(weights, axis=-1, keepdims=True)
    shares = (weights / totals).astype(jnp.bfloat16)
    attended = jnp.einsum("hqk,hkd->hqd", shares, value_rows, preferred_element_type=jnp.float32)
    return (attended, (top_score + jnp.log(totals))[..., 0])


def global_backward(
    query_rows, key_rows, value_rows, seg_query, seg_keys, grad_rows, log_total, scaling
):
    scores = global_scores(query_rows, key_rows, seg_query, seg_keys, scaling)
    shares = jnp.exp(scores - log_total[..., None])
    share_low = shares.astype(jnp.bfloat16)
    grad_shares = jnp.einsum(
        "hqd,hkd->hqk", grad_rows, value_rows, preferred_element_type=jnp.float32
    )
    centre = jnp.sum(shares * grad_shares, axis=-1, keepdims=True)
    grad_scores = (shares * (grad_shares - centre)).astype(jnp.bfloat16)
    grad_query = (
        jnp.einsum("hqk,hkd->hqd", grad_scores, key_rows, preferred_element_type=jnp.float32)
        * scaling
    )
    grad_keys = (
        jnp.einsum("hqk,hqd->hkd", grad_scores, query_rows, preferred_element_type=jnp.float32)
        * scaling
    )
    grad_values = jnp.einsum(
        "hqk,hqd->hkd", share_low, grad_rows, preferred_element_type=jnp.float32
    )
    return (grad_query, grad_keys, grad_values, centre[..., 0])


def general_body(
    inputs,
    segments,
    random_key_blocks,
    adapter_index_table,
    frozen_query_key_value_weight,
    frozen_output_weight,
    frozen_up_weight,
    frozen_down_weight,
    attention_norm_gain,
    feedforward_norm_gain,
    adapter_down_from_width,
    adapter_down_from_hidden,
    adapter_up_to_width,
    adapter_up_to_hidden,
    cotangent,
):
    seq_count = inputs.shape[0]
    local_tokens = inputs.shape[1]
    width = inputs.shape[2]
    shard_count = lax.axis_size("shard")
    full_length = local_tokens * shard_count
    total_blocks = full_length // BLOCK
    local_blocks = local_tokens // BLOCK
    cand_count = 3 + GLOBALS + RANDOMS
    glob_rows = GLOBALS * BLOCK
    scaling = HD ** (-0.5)

    def select_adapter_table(table, table_column):
        return jnp.take(table, adapter_index_table[:, table_column], axis=0)

    adapter_tables_input = [
        select_adapter_table(adapter_down_from_width[table_column], table_column)
        for table_column in range(5)
    ] + [select_adapter_table(adapter_down_from_hidden, 5)]
    adapter_tables_output = [
        select_adapter_table(adapter_up_to_width[table_column], table_column)
        for table_column in range(4)
    ]
    adapter_tables_output = adapter_tables_output + [
        select_adapter_table(adapter_up_to_hidden, 4),
        select_adapter_table(adapter_up_to_width[4], 5),
    ]
    qkv_full, out_full = (
        lax.all_gather(frozen_query_key_value_weight, "shard", axis=0, tiled=True),
        lax.all_gather(frozen_output_weight, "shard", axis=0, tiled=True),
    )
    main_part = dense_forward(inputs, qkv_full)
    rank_parts = []
    projected = []
    for table_column in range(3):
        rank_part, extra = adapt(
            inputs, adapter_tables_input[table_column], adapter_tables_output[table_column]
        )
        rank_parts.append(rank_part)
        projected.append(
            (main_part[..., table_column * width : (table_column + 1) * width] + extra).astype(
                jnp.bfloat16
            )
        )
    seg_low = segments.astype(jnp.bfloat16)
    key_all, value_all, seg_all = (
        lax.all_gather(projected[1], "shard", axis=1, tiled=True),
        lax.all_gather(projected[2], "shard", axis=1, tiled=True),
        lax.all_gather(seg_low, "shard", axis=1, tiled=True),
    )
    shard_pos = lax.axis_index("shard")
    is_first = shard_pos == 0
    first_block = shard_pos * local_blocks
    block_ids = first_block + jnp.arange(local_blocks, dtype=jnp.int32)
    rand_local = lax.dynamic_slice_in_dim(random_key_blocks, first_block, local_blocks, axis=1)
    window_part = jnp.stack([block_ids - 1, block_ids, block_ids + 1], axis=-1)
    global_ids = jnp.broadcast_to(
        jnp.arange(GLOBALS, dtype=jnp.int32)[None, :], (local_blocks, GLOBALS)
    )
    fixed_part = jnp.concatenate([window_part, global_ids], axis=-1)
    candidates = jnp.concatenate(
        [jnp.broadcast_to(fixed_part[None], (H, local_blocks, 3 + GLOBALS)), rand_local], axis=-1
    )
    candidates = jnp.clip(candidates, 0, total_blocks - 1)
    always_true = jnp.ones((local_blocks,), dtype=bool)
    fixed_valid = jnp.stack(
        [block_ids - 1 >= GLOBALS, always_true, block_ids + 1 < total_blocks]
        + [always_true] * GLOBALS,
        axis=-1,
    )
    valid = jnp.concatenate(
        [
            jnp.broadcast_to(fixed_valid[None], (H, local_blocks, 3 + GLOBALS)),
            jnp.ones((H, local_blocks, RANDOMS), dtype=bool),
        ],
        axis=-1,
    )
    valid_keys = jnp.repeat(valid, BLOCK, axis=-1)
    query_heads = (
        projected[0].reshape(seq_count, local_blocks, BLOCK, H, HD).transpose(0, 3, 1, 2, 4)
    )
    key_source = key_all.reshape(seq_count, total_blocks, BLOCK, H, HD).transpose(0, 3, 1, 2, 4)
    value_source = value_all.reshape(seq_count, total_blocks, BLOCK, H, HD).transpose(0, 3, 1, 2, 4)
    head_index = jnp.arange(H, dtype=jnp.int32)[:, None, None]
    key_picked = key_source[:, head_index, candidates].reshape(
        seq_count, H, local_blocks, cand_count * BLOCK, HD
    )
    value_picked = value_source[:, head_index, candidates].reshape(
        seq_count, H, local_blocks, cand_count * BLOCK, HD
    )
    seg_picked = seg_all.reshape(seq_count, total_blocks, BLOCK)[:, candidates].reshape(
        seq_count, H, local_blocks, cand_count * BLOCK
    )
    seg_local = seg_low.reshape(seq_count, local_blocks, BLOCK)
    permit = valid_keys[None, :, :, None, :] & (
        seg_local[:, None, :, :, None] == seg_picked[:, :, :, None, :]
    )
    scores = sparse_scores(query_heads, key_picked, permit, scaling)
    top_score = jnp.max(scores, axis=-1, keepdims=True)
    weights = jnp.exp(scores - top_score)
    totals = jnp.sum(weights, axis=-1, keepdims=True)
    share_low = (weights / totals).astype(jnp.bfloat16)
    sparse_lse = (top_score + jnp.log(totals))[..., 0]
    sparse_out = jnp.einsum(
        "shbqk,shbkd->shbqd", share_low, value_picked, preferred_element_type=jnp.float32
    )
    key_heads = key_source.reshape(seq_count, H, full_length, HD)
    value_heads = value_source.reshape(seq_count, H, full_length, HD)
    glob_query = query_heads[:, :, :GLOBALS].reshape(seq_count, H, glob_rows, HD)
    glob_seg = seg_low[:, :glob_rows]

    def run_forward(operands):
        return lax.map(
            lambda packet: global_forward(
                packet[0], packet[1], packet[2], packet[3], packet[4], scaling
            ),
            operands,
        )

    def skip_forward(operands):
        return (
            jnp.zeros((seq_count, H, glob_rows, HD), jnp.float32),
            jnp.zeros((seq_count, H, glob_rows), jnp.float32),
        )

    global_out, global_lse = lax.cond(
        is_first, run_forward, skip_forward, (glob_query, key_heads, value_heads, glob_seg, seg_all)
    )
    glob_blocks = global_out.reshape(seq_count, H, GLOBALS, BLOCK, HD)
    head_out = jnp.concatenate(
        [jnp.where(is_first, glob_blocks, sparse_out[:, :, :GLOBALS]), sparse_out[:, :, GLOBALS:]],
        axis=2,
    )
    mixed_low = (
        head_out.transpose(0, 2, 3, 1, 4)
        .reshape(seq_count, local_tokens, width)
        .astype(jnp.bfloat16)
    )
    rank_out, extra_out = adapt(mixed_low, adapter_tables_input[3], adapter_tables_output[3])
    branch = dense_forward(mixed_low, out_full) + extra_out
    first, first_pull = jax.vjp(
        lambda hidden: norm_rows(hidden, attention_norm_gain), inputs.astype(jnp.float32) + branch
    )
    first_low = first.astype(jnp.bfloat16)
    up_full, down_full = (
        lax.all_gather(frozen_up_weight, "shard", axis=0, tiled=True),
        lax.all_gather(frozen_down_weight, "shard", axis=0, tiled=True),
    )
    rank_up, extra_up = adapt(first_low, adapter_tables_input[4], adapter_tables_output[4])
    lifted = dense_forward(first_low, up_full) + extra_up
    activated, gelu_pull = jax.vjp(gelu_exact, lifted)
    active_low = activated.astype(jnp.bfloat16)
    rank_down, extra_down = adapt(active_low, adapter_tables_input[5], adapter_tables_output[5])
    lowered = dense_forward(active_low, down_full) + extra_down
    result, final_pull = jax.vjp(
        lambda hidden: norm_rows(hidden, feedforward_norm_gain), first + lowered
    )
    layer_out = result.astype(jnp.bfloat16)
    up_back, down_back = (
        lax.all_gather(frozen_up_weight, "shard", axis=0, tiled=True),
        lax.all_gather(frozen_down_weight, "shard", axis=0, tiled=True),
    )
    grad_adapt_in = [None] * 6
    grad_adapt_out = [None] * 6
    (grad_sum,) = final_pull(cotangent.astype(jnp.float32))
    grad_lowered = grad_sum.astype(jnp.bfloat16)
    grad_adapt_in[5], grad_adapt_out[5], extra_grad = adapt_back(
        active_low, adapter_tables_input[5], adapter_tables_output[5], rank_down, grad_lowered
    )
    grad_active = dense_backward(grad_lowered, down_back) + extra_grad
    (grad_lifted,) = gelu_pull(grad_active)
    grad_lift_low = grad_lifted.astype(jnp.bfloat16)
    grad_adapt_in[4], grad_adapt_out[4], extra_grad = adapt_back(
        first_low, adapter_tables_input[4], adapter_tables_output[4], rank_up, grad_lift_low
    )
    grad_first = grad_sum + dense_backward(grad_lift_low, up_back) + extra_grad
    (grad_branch,) = first_pull(grad_first)
    grad_branch_low = grad_branch.astype(jnp.bfloat16)
    qkv_back, out_back = (
        lax.all_gather(frozen_query_key_value_weight, "shard", axis=0, tiled=True),
        lax.all_gather(frozen_output_weight, "shard", axis=0, tiled=True),
    )
    grad_adapt_in[3], grad_adapt_out[3], extra_grad = adapt_back(
        mixed_low, adapter_tables_input[3], adapter_tables_output[3], rank_out, grad_branch_low
    )
    grad_mixed = (dense_backward(grad_branch_low, out_back) + extra_grad).astype(jnp.bfloat16)
    grad_heads = grad_mixed.reshape(seq_count, local_blocks, BLOCK, H, HD).transpose(0, 3, 1, 2, 4)
    row_keep = (block_ids >= GLOBALS)[None, None, :, None, None]
    grad_sparse = jnp.where(row_keep, grad_heads, jnp.zeros_like(grad_heads))
    scores = sparse_scores(query_heads, key_picked, permit, scaling)
    shares = jnp.exp(scores - sparse_lse[..., None])
    share_low = shares.astype(jnp.bfloat16)
    grad_shares = jnp.einsum(
        "shbqd,shbkd->shbqk", grad_sparse, value_picked, preferred_element_type=jnp.float32
    )
    centre = jnp.sum(shares * grad_shares, axis=-1, keepdims=True)
    grad_scores = (shares * (grad_shares - centre)).astype(jnp.bfloat16)
    grad_query = (
        jnp.einsum(
            "shbqk,shbkd->shbqd", grad_scores, key_picked, preferred_element_type=jnp.float32
        )
        * scaling
    )
    glob_grad = grad_heads[:, :, :GLOBALS].reshape(seq_count, H, glob_rows, HD)

    def run_backward(operands):
        return lax.map(
            lambda packet: global_backward(
                packet[0], packet[1], packet[2], packet[3], packet[4], packet[5], packet[6], scaling
            ),
            operands,
        )

    def skip_backward(operands):
        return (
            jnp.zeros((seq_count, H, glob_rows, HD), jnp.float32),
            jnp.zeros((seq_count, H, full_length, HD), jnp.float32),
            jnp.zeros((seq_count, H, full_length, HD), jnp.float32),
            jnp.zeros((seq_count, H, glob_rows), jnp.float32),
        )

    glob_dq, glob_dk, glob_dv, glob_centre = lax.cond(
        is_first,
        run_backward,
        skip_backward,
        (glob_query, key_heads, value_heads, glob_seg, seg_all, glob_grad, global_lse),
    )
    grad_query = grad_query.at[:, :, :GLOBALS].add(
        glob_dq.reshape(seq_count, H, GLOBALS, BLOCK, HD)
    )
    grad_key_picked = (
        jnp.einsum(
            "shbqk,shbqd->shbkd", grad_scores, query_heads, preferred_element_type=jnp.float32
        )
        * scaling
    )
    grad_value_picked = jnp.einsum(
        "shbqk,shbqd->shbkd", share_low, grad_sparse, preferred_element_type=jnp.float32
    )
    block_shape = (seq_count, H, local_blocks, cand_count, BLOCK, HD)
    key_grad_blocks = (
        jnp.zeros((seq_count, H, total_blocks, BLOCK, HD), jnp.float32)
        .at[:, head_index, candidates]
        .add(grad_key_picked.reshape(block_shape))
    )
    value_grad_blocks = (
        jnp.zeros((seq_count, H, total_blocks, BLOCK, HD), jnp.float32)
        .at[:, head_index, candidates]
        .add(grad_value_picked.reshape(block_shape))
    )
    key_grad_full = (
        (key_grad_blocks.reshape(seq_count, H, full_length, HD) + glob_dk)
        .transpose(0, 2, 1, 3)
        .reshape(seq_count, full_length, width)
    )
    value_grad_full = (
        (value_grad_blocks.reshape(seq_count, H, full_length, HD) + glob_dv)
        .transpose(0, 2, 1, 3)
        .reshape(seq_count, full_length, width)
    )
    key_grad, value_grad = (
        lax.psum_scatter(
            key_grad_full.astype(jnp.bfloat16), "shard", scatter_dimension=1, tiled=True
        ).astype(jnp.float32),
        lax.psum_scatter(
            value_grad_full.astype(jnp.bfloat16), "shard", scatter_dimension=1, tiled=True
        ).astype(jnp.float32),
    )
    query_grad = grad_query.transpose(0, 2, 3, 1, 4).reshape(seq_count, local_tokens, width)
    grad_proj = [
        query_grad.astype(jnp.bfloat16),
        key_grad.astype(jnp.bfloat16),
        value_grad.astype(jnp.bfloat16),
    ]
    input_grad = grad_branch + dense_backward(jnp.concatenate(grad_proj, axis=-1), qkv_back)
    for table_column in range(3):
        grad_adapt_in[table_column], grad_adapt_out[table_column], extra_grad = adapt_back(
            inputs,
            adapter_tables_input[table_column],
            adapter_tables_output[table_column],
            rank_parts[table_column],
            grad_proj[table_column],
        )
        input_grad = input_grad + extra_grad
    adapter_table_count = adapter_down_from_width.shape[1]
    grad_in_d = jnp.stack(
        [
            table_sum(
                grad_adapt_in[table_column],
                adapter_index_table[:, table_column],
                adapter_table_count,
            )
            for table_column in range(5)
        ],
        axis=0,
    )
    grad_in_f = table_sum(grad_adapt_in[5], adapter_index_table[:, 5], adapter_table_count)
    out_list = [
        table_sum(
            grad_adapt_out[table_column], adapter_index_table[:, table_column], adapter_table_count
        )
        for table_column in range(4)
    ]
    grad_out_d = jnp.stack(
        out_list + [table_sum(grad_adapt_out[5], adapter_index_table[:, 5], adapter_table_count)],
        axis=0,
    )
    grad_out_f = table_sum(grad_adapt_out[4], adapter_index_table[:, 4], adapter_table_count)
    owned = (
        lax.psum_scatter(
            grad_in_d.astype(jnp.bfloat16), "shard", scatter_dimension=3, tiled=True
        ).astype(jnp.float32),
        lax.psum_scatter(
            grad_in_f.astype(jnp.bfloat16), "shard", scatter_dimension=2, tiled=True
        ).astype(jnp.float32),
        lax.psum_scatter(
            grad_out_d.astype(jnp.bfloat16), "shard", scatter_dimension=3, tiled=True
        ).astype(jnp.float32),
        lax.psum_scatter(
            grad_out_f.astype(jnp.bfloat16), "shard", scatter_dimension=2, tiled=True
        ).astype(jnp.float32),
    )
    summed = (
        lax.psum(owned[0].astype(jnp.bfloat16), "dp").astype(jnp.float32),
        lax.psum(owned[1].astype(jnp.bfloat16), "dp").astype(jnp.float32),
        lax.psum(owned[2].astype(jnp.bfloat16), "dp").astype(jnp.float32),
        lax.psum(owned[3].astype(jnp.bfloat16), "dp").astype(jnp.float32),
    )
    return (layer_out, input_grad, summed[0], summed[1], summed[2], summed[3])


BF = jnp.bfloat16
F32 = jnp.float32
NT = (((1,), (1,)), ((), ()))
TN = (((0,), (0,)), ((), ()))
BIG = 1e30
RANK = 16
ANY = pl.ANY
VMEM = pltpu.VMEM
MEBI = 1024 * 1024
SMALL_COST = pl.CostEstimate(flops=1_000_000, bytes_accessed=100_000, transcendentals=0)


def mm(left, right):
    return jnp.dot(left, right, preferred_element_type=F32)


def mm_nt(left, right):
    return lax.dot_general(left, right, NT, preferred_element_type=F32)


def mm_tn(left, right):
    return lax.dot_general(left, right, TN, preferred_element_type=F32)


def whole(shape):
    return pl.BlockSpec(shape, lambda *_: (0,) * len(shape))


def away_pairs(dp_count, shard_count, step):
    pairs = []
    for chip in range(dp_count // 2):
        for k in range(2):
            for z in range(shard_count):
                m = (z & 1) ^ step
                source = (2 * chip + k) * shard_count + z
                target = (2 * chip + (z >> 1)) * shard_count + 2 * k + m
                pairs.append((source, target))
    return pairs


def swap_cores(value, dp_count):
    return lax.ppermute(value, "dp", [(i, i ^ 1) for i in range(dp_count)])


def swap_shards(value, shard_count, step):
    return lax.ppermute(value, "shard", [(i, i ^ step) for i in range(shard_count)])


def spread_over_chips(block, dp_count):
    others = [lax.ppermute(block, "dp", [(i, i ^ o) for i in range(dp_count)]) for o in range(2, dp_count, 2)]
    return [block] + others


def swap_chips(block, dp_count, offset):
    return lax.ppermute(block, "dp", [(i, i ^ offset) for i in range(dp_count)])


def spread_over_cores(blocks, dp_count):
    return [one for block in blocks for one in (block, swap_cores(block, dp_count))]


def spread_in_plane(block, dp_count):
    return spread_over_cores(spread_over_chips(block, dp_count), dp_count)


def join_kernel(meta, part0, part1, out_ref):
    for r, part in enumerate((part0, part1)):
        out_ref[(meta[0] & 1) ^ r] = part[...].astype(out_ref.dtype)


def join_parts(meta, parts, dtype):
    rows, width = parts[0].shape
    return pl.pallas_call(
        join_kernel,
        grid_spec=pltpu.PrefetchScalarGridSpec(
            num_scalar_prefetch=1,
            grid=(1,),
            in_specs=[whole((rows, width))] * 2,
            out_specs=whole((2, rows, width)),
        ),
        out_shape=jax.ShapeDtypeStruct((2, rows, width), dtype),
        compiler_params=pltpu.CompilerParams(vmem_limit_bytes=30 * MEBI),
        cost_estimate=SMALL_COST,
        name="join_parts",
    )(meta, *parts)


def send_away(parts, dp_count, shard_count):
    return [
        lax.ppermute(part, ("dp", "shard"), away_pairs(dp_count, shard_count, r))
        for r, part in enumerate(parts)
    ]


def weight_copies(meta, own_ref, pieces, dest, sems, places):
    z, d = meta[0], meta[1]
    own_rows, columns = own_ref.shape
    copies = [
        pltpu.make_async_copy(
            own_ref, dest.at[pl.ds(pl.multiple_of(z * own_rows, 16), own_rows)], sems.at[0]
        )
    ]
    count = 1
    for o, parts in enumerate(pieces):
        who = d ^ o
        for step in range(3):
            shard = z ^ (step + 1)
            for start, row, column, rows, cols in places(who):
                for piece, first in parts:
                    low, high = max(start, first), min(start + rows, first + piece.shape[1])
                    if low >= high:
                        continue
                    copies.append(
                        pltpu.make_async_copy(
                            piece.at[step, pl.ds(low - first, high - low)],
                            dest.at[
                                pl.ds(pl.multiple_of(shard * own_rows + row + low - start, 16), high - low),
                                pl.ds(pl.multiple_of(column, 128), cols),
                            ],
                            sems.at[count],
                        )
                    )
                    count += 1
    return copies


def one_each(refs):
    return [[(ref, 0)] for ref in refs]


UP_SPLIT = 128


def up_parts(refs):
    return one_each(refs[0:6]) + [[(refs[6], 0), (refs[7], UP_SPLIT)], [(refs[8], 0), (refs[9], UP_SPLIT)]]


def qkv_places(who):
    return [(0, (who >> 1) * 48, (who & 1) * 1152, 48, 1152)]


def out_places(who):
    return [(0, (who >> 1) * 48, (who & 1) * 384, 48, 384)]


def up_places(who):
    return [(48, 0, who * 384, 192, 384)]


def down_places(who):
    return [(0, who * 96, 0, 96, 384), (96, who * 96, 384, 96, 384)]


def token_copies(meta, messages, dest, sems):
    copies = []
    for at, message in enumerate(messages):
        row = 512 * (at >> 1) + 256 * ((meta[0] & 1) ^ (at & 1))
        copies.append(
            pltpu.make_async_copy(
                message.at[pl.ds(0, 256)], dest.at[pl.ds(pl.multiple_of(row, 256), 256)], sems.at[at]
            )
        )
    return copies


def zero_padded(rows, position, count):
    zeros = jnp.zeros_like(rows)
    return jnp.concatenate([rows if i == position else zeros for i in range(count)], axis=0)


def qkv_kernel(meta, ids, *refs):
    messages, w_own, pieces = refs[0:4], refs[4], one_each(refs[5:13])
    ins, outs = refs[13:16], refs[16:19]
    q_ref, k_ref, v_ref, mask_ref, hot_ref, own_ref = refs[19:25]
    xs, segs, weight, wsems, xsems, ssems = refs[25:]
    copies = token_copies(meta, messages, xs, xsems)
    for at, message in enumerate(messages):
        copies.append(
            pltpu.make_async_copy(
                message.at[pl.ds(256, 16), pl.ds(0, 256)],
                segs.at[2 * (at >> 1) + ((meta[0] & 1) ^ (at & 1))],
                ssems.at[at],
            )
        )
    copies += weight_copies(meta, w_own, pieces, weight, wsems, qkv_places)
    for copy in copies:
        copy.start()
    for copy in copies:
        copy.wait()
    lane = lax.broadcasted_iota(jnp.int32, (128, 128), 1)
    lane_of_head = lax.rem(lane, 64)
    as_float = lane_of_head.astype(F32)
    is_segment = lane_of_head < 16
    row_block = lax.broadcasted_iota(jnp.int32, (128, 128), 0) // 64
    for place in range(4):
        row = segs[place].astype(F32)[0:1]
        for half in range(2):
            column = jnp.broadcast_to(row[:, 128 * half : 128 * half + 128], (128, 128)).T
            same = column == as_float
            block_lane = lane_of_head == 16 + 4 * place + 2 * half + row_block
            rows = slice(256 * place + 128 * half, 256 * place + 128 * half + 128)
            mask_ref[rows] = jnp.where(
                is_segment, jnp.where(same, 0.0, -BIG), jnp.where(block_lane, 1.0, 0.0)
            ).astype(BF)
            if place < 2:
                hot_ref[rows] = jnp.where(is_segment & same, 1.0, 0.0).astype(BF)
    own_ref[...] = xs[0:512]
    in_all = jnp.concatenate([ref[0, 0] for ref in ins], axis=0)
    out_all = [zero_padded(ref[0, 0], p, 3) for p, ref in enumerate(outs)]
    targets = (q_ref, k_ref, v_ref)
    for tile in range(4):
        rows = slice(256 * tile, 256 * tile + 256)
        x = xs[rows]
        rank = mm_nt(x, in_all).astype(BF)
        for p in range(0 if tile < 2 else 1, 3):
            value = mm(x, weight[:, 768 * p : 768 * p + 768]) + mm(rank, out_all[p])
            value = value.astype(BF)
            if p == 0:
                value = (value.astype(F32) * HD**-0.5).astype(BF)
            targets[p][rows] = value


def table_spec(p, column, width):
    return pl.BlockSpec((1, 1, RANK, width), lambda i, meta, ids: (p, ids[column], 0, 0))


def hidden_spec(column, width):
    return pl.BlockSpec((1, RANK, width), lambda i, meta, ids: (ids[column], 0, 0))


def any_specs(count):
    return [pl.BlockSpec(memory_space=ANY)] * count


def project_qkv(meta, ids, messages, w_own, pieces, table_in, table_out):
    width = w_own.shape[1] // 3
    return pl.pallas_call(
        qkv_kernel,
        grid_spec=pltpu.PrefetchScalarGridSpec(
            num_scalar_prefetch=2,
            grid=(1,),
            in_specs=any_specs(13)
            + [table_spec(p, p, width) for p in range(3)]
            + [table_spec(p, p, width) for p in range(3)],
            out_specs=[
                whole((512, width)),
                whole((1024, width)),
                whole((1024, width)),
                whole((1024, 128)),
                whole((512, 128)),
                whole((512, width)),
            ],
            scratch_shapes=[
                VMEM((1024, width), BF),
                VMEM((4, 16, 256), BF),
                VMEM((width, 3 * width), BF),
                pltpu.SemaphoreType.DMA((25,)),
                pltpu.SemaphoreType.DMA((4,)),
                pltpu.SemaphoreType.DMA((4,)),
            ],
        ),
        out_shape=[
            jax.ShapeDtypeStruct((512, width), BF),
            jax.ShapeDtypeStruct((1024, width), BF),
            jax.ShapeDtypeStruct((1024, width), BF),
            jax.ShapeDtypeStruct((1024, 128), BF),
            jax.ShapeDtypeStruct((512, 128), BF),
            jax.ShapeDtypeStruct((512, width), BF),
        ],
        compiler_params=pltpu.CompilerParams(vmem_limit_bytes=56 * MEBI),
        cost_estimate=SMALL_COST,
        name="project_qkv",
    )(meta, ids, *messages, w_own, *pieces, *([table_in] * 3), *([table_out] * 3))


def attend_kernel(q_ref, k_ref, v_ref, mask_ref, hot_ref, closed_ref, o_ref, p_ref):
    low = lax.broadcasted_iota(jnp.int32, (512, 128), 1) < 64
    low_keys = lax.broadcasted_iota(jnp.int32, (1024, 128), 1) < 64
    closed = jnp.concatenate(
        [jnp.broadcast_to(closed_ref[0, l : l + 1], (64, 128)) for l in range(8)], axis=0
    )
    extra = (hot_ref[...].astype(F32) + closed).astype(BF)
    q, k, v, masks = q_ref[...], k_ref[...], v_ref[...], mask_ref[...]
    wide = [(jnp.where(low, q, extra), jnp.where(low_keys, k, masks)), (jnp.where(low, extra, q), jnp.where(low_keys, masks, k))]
    size = 512
    units = [(start, head) for start in range(0, 512, size) for head in range(2)]
    raw = lambda unit: mm_nt(wide[unit[1]][0][unit[0] : unit[0] + size], wide[unit[1]][1])
    ahead = raw(units[0])
    mixed = {}
    for n, (start, head) in enumerate(units):
        scores = ahead
        if n + 1 < len(units):
            ahead = raw(units[n + 1])
        weights = jnp.exp(scores - jnp.max(scores, axis=1, keepdims=True))
        shares = (weights * (1.0 / jnp.sum(weights, axis=1, keepdims=True))).astype(BF)
        p_ref[head, start : start + size] = shares
        mixed[head] = mm(shares, v)
        if head == 1:
            o_ref[start : start + size] = jnp.where(low[0:size], mixed[0], mixed[1]).astype(BF)


def attend(q, k, v, masks, hot, closed):
    width = q.shape[1]
    pairs = width // 128
    half = pl.BlockSpec((512, 128), lambda g: (0, g))
    full = pl.BlockSpec((1024, 128), lambda g: (0, g))
    return pl.pallas_call(
        attend_kernel,
        grid=(pairs,),
        in_specs=[
            half,
            full,
            full,
            whole((1024, 128)),
            whole((512, 128)),
            pl.BlockSpec((1, 8, 128), lambda g: (g, 0, 0)),
        ],
        out_specs=[half, pl.BlockSpec((2, 512, 1024), lambda g: (g, 0, 0))],
        out_shape=[
            jax.ShapeDtypeStruct((512, width), BF),
            jax.ShapeDtypeStruct((2 * pairs, 512, 1024), BF),
        ],
        compiler_params=pltpu.CompilerParams(vmem_limit_bytes=56 * MEBI),
        cost_estimate=SMALL_COST,
        name="attend",
    )(q, k, v, masks, hot, closed)


def attend_back_kernel(q_ref, k_ref, v_ref, p_ref, grad_ref, mixed_ref, dq_ref, dk_own, dv_own, other_ref):
    low = lax.broadcasted_iota(jnp.int32, (512, 128), 1) < 64
    q, k, v, grad = q_ref[...], k_ref[...], v_ref[...], grad_ref[...]
    products = grad.astype(F32) * mixed_ref[...].astype(F32)
    q_turned, grad_turned = q.T, grad.T
    zeros, none = jnp.zeros_like(grad), jnp.zeros_like(products)
    dq, dk, dv = [], [], []
    for head in range(2):
        mine = low if head == 0 else jnp.logical_not(low)
        centre = jnp.sum(jnp.where(mine, products, none), axis=1, keepdims=True)
        grad_shares = mm_nt(jnp.where(mine, grad, zeros), v)
        shares = p_ref[head]
        grad_scores = (shares.astype(F32) * (grad_shares - centre)).astype(BF)
        rows = slice(64 * head, 64 * head + 64)
        dq.append(mm(grad_scores, k))
        dk.append(mm(q_turned[rows], grad_scores))
        dv.append(mm(grad_turned[rows], shares))
    dq_ref[...] = (jnp.where(low, dq[0], dq[1]) * HD**-0.5).astype(BF)
    dk = jnp.concatenate(dk, axis=0).T
    dv = jnp.concatenate(dv, axis=0).T
    dk_own[...] = dk[0:512].astype(BF)
    dv_own[...] = dv[0:512].astype(BF)
    other_ref[0] = dk[512:1024].astype(BF)
    other_ref[1] = dv[512:1024].astype(BF)


def attend_back(q, k, v, shares, grad, mixed):
    width = q.shape[1]
    half = pl.BlockSpec((512, 128), lambda g: (0, g))
    full = pl.BlockSpec((1024, 128), lambda g: (0, g))
    return pl.pallas_call(
        attend_back_kernel,
        grid=(width // 128,),
        in_specs=[half, full, full, pl.BlockSpec((2, 512, 1024), lambda g: (g, 0, 0)), half, half],
        out_specs=[half] * 3 + [pl.BlockSpec((2, 512, 128), lambda g: (0, 0, g))],
        out_shape=[
            jax.ShapeDtypeStruct((512, width), BF),
            jax.ShapeDtypeStruct((512, width), BF),
            jax.ShapeDtypeStruct((512, width), BF),
            jax.ShapeDtypeStruct((2, 512, width), BF),
        ],
        compiler_params=pltpu.CompilerParams(vmem_limit_bytes=56 * MEBI),
        cost_estimate=SMALL_COST,
        name="attend_back",
    )(q, k, v, shares, grad, mixed)


def gelu_and_slope(lifted):
    size = jnp.abs(lifted)
    t = 1.0 / (1.0 + 0.23164189 * size)
    poly = t * (
        0.127414796 + t * (-0.142248368 + t * (0.7107068705 + t * (-0.7265760135 + t * 0.5307027145)))
    )
    decay = jnp.exp2(lifted * lifted * -0.7213475204444817)
    tail = poly * decay
    below = jnp.where(lifted < 0.0, tail, 1.0 - tail)
    return jnp.maximum(lifted, 0.0) - size * tail, below + lifted * (decay * 0.3989422804014327)


def norm_parts(hidden):
    average = jnp.mean(hidden, axis=-1, keepdims=True)
    centred = hidden - average
    spread = jnp.mean(centred * centred, axis=-1, keepdims=True)
    inverse = lax.rsqrt(spread + EPSILON)
    return centred * inverse, inverse


def norm_back(grad, gain, normal, inverse):
    scaled = grad * gain
    return inverse * (
        scaled
        - jnp.mean(scaled, axis=-1, keepdims=True)
        - normal * jnp.mean(scaled * normal, axis=-1, keepdims=True)
    )


MID_TILE = 256
MID_PARTS = 4


def first_half_kernel(meta, ids, *refs):
    out_own, up_own, up_pieces = refs[0], refs[1], up_parts(refs[2:12])
    x_ref, mixed_ref, gain1, in3, in4, out3, out4 = refs[12:19]
    normal_ref, inverse_ref, active, slope = refs[19:23]
    w_out, w_up, osems, usems = refs[23:]
    out_copies = weight_copies(meta, out_own, up_pieces, w_out, osems, out_places)
    up_copies = weight_copies(meta, up_own, up_pieces, w_up, usems, up_places)
    is_first = pl.program_id(0) == 0

    @pl.when(is_first)
    def _():
        for copy in out_copies + up_copies:
            copy.start()
        for copy in out_copies:
            copy.wait()

    mixed = mixed_ref[...]
    rank3 = mm_nt(mixed, in3[0, 0]).astype(BF)
    branch = mm(mixed, w_out[...]) + mm(rank3, out3[0, 0])
    normal, inverse = norm_parts(x_ref[...].astype(F32) + branch)
    normal_ref[...] = normal
    inverse_ref[...] = jnp.broadcast_to(inverse, inverse_ref.shape)
    low = (normal * gain1[...][None]).astype(BF)
    rank4 = mm_nt(low, in4[0, 0]).astype(BF)

    @pl.when(is_first)
    def _():
        for copy in up_copies:
            copy.wait()

    part = w_up.shape[1] // MID_PARTS
    columns = [slice(n * part, n * part + part) for n in range(MID_PARTS)]
    lift = lambda cols: mm(low, w_up[:, cols]) + mm(rank4, out4[0, :, cols])
    ahead = lift(columns[0])
    for n, cols in enumerate(columns):
        lifted = ahead
        if n + 1 < MID_PARTS:
            ahead = lift(columns[n + 1])
        value, tangent = gelu_and_slope(lifted)
        active[:, cols] = value.astype(BF)
        slope[:, cols] = tangent.astype(BF)


def first_half(meta, ids, out_own, up_own, up_pieces, x, mixed, gain1, table_in, table_out, table_out_hidden):
    width, hidden = x.shape[1], up_own.shape[1]
    tile = lambda columns: pl.BlockSpec((MID_TILE, columns), lambda i, *_: (i, 0))
    return pl.pallas_call(
        first_half_kernel,
        grid_spec=pltpu.PrefetchScalarGridSpec(
            num_scalar_prefetch=2,
            grid=(512 // MID_TILE,),
            in_specs=any_specs(12)
            + [
                tile(width),
                tile(width),
                whole((width,)),
                table_spec(3, 3, width),
                table_spec(4, 4, width),
                table_spec(3, 3, width),
                hidden_spec(4, hidden),
            ],
            out_specs=[tile(width), tile(128), tile(hidden), tile(hidden)],
            scratch_shapes=[
                VMEM((width, width), BF),
                VMEM((width, hidden), BF),
                pltpu.SemaphoreType.DMA((25,)),
                pltpu.SemaphoreType.DMA((31,)),
            ],
        ),
        out_shape=[
            jax.ShapeDtypeStruct((512, width), F32),
            jax.ShapeDtypeStruct((512, 128), F32),
            jax.ShapeDtypeStruct((512, hidden), BF),
            jax.ShapeDtypeStruct((512, hidden), BF),
        ],
        compiler_params=pltpu.CompilerParams(vmem_limit_bytes=56 * MEBI),
        cost_estimate=SMALL_COST,
        name="first_half",
    )(meta, ids, out_own, up_own, *up_pieces, x, mixed, gain1, table_in, table_in, table_out, table_out_hidden)


def write_halves(meta, gathered, groups, own_half, other_half):
    core = meta[1] & 1
    for r in range(4):
        for half, ref in enumerate((own_half, other_half)):
            rows = [
                gathered[meta[0] ^ r, pl.ds(pl.multiple_of(16 * group + 8 * (core ^ half), 8), 8), :]
                for group in range(groups)
            ]
            ref[r] = jnp.concatenate(rows, axis=0).astype(ref.dtype)


def second_half_kernel(meta, ids, *refs):
    cots, out_own, up_own, down_own = refs[0:2], refs[2], refs[3], refs[4]
    up_pieces, down_pieces = up_parts(refs[5:15]), one_each(refs[15:23])
    normal_ref, inverse_ref, active, slope, mixed_ref = refs[23:28]
    gain1, gain2, in3, in4, in5, out3, out4, out5 = refs[28:36]
    layer_parts, grad_branch_ref, grad_mixed_ref, own_half, other_half = refs[36:38], refs[38], refs[39], refs[40], refs[41]
    (
        cot, w_out, w_up, w_down, layer,
        s_in3, s_in4, s_in5, s_out3, s_out4, s_out5, gathered,
        osems, usems, dsems, xsems,
    ) = refs[42:]
    tile = pl.program_id(0)
    is_first = tile == 0
    near = token_copies(meta, cots, cot, xsems)
    out_copies = weight_copies(meta, out_own, up_pieces, w_out, osems, out_places)
    up_copies = weight_copies(meta, up_own, up_pieces, w_up, usems, up_places)
    down_copies = weight_copies(meta, down_own, down_pieces, w_down, dsems, down_places)

    @pl.when(is_first)
    def _():
        for copy in down_copies + near + up_copies + out_copies:
            copy.start()
        for ref in (s_in3, s_in4, s_in5, s_out3, s_out4, s_out5):
            ref[...] = jnp.zeros_like(ref)
        for copy in down_copies + near:
            copy.wait()

    part = w_up.shape[1] // MID_PARTS
    a_in3, a_in4, a_out3, a_out5 = in3[0, 0], in4[0, 0], out3[0, 0], out5[0, 0]
    rows = pl.ds(pl.multiple_of(tile * MID_TILE, MID_TILE), MID_TILE)
    normal1 = normal_ref[...]
    inverse1 = inverse_ref[:, 0:1]
    first = normal1 * gain1[...][None]
    low1 = first.astype(BF)
    r4 = mm_nt(low1, a_in4).astype(BF)
    r5 = mm_nt(active[...], in5[0]).astype(BF)
    lowered = first + mm(active[...], w_down[...]) + mm(r5, a_out5)
    normal2, inverse2 = norm_parts(lowered)
    layer[rows, :] = (normal2 * gain2[...][None]).astype(BF)
    grad_sum = norm_back(cot[rows, :].astype(F32), gain2[...][None], normal2, inverse2)
    e5 = grad_sum.astype(BF)
    rg5 = mm_nt(e5, a_out5).astype(BF)
    s_out5[...] += mm_tn(r5, e5)

    @pl.when(is_first)
    def _():
        for copy in up_copies + out_copies:
            copy.wait()

    grad_first = grad_sum
    rg4 = jnp.zeros((MID_TILE, RANK), F32)
    for n in range(MID_PARTS):
        cols = slice(n * part, n * part + part)
        grad_active = mm_nt(e5, w_down[cols, :]) + mm(rg5, in5[0, :, cols])
        e4 = (slope[:, cols].astype(F32) * grad_active).astype(BF)
        s_in5[:, cols] += mm_tn(rg5, active[:, cols])
        s_out4[:, cols] += mm_tn(r4, e4)
        grad_first = grad_first + mm_nt(e4, w_up[:, cols])
        rg4 = rg4 + mm_nt(e4, out4[0, :, cols])
    rg4 = rg4.astype(BF)
    s_in4[...] += mm_tn(rg4, low1)
    grad_first = grad_first + mm(rg4, a_in4)
    grad_branch = norm_back(grad_first, gain1[...][None], normal1, inverse1)
    grad_branch_ref[...] = grad_branch
    e3 = grad_branch.astype(BF)
    mixed = mixed_ref[...]
    rank3 = mm_nt(mixed, a_in3).astype(BF)
    rg3 = mm_nt(e3, a_out3).astype(BF)
    s_out3[...] += mm_tn(rank3, e3)
    s_in3[...] += mm_tn(rg3, mixed)
    grad_mixed_ref[...] = (mm_nt(e3, w_out[...]) + mm(rg3, a_in3)).astype(BF)

    @pl.when(tile == 512 // MID_TILE - 1)
    def _():
        wide, narrow = 768, 192
        for owner in range(4):
            start = 0
            for ref, size in (
                (s_in5, wide), (s_out4, wide), (s_in3, narrow), (s_in4, narrow), (s_out3, narrow), (s_out5, narrow),
            ):
                row, column = 16 * (start // 768), start % 768
                gathered[owner, row : row + 16, column : column + size] = ref[:, owner * size : owner * size + size]
                start += size
        for r, ref in enumerate(layer_parts):
            ref[...] = layer[pl.ds(pl.multiple_of(256 * ((meta[0] & 1) ^ r), 256), 256), :]
        write_halves(meta, gathered, 3, own_half, other_half)


def second_half(meta, ids, cots, out_own, up_own, down_own, up_pieces, down_pieces, normal, inverse, active, slope,
                mixed, gain1, gain2, table_in, table_in_hidden, table_out, table_out_hidden):
    width, hidden = normal.shape[1], up_own.shape[1]
    tile = lambda columns: pl.BlockSpec((MID_TILE, columns), lambda i, *_: (i, 0))
    return pl.pallas_call(
        second_half_kernel,
        grid_spec=pltpu.PrefetchScalarGridSpec(
            num_scalar_prefetch=2,
            grid=(512 // MID_TILE,),
            in_specs=any_specs(23)
            + [
                tile(width),
                tile(128),
                tile(hidden),
                tile(hidden),
                tile(width),
                whole((width,)),
                whole((width,)),
                table_spec(3, 3, width),
                table_spec(4, 4, width),
                hidden_spec(5, hidden),
                table_spec(3, 3, width),
                hidden_spec(4, hidden),
                table_spec(4, 5, width),
            ],
            out_specs=[whole((256, width))] * 2 + [tile(width), tile(width)] + [whole((4, 24, width))] * 2,
            scratch_shapes=[
                VMEM((512, width), BF),
                VMEM((width, width), BF),
                VMEM((width, hidden), BF),
                VMEM((hidden, width), BF),
                VMEM((512, width), BF),
                VMEM((RANK, width), F32),
                VMEM((RANK, width), F32),
                VMEM((RANK, hidden), F32),
                VMEM((RANK, width), F32),
                VMEM((RANK, hidden), F32),
                VMEM((RANK, width), F32),
                VMEM((4, 3 * RANK, 768), F32),
                pltpu.SemaphoreType.DMA((25,)),
                pltpu.SemaphoreType.DMA((31,)),
                pltpu.SemaphoreType.DMA((49,)),
                pltpu.SemaphoreType.DMA((2,)),
            ],
        ),
        out_shape=[jax.ShapeDtypeStruct((256, width), BF)] * 2
        + [jax.ShapeDtypeStruct((512, width), F32), jax.ShapeDtypeStruct((512, width), BF)]
        + [jax.ShapeDtypeStruct((4, 24, width), F32), jax.ShapeDtypeStruct((4, 24, width), BF)],
        compiler_params=pltpu.CompilerParams(vmem_limit_bytes=56 * MEBI),
        cost_estimate=SMALL_COST,
        name="second_half",
    )(meta, ids, *cots, out_own, up_own, down_own, *up_pieces, *down_pieces, normal, inverse, active, slope, mixed,
      gain1, gain2, table_in, table_in, table_in_hidden, table_out, table_out_hidden, table_out)


def first_grads_kernel(meta, ids, *refs):
    xs, dq_ref, dk_ref, dv_ref, got_ref = refs[0:5]
    ins, outs = refs[5:8], refs[8:11]
    grads_ref, rank_grad_ref = refs[11:13]
    own_half, other_half = refs[13:15]
    s_in, s_out, gathered = refs[15:]
    in_all = jnp.concatenate([ref[0, 0] for ref in ins], axis=0)
    out_all = jnp.concatenate([zero_padded(ref[0, 0], p, 3) for p, ref in enumerate(outs)], axis=1)
    for tile in range(2):
        rows = slice(256 * tile, 256 * tile + 256)
        grads = jnp.concatenate(
            [dq_ref[rows]]
            + [(ref[rows].astype(F32) + got_ref[n, rows].astype(F32)).astype(BF) for n, ref in enumerate((dk_ref, dv_ref))],
            axis=1,
        )
        grads_ref[rows] = grads
        x = xs[rows]
        rank = mm_nt(x, in_all).astype(BF)
        rank_grad = mm_nt(grads, out_all).astype(BF)
        rank_grad_ref[rows] = rank_grad
        part_in, part_out = mm_tn(rank_grad, x), mm_tn(rank, grads)
        if tile == 0:
            s_in[...] = part_in
            s_out[...] = part_out
        else:
            s_in[...] += part_in
            s_out[...] += part_out
    gathered[...] = jnp.zeros_like(gathered)
    for owner in range(4):
        for p in range(3):
            rows, columns = slice(RANK * p, RANK * p + RANK), slice(192 * owner, 192 * owner + 192)
            gathered[owner, 0:16, 192 * p : 192 * p + 192] = s_in[rows, columns]
            columns = slice(768 * p + 192 * owner, 768 * p + 192 * owner + 192)
            at = (0, 576) if p == 0 else (16, 192 * (p - 1))
            gathered[owner, at[0] : at[0] + 16, at[1] : at[1] + 192] = s_out[rows, columns]
    write_halves(meta, gathered, 2, own_half, other_half)


def first_grads(meta, ids, x, dq, dk, dv, got, table_in, table_out):
    width = x.shape[1]
    return pl.pallas_call(
        first_grads_kernel,
        grid_spec=pltpu.PrefetchScalarGridSpec(
            num_scalar_prefetch=2,
            grid=(1,),
            in_specs=[whole((512, width))] * 4
            + [whole((2, 512, width))]
            + [table_spec(p, p, width) for p in range(3)] * 2,
            out_specs=[whole((512, 3 * width)), whole((512, 3 * RANK))] + [whole((4, 16, width))] * 2,
            scratch_shapes=[
                VMEM((3 * RANK, width), F32),
                VMEM((3 * RANK, 3 * width), F32),
                VMEM((4, 2 * RANK, 768), F32),
            ],
        ),
        out_shape=[jax.ShapeDtypeStruct((512, 3 * width), BF), jax.ShapeDtypeStruct((512, 3 * RANK), BF)]
        + [jax.ShapeDtypeStruct((4, 16, width), F32), jax.ShapeDtypeStruct((4, 16, width), BF)],
        compiler_params=pltpu.CompilerParams(vmem_limit_bytes=30 * MEBI),
        cost_estimate=SMALL_COST,
        name="first_grads",
    )(meta, ids, x, dq, dk, dv, got, *([table_in] * 3), *([table_out] * 3))


def input_grad_kernel(meta, ids, *refs):
    w_own, pieces = refs[0], one_each(refs[1:9])
    branch_ref, grads_ref, rank_grad_ref = refs[9:12]
    ins, parts = refs[12:15], refs[15:17]
    weight, wsems = refs[17:]
    copies = weight_copies(meta, w_own, pieces, weight, wsems, qkv_places)
    for copy in copies:
        copy.start()
    for copy in copies:
        copy.wait()
    in_all = jnp.concatenate([ref[0, 0] for ref in ins], axis=0)
    for r, ref in enumerate(parts):
        rows = pl.ds(pl.multiple_of(256 * ((meta[0] & 1) ^ r), 256), 256)
        ref[...] = (
            branch_ref[rows, :] + mm_nt(grads_ref[rows, :], weight[...]) + mm(rank_grad_ref[rows, :], in_all)
        ).astype(BF)


def project_back(meta, ids, w_own, pieces, branch, grads, rank_grad, table_in):
    width = branch.shape[1]
    return pl.pallas_call(
        input_grad_kernel,
        grid_spec=pltpu.PrefetchScalarGridSpec(
            num_scalar_prefetch=2,
            grid=(1,),
            in_specs=any_specs(9)
            + [whole((512, width)), whole((512, 3 * width)), whole((512, 3 * RANK))]
            + [table_spec(p, p, width) for p in range(3)],
            out_specs=[whole((256, width))] * 2,
            scratch_shapes=[VMEM((width, 3 * width), BF), pltpu.SemaphoreType.DMA((25,))],
        ),
        out_shape=[jax.ShapeDtypeStruct((256, width), BF)] * 2,
        compiler_params=pltpu.CompilerParams(vmem_limit_bytes=30 * MEBI),
        cost_estimate=SMALL_COST,
        name="project_back",
    )(meta, ids, w_own, *pieces, branch, grads, rank_grad, *([table_in] * 3))


def sum_cores_kernel(ids, mid_own, mid_other, first_own, first_other, *messages):
    row = lax.broadcasted_iota(jnp.int32, (16, 768), 0)
    lane = lax.broadcasted_iota(jnp.int32, (16, 768), 1)
    for r, ref in enumerate(messages):
        mid = mid_own[r] + mid_other[r].astype(F32)
        first = first_own[r] + first_other[r].astype(F32)
        for p in range(6):
            first = jnp.where((row >= 8) & (lane == 384 + p), ids[p].astype(F32), first)
        ref[...] = jnp.concatenate([mid, first], axis=0).astype(BF)


def sum_cores(ids, *halves):
    width = halves[0].shape[-1]
    return pl.pallas_call(
        sum_cores_kernel,
        grid_spec=pltpu.PrefetchScalarGridSpec(
            num_scalar_prefetch=1,
            grid=(1,),
            in_specs=[whole(half.shape) for half in halves],
            out_specs=[whole((40, width))] * 4,
        ),
        out_shape=[jax.ShapeDtypeStruct((40, width), BF)] * 4,
        compiler_params=pltpu.CompilerParams(vmem_limit_bytes=30 * MEBI),
        cost_estimate=SMALL_COST,
        name="sum_cores",
    )(ids, *halves)


def combine_kernel(ids, meta, own, other, in_d, in_f, out_d, out_f):
    for ref in (in_d, in_f, out_d, out_f):
        ref[...] = jnp.zeros_like(ref)
    narrow = in_d.shape[-1]
    for chip in range(4):
        for r in range(4):
            chosen = [ids[(chip * 4 + r) * 6 + p] for p in range(6)]
            for half, messages in enumerate((own, other)):
                ranks = pl.ds(pl.multiple_of(8 * ((meta[1] & 1) ^ half), 8), 8)
                part = messages[chip, r].astype(F32)
                in_f[chosen[5], ranks, :] += part[0:8]
                out_f[chosen[4], ranks, :] += part[8:16]
                for at, (ref, p, which) in enumerate(
                    (
                        (in_d, 3, 3), (in_d, 4, 4), (out_d, 3, 3), (out_d, 4, 5),
                        (in_d, 0, 0), (in_d, 1, 1), (in_d, 2, 2), (out_d, 0, 0),
                        (out_d, 1, 1), (out_d, 2, 2),
                    )
                ):
                    row, column = 16 + 8 * (at // 4), narrow * (at % 4)
                    ref[p, chosen[which], ranks, :] += part[row : row + 8, column : column + narrow]


def combine(ids, meta, own, other, tables, narrow, wide):
    shapes = [(5, tables, RANK, narrow), (tables, RANK, wide)] * 2
    return pl.pallas_call(
        combine_kernel,
        grid_spec=pltpu.PrefetchScalarGridSpec(
            num_scalar_prefetch=2,
            grid=(1,),
            in_specs=[whole(own.shape)] * 2,
            out_specs=[whole(shape) for shape in shapes],
        ),
        out_shape=[jax.ShapeDtypeStruct(shape, F32) for shape in shapes],
        compiler_params=pltpu.CompilerParams(vmem_limit_bytes=30 * MEBI),
        cost_estimate=SMALL_COST,
        name="combine",
    )(ids, meta, own, other)


def after(value, *others):
    return lax.optimization_barrier((value, *others))[0]


def beside(work, transfers, values, moved):
    given = lax.optimization_barrier((tuple(values), tuple(moved)))
    return lax.optimization_barrier((tuple(work(*given[0])), tuple(transfers(*given[1]))))


def paired_body(
    inputs,
    segments,
    random_key_blocks,
    adapter_index_table,
    frozen_query_key_value_weight,
    frozen_output_weight,
    frozen_up_weight,
    frozen_down_weight,
    attention_norm_gain,
    feedforward_norm_gain,
    adapter_down_from_width,
    adapter_down_from_hidden,
    adapter_up_to_width,
    adapter_up_to_hidden,
    cotangent,
):
    dp_count, shard_count = lax.axis_size("dp"), lax.axis_size("shard")
    d, z = lax.axis_index("dp"), lax.axis_index("shard")
    core = d & 1
    meta = jnp.stack([z, d]).astype(jnp.int32)

    def piece(weight, rows, columns, row, column):
        return lax.dynamic_slice(weight, (row, column), (rows, columns))

    def fetch(part):
        return [swap_shards(part, shard_count, step) for step in range(1, shard_count)]

    def slices(values):
        return [lax.dynamic_index_in_dim(values, (z & 1) ^ r, 0, keepdims=False) for r in range(2)]

    def chips(block, *offsets):
        return [swap_chips(block, dp_count, offset) for offset in offsets]

    def swap(block):
        return swap_cores(block, dp_count)

    qkv_own = jnp.stack(fetch(piece(frozen_query_key_value_weight, 48, 1152, (d >> 1) * 48, core * 1152)))
    up_piece = jnp.concatenate(
        [
            piece(frozen_output_weight, 48, 384, (d >> 1) * 48, core * 384),
            piece(frozen_up_weight, 192, 384, 0, d * 384),
        ],
        axis=0,
    )
    down_piece = piece(frozen_down_weight, 96, 768, d * 96, 0)
    down_piece = jnp.concatenate([down_piece[:, 0:384], down_piece[:, 384:768]], axis=0)
    seg_rows = jnp.pad(segments.astype(BF)[:, None, :], ((0, 0), (0, 15), (0, inputs.shape[-1] - 256)))
    own = send_away(slices(jnp.concatenate([inputs, seg_rows], axis=1)), dp_count, shard_count)
    there = swap_cores(adapter_index_table, dp_count)
    column_ids = jnp.where(
        core == 0,
        jnp.concatenate([adapter_index_table, there], axis=0),
        jnp.concatenate([there, adapter_index_table], axis=0),
    )
    ids = lax.dynamic_index_in_dim(column_ids, z, 0, keepdims=False)

    blocks = jnp.arange(16, dtype=jnp.int32)
    query_block = (8 * core + blocks[0:8])[None, :, None]
    key_block = jnp.where(blocks < 8, 8 * core + blocks, 8 * (1 - core) + blocks - 8)[None, None, :]
    drawn = lax.dynamic_slice_in_dim(random_key_blocks, 8 * core, 8, axis=1)
    allowed = (jnp.abs(query_block - key_block) <= 1) | (query_block < GLOBALS) | (key_block < GLOBALS)
    for n in range(RANDOMS):
        allowed = allowed | (drawn[:, :, n : n + 1] == key_block)
    closed = jnp.pad(jnp.where(allowed, 0.0, -BIG), ((0, 0), (0, 0), (16, 32)))
    closed = closed.reshape(H // 2, 2, 8, 64)
    closed = jnp.concatenate([closed[:, 1], closed[:, 0]], axis=-1)

    own, meta, closed, up_piece, down_piece = lax.optimization_barrier(
        (own, meta, closed, up_piece, down_piece)
    )
    tokens = own + [swap(part) for part in own]
    qkv_pieces = spread_over_cores((qkv_own, *chips(qkv_own, 2, 4, 6)), dp_count)
    up_own = fetch(after(up_piece, *own))

    def work(*given):
        return project_qkv(
            meta, ids, given[0:4], frozen_query_key_value_weight, given[4:],
            adapter_down_from_width, adapter_up_to_width,
        )

    (q, k, v, masks, hot, x), up_own = lax.optimization_barrier((work(*tokens, *qkv_pieces), up_own))
    up_own = jnp.stack(up_own)
    (mixed, shares), (up_x, up_y, *down_own) = beside(
        lambda *given: attend(*given, closed),
        lambda block, part: (*chips(block, 2, 4), *fetch(part)),
        (q, k, v, masks, hot),
        (up_own, down_piece),
    )
    down_own = jnp.stack(down_own)
    mixed, up_a, up_b, *others = lax.optimization_barrier(
        (
            mixed,
            *chips(up_x[:, 0:UP_SPLIT], 4),
            *chips(up_y[:, UP_SPLIT:], 2),
            swap(up_own),
            swap(up_x),
            swap(up_y),
        )
    )
    up_pieces = (up_own, others[0], up_x, others[1], up_y, others[2], up_a, up_b, swap(up_a), swap(up_b))
    gain1, gain2 = attention_norm_gain, feedforward_norm_gain

    def work(mixed, *pieces):
        return first_half(
            meta, ids, frozen_output_weight, frozen_up_weight, pieces, x, mixed, gain1,
            adapter_down_from_width, adapter_up_to_width, adapter_up_to_hidden,
        )

    (normal, inverse, active, slope), (*down_pieces, cot_a, cot_b) = beside(
        work,
        lambda block, values: (*chips(block, 2, 4, 6), *send_away(slices(values), dp_count, shard_count)),
        (mixed, *up_pieces),
        (after(down_own, up_a, up_b), cotangent),
    )
    down_pieces = spread_over_cores((down_own, *down_pieces), dp_count)
    cots = (cot_a, cot_b)
    results = second_half(
        meta, ids, cots, frozen_output_weight, frozen_up_weight, frozen_down_weight, up_pieces, down_pieces,
        normal, inverse, active, slope, mixed, gain1, gain2,
        adapter_down_from_width, adapter_down_from_hidden, adapter_up_to_width, adapter_up_to_hidden,
    )
    grad_branch = results[2]

    def home(r, part):
        return lax.ppermute(part, ("dp", "shard"), away_pairs(dp_count, shard_count, r))

    def swap_over_shards(*parts):
        return [swap_shards(part, shard_count, step + 1) for step, part in enumerate(parts)]

    (dq, dk, dv, other_sums), (layer_a, layer_b) = beside(
        lambda grad: attend_back(q, k, v, shares, grad, mixed),
        lambda part_a, part_b: (home(0, part_a), home(1, part_b)),
        (results[3],),
        results[0:2],
    )
    grads, rank_grad, first_own, first_other = first_grads(
        meta, ids, x, dq, dk, dv, swap(other_sums), adapter_down_from_width, adapter_up_to_width
    )
    input_parts, (first_other, mid_other) = beside(
        lambda grads: project_back(
            meta, ids, frozen_query_key_value_weight, qkv_pieces, grad_branch, grads, rank_grad,
            adapter_down_from_width,
        ),
        lambda *halves: [swap(half) for half in halves],
        (grads,),
        (first_other, results[5]),
    )
    message, *others = sum_cores(ids, results[4], mid_other, first_own, first_other)
    (layer_out,), moved = beside(
        lambda *parts: (join_parts(meta, parts, BF),),
        swap_over_shards,
        (layer_a, layer_b),
        others,
    )
    messages = jnp.stack([message, *moved])
    _, (part_a, part_b, *moved) = beside(
        lambda: (),
        lambda part_a, part_b, block: (home(0, part_a), home(1, part_b), *chips(block, 2, 4, 6)),
        (),
        (*input_parts, messages),
    )
    messages = jnp.stack([messages, *moved])
    chosen = messages[:, :, 32, 384:390].astype(jnp.int32).reshape(-1)
    in_d, in_f, out_d, out_f = combine(
        chosen, meta, messages, swap(messages), adapter_down_from_width.shape[1], 192, 768
    )
    return (layer_out, join_parts(meta, (part_a, part_b), F32), in_d, in_f, out_d, out_f)


def solution(mesh):
    dp_count, shard_count = mesh.shape["dp"], mesh.shape["shard"]
    paired = dp_count == 8 and shard_count == 4
    return jax.shard_map(
        paired_body if paired else general_body,
        mesh=mesh,
        in_specs=(
            P("dp", "shard", None),
            P("dp", "shard"),
            P(),
            P("dp", None),
            P("shard", None),
            P("shard", None),
            P("shard", None),
            P("shard", None),
            P(),
            P(),
            P(),
            P(),
            P(),
            P(),
            P("dp", "shard", None),
        ),
        out_specs=(
            P("dp", "shard", None),
            P("dp", "shard", None),
            P(None, None, None, "shard"),
            P(None, None, "shard"),
            P(None, None, None, "shard"),
            P(None, None, "shard"),
        ),
        check_vma=False,
    )
```

profile of v0, /device:TPU:0, one launch (start us, length us, event | category | flops | bytes accessed | tf_op | source)
XLA Modules:
  0.0 218.9 jit_solution(11145872605356436387)
XLA Ops:
  1.6 5.1 %collective-permute-start.7 = (bf16[48,1152]{1,0:T(8,128)(2,1)S(1)}, bf16[48,1152]{1,0:T(8,128)(2,1)S(1)}, u32[]{:S(2)}, u32[]{:S(2)}) collective-permute-start(bf16[48,1152]{1,0:T(8,128)(2,1)S(1)} %dynamic_slice.40), channel_id=1, source_target_pairs={{0,3},{1,2},{2,1},{3,0},{4,7},{5,6},{6,5},{7,4},{8,11},{9,10},{10,... | collective-permute-start | bytes 331784 | tf_op jit(solution)/shard_map/ppermute | solution.py:514
  13.6 3.2 %collective-permute-done.6 = bf16[48,1152]{1,0:T(8,128)(2,1)S(1)} collective-permute-done((bf16[48,1152]{1,0:T(8,128)(2,1)S(1)}, bf16[48,1152]{1,0:T(8,128)(2,1)S(1)}, u32[]{:S(2)}, u32[]{:S(2)}) %collective-permute-start.6) | collective-permute-done | bytes 110624 | tf_op jit(solution)/shard_map/ppermute | solution.py:514
  16.8 2.3 %collective-permute-start.13 = (bf16[3,48,1152]{2,1,0:T(8,128)(2,1)S(1)}, bf16[3,48,1152]{2,1,0:T(8,128)(2,1)S(1)}, u32[]{:S(2)}, u32[]{:S(2)}) collective-permute-start(bf16[3,48,1152]{2,1,0:T(8,128)(2,1)S(1)} %pad_maximum_fusion.3.refs_5_.refs_1_), channel_id=1, source_target_pairs={{0,24},{4,28},{8,16},{12,20},{16,8},{20,12},{24,0},{28,4},{1,25},{... | collective-permute-start | bytes 995336 | tf_op jit(solution)/shard_map/ppermute | solution.py:523
  22.0 2.1 collective-permute-done.1.refs_1_
  24.9 3.7 %collective-permute-done.13.refs_11_.refs_7_ = bf16[3,48,1152]{2,1,0:T(8,128)(2,1)S(1)} collective-permute-done((bf16[3,48,1152]{2,1,0:T(8,128)(2,1)S(1)}, bf16[3,48,1152]{2,1,0:T(8,128)(2,1)S(1)}, u32[]{:S(2)}, u32[]{:S(2)}) %collective-permute-start.13) | collective-permute-done | bytes 331808 | tf_op jit(solution)/shard_map/ppermute | solution.py:523
  28.5 5.9 %collective-permute-done.11.refs_9_.refs_5_ = bf16[3,48,1152]{2,1,0:T(8,128)(2,1)S(1)} collective-permute-done((bf16[3,48,1152]{2,1,0:T(8,128)(2,1)S(1)}, bf16[3,48,1152]{2,1,0:T(8,128)(2,1)S(1)}, u32[]{:S(2)}, u32[]{:S(2)}) %collective-permute-start.11) | collective-permute-done | bytes 331808 | tf_op jit(solution)/shard_map/ppermute | solution.py:523
  40.2 2.3 %collective-permute-start.15 = (bf16[240,384]{1,0:T(8,128)(2,1)S(1)}, bf16[240,384]{1,0:T(8,128)(2,1)S(1)}, u32[]{:S(2)}, u32[]{:S(2)}) collective-permute-start(bf16[240,384]{1,0:T(8,128)(2,1)S(1)} %pad_maximum_fusion.5), channel_id=1, source_target_pairs={{0,1},{1,0},{2,3},{3,2},{4,5},{5,4},{6,7},{7,6},{8,9},{9,8},{10,11... | collective-permute-start | bytes 552968 | tf_op jit(solution)/shard_map/ppermute | solution.py:514
  43.8 11.2 %project_qkv.1 = (bf16[512,768]{1,0:T(8,128)(2,1)}, bf16[1024,768]{1,0:T(8,128)(2,1)}, bf16[1024,768]{1,0:T(8,128)(2,1)}, bf16[1024,128]{1,0:T(8,128)(2,1)}, bf1...) custom-call(s32[2]{0:T(128)} %pad_add_fusion.meta, s32[6]{0:T(128)} %fusion.5.ids, ...), custom_call_target="tpu_custom_call" | custom-call | flops 1000000 | bytes 100000 | tf_op jit(solution)/shard_map/project_qkv/pallas_call | solution.py:705
  55.0 1.7 collective-permute-done.16
  56.8 1.6 collective-permute-start.19
  60.4 3.2 %collective-permute-start.20 = (bf16[192,384]{1,0:T(8,128)(2,1)S(1)}, bf16[192,384]{1,0:T(8,128)(2,1)S(1)}, u32[]{:S(2)}, u32[]{:S(2)}) collective-permute-start(bf16[192,384]{1,0:T(8,128)(2,1)S(1)} %copy-done.50), channel_id=1, source_target_pairs={{0,1},{1,0},{2,3},{3,2},{4,5},{5,4},{6,7},{7,6},{8,9},{9,8},{10,11... | collective-permute-start | bytes 442376 | tf_op jit(solution)/shard_map/ppermute | solution.py:514
  63.6 14.0 %attend.1 = (bf16[512,768]{1,0:T(8,128)(2,1)}, bf16[12,512,1024]{2,1,0:T(8,128)(2,1)}) custom-call(bf16[512,768]{1,0:T(8,128)(2,1)} %get-tuple-element.154.q_ref, bf16[1024,768]{1,0:T(8,128)(2,1)} %get-tuple-element.155.k_ref, bf16[1024,768]{1,0:T(8,128)(2,1)} %get-tuple-element.156.v_ref, bf16[1024,128]{1,0:T(8,128)(2,1)} %get-tuple-element.157.mask_ref, ...), custom_call_target="tpu_custom_call" | custom-call | flops 1000000 | bytes 100000 | tf_op jit(solution)/shard_map/attend/pallas_call | solution.py:775
  80.3 7.7 %collective-permute-done.24.refs_9_.refs_12_ = bf16[3,112,384]{2,1,0:T(8,128)(2,1)S(1)} collective-permute-done((bf16[3,112,384]{2,1,0:T(8,128)(2,1)S(1)}, bf16[3,112,384]{2,1,0:T(8,128)(2,1)S(1)}, u32[]{:S(2)}, u32[]{:S(2)}) %collective-permute-start.24) | collective-permute-done | bytes 258080 | tf_op jit(solution)/shard_map/ppermute | solution.py:523
  90.2 1.6 collective-permute-start.32
  94.8 18.3 %first_half.1 = (f32[512,768]{1,0:T(8,128)}, f32[512,128]{1,0:T(8,128)}, bf16[512,3072]{1,0:T(8,128)(2,1)}, bf16[512,3072]{1,0:T(8,128)(2,1)}) custom-call(s32[2]{0:T(128)} %pad_add_fusion.meta, s32[6]{0:T(128)} %fusion.5.ids, bf16[192,768]{1,0:T(8,128)(2,1)} %refs_2_.1, bf16[192,3072]{1,0:T(8,128)(2,1)} %refs_3_.1, bf16[3,240,384]{2,1,0:T(8,128)(2,1)} %copy-done.27, ...), custom_call_target="tpu_custom_call" | custom-call | flops 1000000 | bytes 100000 | tf_op jit(solution)/shard_map/first_half/pallas_call | solution.py:923
  113.1 2.6 %collective-permute-start.35 = (bf16[3,192,384]{2,1,0:T(8,128)(2,1)S(1)}, bf16[3,192,384]{2,1,0:T(8,128)(2,1)S(1)}, u32[]{:S(2)}, u32[]{:S(2)}) collective-permute-start(bf16[3,192,384]{2,1,0:T(8,128)(2,1)S(1)} %pad_maximum_fusion.2.refs_15_), channel_id=1, source_target_pairs={{0,4},{4,0},{8,12},{12,8},{16,20},{20,16},{24,28},{28,24},{1,5},{5... | collective-permute-start | bytes 1327112 | tf_op jit(solution)/shard_map/ppermute | solution.py:510
  120.0 29.1 %second_half.1 = (bf16[256,768]{1,0:T(8,128)(2,1)}, bf16[256,768]{1,0:T(8,128)(2,1)}, f32[512,768]{1,0:T(8,128)}, bf16[512,768]{1,0:T(8,128)(2,1)}, f32[4,24,768]{2,1,0:T(8,128)}, /*index=5*/bf16[4,24,768]{2,1,0:T(8,128)(2,1)}) custom-call(s32[2]{0:T(128)} %pad_add_fusion.meta, s32[6]{0:T(128)} %fusion.5.ids, bf16[256,768]{1,0:T(8,128)(2,1)} %copy-done.49, ...), custom_call_target="tpu_custom_call" | custom-call | flops 1000000 | bytes 100000 | tf_op jit(solution)/shard_map/second_half/pallas_call | solution.py:1061
  149.1 1.8 collective-permute-start.39
  150.9 2.0 collective-permute-start.40
  152.9 15.1 %attend_back.1 = (bf16[512,768]{1,0:T(8,128)(2,1)}, bf16[512,768]{1,0:T(8,128)(2,1)}, bf16[512,768]{1,0:T(8,128)(2,1)}, bf16[2,512,768]{2,1,0:T(8,128)(2,1)}) custom-call(bf16[512,768]{1,0:T(8,128)(2,1)} %get-tuple-element.154.q_ref, bf16[1024,768]{1,0:T(8,128)(2,1)} %get-tuple-element.155.k_ref, bf16[1024,768]{1,0:T(8,128)(2,1)} %get-tuple-element.156.v_ref, ...), custom_call_target="tpu_custom_call" | custom-call | flops 1000000 | bytes 100000 | tf_op jit(solution)/shard_map/attend_back/pallas_call | solution.py:827
  168.2 3.0 %collective-permute-start.41 = (bf16[2,512,768]{2,1,0:T(8,128)(2,1)}, bf16[2,512,768]{2,1,0:T(8,128)(2,1)S(1)}, u32[]{:S(2)}, u32[]{:S(2)}) collective-permute-start(bf16[2,512,768]{2,1,0:T(8,128)(2,1)} %get-tuple-element.222), channel_id=1, source_target_pairs={{0,4},{4,0},{8,12},{12,8},{16,20},{20,16},{24,28},{28,24},{1,5},{5... | collective-permute-start | bytes 4718600 | tf_op jit(solution)/shard_map/ppermute | solution.py:510
  171.1 3.2 %collective-permute-done.41.refs_4_ = bf16[2,512,768]{2,1,0:T(8,128)(2,1)S(1)} collective-permute-done((bf16[2,512,768]{2,1,0:T(8,128)(2,1)}, bf16[2,512,768]{2,1,0:T(8,128)(2,1)S(1)}, u32[]{:S(2)}, u32[]{:S(2)}) %collective-permute-start.41) | collective-permute-done | bytes 1572896 | tf_op jit(solution)/shard_map/ppermute | solution.py:510
  177.8 2.6 %first_grads.1 = (bf16[512,2304]{1,0:T(8,128)(2,1)S(1)}, bf16[512,48]{1,0:T(8,128)(2,1)S(1)}, f32[4,16,768]{2,1,0:T(8,128)S(1)}, bf16[4,16,768]{2,1,0:T(8,128)(2,1)S(1)}) custom-call(s32[2]{0:T(128)S(1)} %copy-done.25, s32[6]{0:T(128)S(1)} %copy-done.26, bf16[512,768]{1,0:T(8,128)(2,1)S(1)} %copy-done.3, bf16[512,768]{1,0:T(8,128)(2,1)S(1)} %copy-done.21, ...), custom_call_target="tpu_custom_call" | custom-call | flops 1000000 | bytes 100000 | tf_op jit(solution)/shard_map/first_grads/pallas_call | solution.py:1152
  181.1 4.1 %project_back.1 = (bf16[256,768]{1,0:T(8,128)(2,1)S(1)}, bf16[256,768]{1,0:T(8,128)(2,1)S(1)}) custom-call(s32[2]{0:T(128)S(1)} %copy-done.25, s32[6]{0:T(128)S(1)} %copy-done.26, bf16[192,2304]{1,0:T(8,128)(2,1)S(1)} %copy-done.2, bf16[3,48,1152]{2,1,0:T(8,128)(2,1)S(1)} %copy-done.5, bf16[3,48,1152]{2,1,0:T(8,128)(2,1)S(1)} %copy-done.14, ...), custom_call_target="tpu_custom_call" | custom-call | flops 1000000 | bytes 100000 | tf_op jit(solution)/shard_map/project_back/pallas_call | solution.py:1195
  185.8 2.3 %collective-permute-start.44 = (bf16[40,768]{1,0:T(8,128)(2,1)S(1)}, bf16[40,768]{1,0:T(8,128)(2,1)S(1)}, u32[]{:S(2)}, u32[]{:S(2)}) collective-permute-start(bf16[40,768]{1,0:T(8,128)(2,1)S(1)} %get-tuple-element.240), channel_id=1, source_target_pairs={{0,1},{1,0},{2,3},{3,2},{4,5},{5,4},{6,7},{7,6},{8,9},{9,8},{10,11... | collective-permute-start | bytes 184328 | tf_op jit(solution)/shard_map/ppermute | solution.py:514
  188.7 1.8 collective-permute-start.46
  192.0 3.9 %collective-permute-done.45 = bf16[40,768]{1,0:T(8,128)(2,1)S(1)} collective-permute-done((bf16[40,768]{1,0:T(8,128)(2,1)S(1)}, bf16[40,768]{1,0:T(8,128)(2,1)S(1)}, u32[]{:S(2)}, u32[]{:S(2)}) %collective-permute-start.45) | collective-permute-done | bytes 61472 | tf_op jit(solution)/shard_map/ppermute | solution.py:514
  196.7 1.5 collective-permute-start.48
  201.7 4.2 %collective-permute-done.51 = bf16[4,40,768]{2,1,0:T(8,128)(2,1)S(1)} collective-permute-done((bf16[4,40,768]{2,1,0:T(8,128)(2,1)S(1)}, bf16[4,40,768]{2,1,0:T(8,128)(2,1)S(1)}, u32[]{:S(2)}, u32[]{:S(2)}) %collective-permute-start.51) | collective-permute-done | bytes 245792 | tf_op jit(solution)/shard_map/ppermute | solution.py:523
  206.0 7.2 %collective-permute-done.50 = bf16[4,40,768]{2,1,0:T(8,128)(2,1)S(1)} collective-permute-done((bf16[4,40,768]{2,1,0:T(8,128)(2,1)S(1)}, bf16[4,40,768]{2,1,0:T(8,128)(2,1)S(1)}, u32[]{:S(2)}, u32[]{:S(2)}) %collective-permute-start.50) | collective-permute-done | bytes 245792 | tf_op jit(solution)/shard_map/ppermute | solution.py:523
  214.1 1.8 join_parts.3
  216.1 2.8 %combine.1 = (f32[5,8,16,192]{3,2,1,0:T(8,128)}, f32[8,16,768]{2,1,0:T(8,128)}, f32[5,8,16,192]{3,2,1,0:T(8,128)}, f32[8,16,768]{2,1,0:T(8,128)}) custom-call(s32[96]{0:T(128)S(1)} %reshape.102.ids, s32[2]{0:T(128)S(1)} %copy-done.25, bf16[4,4,40,768]{3,2,1,0:T(8,128)(2,1)S(1)} %pad_maximum_fusion.own, bf16[4,4,40,768]{3,2,1,0:T(8,128)(2,1)S(1)} %collective-permute-done.52.other), custom_call_target="tpu_custom_call" | custom-call | flops 1000000 | bytes 100000 | tf_op jit(solution)/shard_map/combine/pallas_call | solution.py:1266
  (227 shorter events, 44.4 us)
Async XLA Ops:
  1.6 12.0 %collective-permute-start.7 = (bf16[48,1152]{1,0:T(8,128)(2,1)S(1)}, bf16[48,1152]{1,0:T(8,128)(2,1)S(1)}, u32[]{:S(2)}, u32[]{:S(2)}) collective-permute-start(bf16[48,1152]{1,0:T(8,128)(2,1)S(1)} %dynamic_slice.40), channel_id=1, source_target_pairs={{0,3},{1,2},{2,1},{3,0},{4,7},{5,6},{6,5},{7,4},{8,11},{9,10},{10,... | collective-permute-start | bytes 331784 | tf_op jit(solution)/shard_map/ppermute | solution.py:514
  6.7 10.1 %collective-permute-start.6 = (bf16[48,1152]{1,0:T(8,128)(2,1)S(1)}, bf16[48,1152]{1,0:T(8,128)(2,1)S(1)}, u32[]{:S(2)}, u32[]{:S(2)}) collective-permute-start(bf16[48,1152]{1,0:T(8,128)(2,1)S(1)} %dynamic_slice.40), channel_id=1, source_target_pairs={{0,2},{1,3},{2,0},{3,1},{4,6},{5,7},{6,4},{7,5},{8,10},{9,11},{10,... | collective-permute-start | bytes 331784 | tf_op jit(solution)/shard_map/ppermute | solution.py:514
  6.7 10.1 %collective-permute-start.5 = (bf16[48,1152]{1,0:T(8,128)(2,1)S(1)}, bf16[48,1152]{1,0:T(8,128)(2,1)S(1)}, u32[]{:S(2)}, u32[]{:S(2)}) collective-permute-start(bf16[48,1152]{1,0:T(8,128)(2,1)S(1)} %dynamic_slice.40), channel_id=1, source_target_pairs={{0,1},{1,0},{2,3},{3,2},{4,5},{5,4},{6,7},{7,6},{8,9},{9,8},{10,11... | collective-permute-start | bytes 331784 | tf_op jit(solution)/shard_map/ppermute | solution.py:514
  9.3 14.8 %collective-permute-start.1 = (bf16[272,768]{1,0:T(8,128)(2,1)S(1)}, bf16[272,768]{1,0:T(8,128)(2,1)S(1)}, u32[]{:S(2)}, u32[]{:S(2)}) collective-permute-start(bf16[272,768]{1,0:T(8,128)(2,1)S(1)} %get-tuple-element.268), channel_id=1, source_target_pairs={{0,1},{1,0},{2,5},{3,4},{4,3},{5,2},{6,7},{7,6},{8,9},{9,8},{10,13... | collective-permute-start | bytes 1253384 | tf_op jit(solution)/shard_map/ppermute | solution.py:558
  10.7 25.6 %collective-permute-start = (bf16[272,768]{1,0:T(8,128)(2,1)S(1)}, bf16[272,768]{1,0:T(8,128)(2,1)}, u32[]{:S(2)}, u32[]{:S(2)}) collective-permute-start(bf16[272,768]{1,0:T(8,128)(2,1)S(1)} %get-tuple-element.269), channel_id=1, source_target_pairs={{0,0},{1,1},{2,4},{3,5},{4,2},{5,3},{6,6},{7,7},{8,8},{9,9},{10,12... | collective-permute-start | bytes 1253384 | tf_op jit(solution)/shard_map/ppermute | solution.py:558
  16.8 11.7 %collective-permute-start.13 = (bf16[3,48,1152]{2,1,0:T(8,128)(2,1)S(1)}, bf16[3,48,1152]{2,1,0:T(8,128)(2,1)S(1)}, u32[]{:S(2)}, u32[]{:S(2)}) collective-permute-start(bf16[3,48,1152]{2,1,0:T(8,128)(2,1)S(1)} %pad_maximum_fusion.3.refs_5_.refs_1_), channel_id=1, source_target_pairs={{0,24},{4,28},{8,16},{12,20},{16,8},{20,12},{24,0},{28,4},{1,25},{... | collective-permute-start | bytes 995336 | tf_op jit(solution)/shard_map/ppermute | solution.py:523
  19.2 15.3 %collective-permute-start.11 = (bf16[3,48,1152]{2,1,0:T(8,128)(2,1)S(1)}, bf16[3,48,1152]{2,1,0:T(8,128)(2,1)S(1)}, u32[]{:S(2)}, u32[]{:S(2)}) collective-permute-start(bf16[3,48,1152]{2,1,0:T(8,128)(2,1)S(1)} %pad_maximum_fusion.3.refs_5_.refs_1_), channel_id=1, source_target_pairs={{0,16},{4,20},{8,24},{12,28},{16,0},{20,4},{24,8},{28,12},{1,17},{... | collective-permute-start | bytes 995336 | tf_op jit(solution)/shard_map/ppermute | solution.py:523
  19.7 14.9 %collective-permute-start.9 = (bf16[3,48,1152]{2,1,0:T(8,128)(2,1)S(1)}, bf16[3,48,1152]{2,1,0:T(8,128)(2,1)S(1)}, u32[]{:S(2)}, u32[]{:S(2)}) collective-permute-start(bf16[3,48,1152]{2,1,0:T(8,128)(2,1)S(1)} %pad_maximum_fusion.3.refs_5_.refs_1_), channel_id=1, source_target_pairs={{0,8},{4,12},{8,0},{12,4},{16,24},{20,28},{24,16},{28,20},{1,9},{5... | collective-permute-start | bytes 995336 | tf_op jit(solution)/shard_map/ppermute | solution.py:523
  24.1 13.7 %collective-permute-start.8 = (bf16[3,48,1152]{2,1,0:T(8,128)(2,1)S(1)}, bf16[3,48,1152]{2,1,0:T(8,128)(2,1)S(1)}, u32[]{:S(2)}, u32[]{:S(2)}) collective-permute-start(bf16[3,48,1152]{2,1,0:T(8,128)(2,1)S(1)} %pad_maximum_fusion.3.refs_5_.refs_1_), channel_id=1, source_target_pairs={{0,4},{4,0},{8,12},{12,8},{16,20},{20,16},{24,28},{28,24},{1,5},{5... | collective-permute-start | bytes 995336 | tf_op jit(solution)/shard_map/ppermute | solution.py:510
  28.5 9.6 %collective-permute-start.14 = (bf16[3,48,1152]{2,1,0:T(8,128)(2,1)S(1)}, bf16[3,48,1152]{2,1,0:T(8,128)(2,1)S(1)}, u32[]{:S(2)}, u32[]{:S(2)}) collective-permute-start(bf16[3,48,1152]{2,1,0:T(8,128)(2,1)S(1)} %collective-permute-done.13.refs_11_.refs_7_), channel_id=1, source_target_pairs={{0,4},{4,0},{8,12},{12,8},{16,20},{20,16},{24,28},{28,24},{1,5},{5... | collective-permute-start | bytes 995336 | tf_op jit(solution)/shard_map/ppermute | solution.py:510
  38.1 16.8 %collective-permute-start.17 = (bf16[240,384]{1,0:T(8,128)(2,1)S(1)}, bf16[240,384]{1,0:T(8,128)(2,1)S(1)}, u32[]{:S(2)}, u32[]{:S(2)}) collective-permute-start(bf16[240,384]{1,0:T(8,128)(2,1)S(1)} %pad_maximum_fusion.5), channel_id=1, source_target_pairs={{0,3},{1,2},{2,1},{3,0},{4,7},{5,6},{6,5},{7,4},{8,11},{9,10},{10,... | collective-permute-start | bytes 552968 | tf_op jit(solution)/shard_map/ppermute | solution.py:514
  39.0 17.7 %collective-permute-start.16 = (bf16[240,384]{1,0:T(8,128)(2,1)S(1)}, bf16[240,384]{1,0:T(8,128)(2,1)S(1)}, u32[]{:S(2)}, u32[]{:S(2)}) collective-permute-start(bf16[240,384]{1,0:T(8,128)(2,1)S(1)} %pad_maximum_fusion.5), channel_id=1, source_target_pairs={{0,2},{1,3},{2,0},{3,1},{4,6},{5,7},{6,4},{7,5},{8,10},{9,11},{10,... | collective-permute-start | bytes 552968 | tf_op jit(solution)/shard_map/ppermute | solution.py:514
  40.2 16.5 %collective-permute-start.15 = (bf16[240,384]{1,0:T(8,128)(2,1)S(1)}, bf16[240,384]{1,0:T(8,128)(2,1)S(1)}, u32[]{:S(2)}, u32[]{:S(2)}) collective-permute-start(bf16[240,384]{1,0:T(8,128)(2,1)S(1)} %pad_maximum_fusion.5), channel_id=1, source_target_pairs={{0,1},{1,0},{2,3},{3,2},{4,5},{5,4},{6,7},{7,6},{8,9},{9,8},{10,11... | collective-permute-start | bytes 552968 | tf_op jit(solution)/shard_map/ppermute | solution.py:514
  56.8 20.9 %collective-permute-start.19 = (bf16[3,240,384]{2,1,0:T(8,128)(2,1)S(1)}, bf16[3,240,384]{2,1,0:T(8,128)(2,1)S(1)}, u32[]{:S(2)}, u32[]{:S(2)}) collective-permute-start(bf16[3,240,384]{2,1,0:T(8,128)(2,1)S(1)} %pad_maximum_fusion.1.refs_2_.refs_5_), channel_id=1, source_target_pairs={{0,16},{4,20},{8,24},{12,28},{16,0},{20,4},{24,8},{28,12},{1,17},{... | collective-permute-start | bytes 1658888 | tf_op jit(solution)/shard_map/ppermute | solution.py:523
  58.4 19.4 %collective-permute-start.18 = (bf16[3,240,384]{2,1,0:T(8,128)(2,1)S(1)}, bf16[3,240,384]{2,1,0:T(8,128)(2,1)S(1)}, u32[]{:S(2)}, u32[]{:S(2)}) collective-permute-start(bf16[3,240,384]{2,1,0:T(8,128)(2,1)S(1)} %pad_maximum_fusion.1.refs_2_.refs_5_), channel_id=1, source_target_pairs={{0,8},{4,12},{8,0},{12,4},{16,24},{20,28},{24,16},{28,20},{1,9},{5... | collective-permute-start | bytes 1658888 | tf_op jit(solution)/shard_map/ppermute | solution.py:523
  59.2 18.4 %collective-permute-start.22 = (bf16[192,384]{1,0:T(8,128)(2,1)S(1)}, bf16[192,384]{1,0:T(8,128)(2,1)S(1)}, u32[]{:S(2)}, u32[]{:S(2)}) collective-permute-start(bf16[192,384]{1,0:T(8,128)(2,1)S(1)} %copy-done.50), channel_id=1, source_target_pairs={{0,3},{1,2},{2,1},{3,0},{4,7},{5,6},{6,5},{7,4},{8,11},{9,10},{10,... | collective-permute-start | bytes 442376 | tf_op jit(solution)/shard_map/ppermute | solution.py:514
  60.4 17.4 %collective-permute-start.21 = (bf16[192,384]{1,0:T(8,128)(2,1)S(1)}, bf16[192,384]{1,0:T(8,128)(2,1)S(1)}, u32[]{:S(2)}, u32[]{:S(2)}) collective-permute-start(bf16[192,384]{1,0:T(8,128)(2,1)S(1)} %copy-done.50), channel_id=1, source_target_pairs={{0,2},{1,3},{2,0},{3,1},{4,6},{5,7},{6,4},{7,5},{8,10},{9,11},{10,... | collective-permute-start | bytes 442376 | tf_op jit(solution)/shard_map/ppermute | solution.py:514
  60.4 17.4 %collective-permute-start.20 = (bf16[192,384]{1,0:T(8,128)(2,1)S(1)}, bf16[192,384]{1,0:T(8,128)(2,1)S(1)}, u32[]{:S(2)}, u32[]{:S(2)}) collective-permute-start(bf16[192,384]{1,0:T(8,128)(2,1)S(1)} %copy-done.50), channel_id=1, source_target_pairs={{0,1},{1,0},{2,3},{3,2},{4,5},{5,4},{6,7},{7,6},{8,9},{9,8},{10,11... | collective-permute-start | bytes 442376 | tf_op jit(solution)/shard_map/ppermute | solution.py:514
  77.8 10.3 %collective-permute-start.26 = (bf16[3,240,384]{2,1,0:T(8,128)(2,1)S(1)}, bf16[3,240,384]{2,1,0:T(8,128)(2,1)S(1)}, u32[]{:S(2)}, u32[]{:S(2)}) collective-permute-start(bf16[3,240,384]{2,1,0:T(8,128)(2,1)S(1)} %collective-permute-done.18.refs_4_.refs_7_), channel_id=1, source_target_pairs={{0,4},{4,0},{8,12},{12,8},{16,20},{20,16},{24,28},{28,24},{1,5},{5... | collective-permute-start | bytes 1658888 | tf_op jit(solution)/shard_map/ppermute | solution.py:510
  78.3 9.8 %collective-permute-start.27 = (bf16[3,240,384]{2,1,0:T(8,128)(2,1)S(1)}, bf16[3,240,384]{2,1,0:T(8,128)(2,1)S(1)}, u32[]{:S(2)}, u32[]{:S(2)}) collective-permute-start(bf16[3,240,384]{2,1,0:T(8,128)(2,1)S(1)} %collective-permute-done.19.refs_6_.refs_9_), channel_id=1, source_target_pairs={{0,4},{4,0},{8,12},{12,8},{16,20},{20,16},{24,28},{28,24},{1,5},{5... | collective-permute-start | bytes 1658888 | tf_op jit(solution)/shard_map/ppermute | solution.py:510
  78.4 9.7 %collective-permute-start.23 = (bf16[3,128,384]{2,1,0:T(8,128)(2,1)S(1)}, bf16[3,128,384]{2,1,0:T(8,128)(2,1)S(1)}, u32[]{:S(2)}, u32[]{:S(2)}) collective-permute-start(bf16[3,128,384]{2,1,0:T(8,128)(2,1)S(1)} %slice.41), channel_id=1, source_target_pairs={{0,16},{4,20},{8,24},{12,28},{16,0},{20,4},{24,8},{28,12},{1,17},{... | collective-permute-start | bytes 884744 | tf_op jit(solution)/shard_map/ppermute | solution.py:523
  90.2 25.6 %collective-permute-start.32 = (bf16[3,192,384]{2,1,0:T(8,128)(2,1)S(1)}, bf16[3,192,384]{2,1,0:T(8,128)(2,1)S(1)}, u32[]{:S(2)}, u32[]{:S(2)}) collective-permute-start(bf16[3,192,384]{2,1,0:T(8,128)(2,1)S(1)} %pad_maximum_fusion.2.refs_15_), channel_id=1, source_target_pairs={{0,24},{4,28},{8,16},{12,20},{16,8},{20,12},{24,0},{28,4},{1,25},{... | collective-permute-start | bytes 1327112 | tf_op jit(solution)/shard_map/ppermute | solution.py:523
  91.7 24.0 %collective-permute-start.31 = (bf16[3,192,384]{2,1,0:T(8,128)(2,1)S(1)}, bf16[3,192,384]{2,1,0:T(8,128)(2,1)S(1)}, u32[]{:S(2)}, u32[]{:S(2)}) collective-permute-start(bf16[3,192,384]{2,1,0:T(8,128)(2,1)S(1)} %pad_maximum_fusion.2.refs_15_), channel_id=1, source_target_pairs={{0,16},{4,20},{8,24},{12,28},{16,0},{20,4},{24,8},{28,12},{1,17},{... | collective-permute-start | bytes 1327112 | tf_op jit(solution)/shard_map/ppermute | solution.py:523
  92.7 23.1 %collective-permute-start.30 = (bf16[3,192,384]{2,1,0:T(8,128)(2,1)S(1)}, bf16[3,192,384]{2,1,0:T(8,128)(2,1)S(1)}, u32[]{:S(2)}, u32[]{:S(2)}) collective-permute-start(bf16[3,192,384]{2,1,0:T(8,128)(2,1)S(1)} %pad_maximum_fusion.2.refs_15_), channel_id=1, source_target_pairs={{0,8},{4,12},{8,0},{12,4},{16,24},{20,28},{24,16},{28,20},{1,9},{5... | collective-permute-start | bytes 1327112 | tf_op jit(solution)/shard_map/ppermute | solution.py:523
  93.8 19.3 %collective-permute-start.34 = (bf16[256,768]{1,0:T(8,128)(2,1)S(1)}, bf16[256,768]{1,0:T(8,128)(2,1)S(1)}, u32[]{:S(2)}, u32[]{:S(2)}) collective-permute-start(bf16[256,768]{1,0:T(8,128)(2,1)S(1)} %get-tuple-element.270), channel_id=1, source_target_pairs={{0,1},{1,0},{2,5},{3,4},{4,3},{5,2},{6,7},{7,6},{8,9},{9,8},{10,13... | collective-permute-start | bytes 1179656 | tf_op jit(solution)/shard_map/ppermute | solution.py:558
  93.9 21.8 %collective-permute-start.33 = (bf16[256,768]{1,0:T(8,128)(2,1)S(1)}, bf16[256,768]{1,0:T(8,128)(2,1)S(1)}, u32[]{:S(2)}, u32[]{:S(2)}) collective-permute-start(bf16[256,768]{1,0:T(8,128)(2,1)S(1)} %get-tuple-element.271), channel_id=1, source_target_pairs={{0,0},{1,1},{2,4},{3,5},{4,2},{5,3},{6,6},{7,7},{8,8},{9,9},{10,12... | collective-permute-start | bytes 1179656 | tf_op jit(solution)/shard_map/ppermute | solution.py:558
  149.1 18.9 %collective-permute-start.39 = (bf16[256,768]{1,0:T(8,128)(2,1)}, bf16[256,768]{1,0:T(8,128)(2,1)S(1)}, u32[]{:S(2)}, u32[]{:S(2)}) collective-permute-start(bf16[256,768]{1,0:T(8,128)(2,1)} %get-tuple-element.213), channel_id=1, source_target_pairs={{0,0},{1,1},{2,4},{3,5},{4,2},{5,3},{6,6},{7,7},{8,8},{9,9},{10,12... | collective-permute-start | bytes 1179656 | tf_op jit(solution)/shard_map/ppermute | solution.py:1415
  150.9 17.2 %collective-permute-start.40 = (bf16[256,768]{1,0:T(8,128)(2,1)}, bf16[256,768]{1,0:T(8,128)(2,1)S(1)}, u32[]{:S(2)}, u32[]{:S(2)}) collective-permute-start(bf16[256,768]{1,0:T(8,128)(2,1)} %get-tuple-element.214), channel_id=1, source_target_pairs={{0,1},{1,0},{2,5},{3,4},{4,3},{5,2},{6,7},{7,6},{8,9},{9,8},{10,13... | collective-permute-start | bytes 1179656 | tf_op jit(solution)/shard_map/ppermute | solution.py:1415
  196.0 17.1 %collective-permute-start.47 = (bf16[256,768]{1,0:T(8,128)(2,1)S(1)}, bf16[256,768]{1,0:T(8,128)(2,1)S(1)}, u32[]{:S(2)}, u32[]{:S(2)}) collective-permute-start(bf16[256,768]{1,0:T(8,128)(2,1)S(1)} %get-tuple-element.250), channel_id=1, source_target_pairs={{0,0},{1,1},{2,4},{3,5},{4,2},{5,3},{6,6},{7,7},{8,8},{9,9},{10,12... | collective-permute-start | bytes 1179656 | tf_op jit(solution)/shard_map/ppermute | solution.py:1415
  196.7 16.4 %collective-permute-start.48 = (bf16[256,768]{1,0:T(8,128)(2,1)S(1)}, bf16[256,768]{1,0:T(8,128)(2,1)S(1)}, u32[]{:S(2)}, u32[]{:S(2)}) collective-permute-start(bf16[256,768]{1,0:T(8,128)(2,1)S(1)} %get-tuple-element.251), channel_id=1, source_target_pairs={{0,1},{1,0},{2,5},{3,4},{4,3},{5,2},{6,7},{7,6},{8,9},{9,8},{10,13... | collective-permute-start | bytes 1179656 | tf_op jit(solution)/shard_map/ppermute | solution.py:1415
  199.7 13.4 %collective-permute-start.50 = (bf16[4,40,768]{2,1,0:T(8,128)(2,1)S(1)}, bf16[4,40,768]{2,1,0:T(8,128)(2,1)S(1)}, u32[]{:S(2)}, u32[]{:S(2)}) collective-permute-start(bf16[4,40,768]{2,1,0:T(8,128)(2,1)S(1)} %get-tuple-element.252), channel_id=1, source_target_pairs={{0,16},{4,20},{8,24},{12,28},{16,0},{20,4},{24,8},{28,12},{1,17},{... | collective-permute-start | bytes 737288 | tf_op jit(solution)/shard_map/ppermute | solution.py:523
  200.6 12.5 %collective-permute-start.49 = (bf16[4,40,768]{2,1,0:T(8,128)(2,1)S(1)}, bf16[4,40,768]{2,1,0:T(8,128)(2,1)S(1)}, u32[]{:S(2)}, u32[]{:S(2)}) collective-permute-start(bf16[4,40,768]{2,1,0:T(8,128)(2,1)S(1)} %get-tuple-element.252), channel_id=1, source_target_pairs={{0,8},{4,12},{8,0},{12,4},{16,24},{20,28},{24,16},{28,20},{1,9},{5... | collective-permute-start | bytes 737288 | tf_op jit(solution)/shard_map/ppermute | solution.py:523
  (75 other events, 653.3 us)
where the time goes:
time: 222 us; the launch traced here: 219 us
  Pallas kernels  101 us (45%)
  starting transfers between devices  53.8 us (24%)
  waiting for transfers between devices  48.4 us (22%)
  local copies, waits for them, and re-layouts  9.7 us (4%)
  other arithmetic  4.52 us (2%)
    pallas_call x1, Pallas kernels, second_half(): pl.pallas_call(second_half_kernel, grid_spec=pltpu.PrefetchScalarGridSpec...  29.1 us
    ppermute x13, waiting for transfers between devices, swap_chips(): return lax.ppermute(block, 'dp', [(i, i ^ offset) for i in range(dp_count)])  28.8 us
    ppermute x12, starting transfers between devices, swap_shards(): lax.ppermute(value, 'shard', [(i, i ^ step) for i in range(shard_count)])  19.3 us
    pallas_call x1, Pallas kernels, first_half(): pl.pallas_call(first_half_kernel, grid_spec=pltpu.PrefetchScalarGridSpec(...  18.3 us
    pallas_call x1, Pallas kernels, attend_back(): pl.pallas_call(attend_back_kernel, grid=(width // 128,), in_specs=[half,...  15.1 us
    ppermute x13, starting transfers between devices, swap_chips(): return lax.ppermute(block, 'dp', [(i, i ^ offset) for i in range(dp_count)])  14.8 us
    pallas_call x1, Pallas kernels, attend(): pl.pallas_call(attend_kernel, grid=(pairs,), in_specs=[half, full, full,...  14 us
    pallas_call x1, Pallas kernels, project_qkv(): pl.pallas_call(qkv_kernel, grid_spec=pltpu.PrefetchScalarGridSpec(num_sca...  11.2 us
  transfers between devices with their start and end apart: 53, of which 18 were waited for; matrix products, arithmetic and copies ran while one was open for 4% of the time, Pallas kernels for 30%

commit v1 on v0

--- a/solution.py
+++ b/solution.py
@@ -835,7 +835,7 @@
             jax.ShapeDtypeStruct((512, width), BF),
             jax.ShapeDtypeStruct((2, 512, width), BF),
         ],
-        compiler_params=pltpu.CompilerParams(vmem_limit_bytes=56 * MEBI),
+        compiler_params=pltpu.CompilerParams(vmem_limit_bytes=45 * MEBI),
         cost_estimate=SMALL_COST,
         name="attend_back",
     )(q, k, v, shares, grad, mixed)
@@ -949,7 +949,7 @@
             jax.ShapeDtypeStruct((512, hidden), BF),
             jax.ShapeDtypeStruct((512, hidden), BF),
         ],
-        compiler_params=pltpu.CompilerParams(vmem_limit_bytes=56 * MEBI),
+        compiler_params=pltpu.CompilerParams(vmem_limit_bytes=50 * MEBI),
         cost_estimate=SMALL_COST,
         name="first_half",
     )(meta, ids, out_own, up_own, *up_pieces, x, mixed, gain1, table_in, table_in, table_out, table_out_hidden)
@@ -1355,11 +1355,11 @@
     closed = closed.reshape(H // 2, 2, 8, 64)
     closed = jnp.concatenate([closed[:, 1], closed[:, 0]], axis=-1)
 
-    own, meta, closed, up_piece, down_piece = lax.optimization_barrier(
-        (own, meta, closed, up_piece, down_piece)
-    )
+    qkv_own, meta, up_piece = lax.optimization_barrier((qkv_own, meta, up_piece))
     tokens = own + [swap(part) for part in own]
-    qkv_pieces = spread_over_cores((qkv_own, *chips(qkv_own, 2, 4, 6)), dp_count)
+    qkv_x, qkv_y, qkv_xy = chips(qkv_own, 2, 4, 6)
+    qkv_xy, closed, down_piece, ids = lax.optimization_barrier((qkv_xy, closed, down_piece, ids))
+    qkv_pieces = spread_over_cores((qkv_own, qkv_x, qkv_y, qkv_xy), dp_count)
     up_own = fetch(after(up_piece, *own))
 
     def work(*given):
@@ -1370,24 +1370,26 @@
 
     (q, k, v, masks, hot, x), up_own = lax.optimization_barrier((work(*tokens, *qkv_pieces), up_own))
     up_own = jnp.stack(up_own)
-    (mixed, shares), (up_x, up_y, *down_own) = beside(
+    (mixed, shares), (up_x, up_y, up_there, down_1, down_2) = beside(
         lambda *given: attend(*given, closed),
-        lambda block, part: (*chips(block, 2, 4), *fetch(part)),
+        lambda block, part: (
+            *chips(block, 2, 4), swap(block), swap_shards(part, shard_count, 1), swap_shards(part, shard_count, 2)
+        ),
         (q, k, v, masks, hot),
         (up_own, down_piece),
     )
-    down_own = jnp.stack(down_own)
-    mixed, up_a, up_b, *others = lax.optimization_barrier(
+    mixed, up_a, up_b, up_x_there, up_y_there, down_3 = lax.optimization_barrier(
         (
             mixed,
             *chips(up_x[:, 0:UP_SPLIT], 4),
             *chips(up_y[:, UP_SPLIT:], 2),
-            swap(up_own),
             swap(up_x),
             swap(up_y),
-        )
-    )
-    up_pieces = (up_own, others[0], up_x, others[1], up_y, others[2], up_a, up_b, swap(up_a), swap(up_b))
+            swap_shards(after(down_piece, mixed), shard_count, 3),
+        )
+    )
+    down_own = jnp.stack([down_1, down_2, down_3])
+    up_pieces = (up_own, up_there, up_x, up_x_there, up_y, up_y_there, up_a, up_b, swap(up_a), swap(up_b))
     gain1, gain2 = attention_norm_gain, feedforward_norm_gain
 
     def work(mixed, *pieces):

time: 222 us -> 215 us (0.968)
  waiting for transfers between devices: 48.4 us -> 41.4 us
  starting transfers between devices: 53.8 us -> 56.2 us
    ppermute x13, waiting for transfers between devices: 28.8 us -> 22.5 us  [swap_chips(): return lax.ppermute(block, 'dp', [(i, i ^ offset) for i in range(dp_count)])]
    ppermute x20, starting transfers between devices: 9.84 us -> 12.2 us  [swap_cores(): return lax.ppermute(value, 'dp', [(i, i ^ 1) for i in range(dp_count)])]
    ppermute x12, waiting for transfers between devices: 8.9 us -> 11.2 us  [swap_shards(): lax.ppermute(value, 'shard', [(i, i ^ step) for i in range(shard_count)])]
    unnamed x109 -> x121, local copies, waits for them, and re-layouts: 5.19 us -> 4.41 us
where the time goes in v1:
time: 215 us; the launch traced here: 212 us
  Pallas kernels  99.6 us (46%)
  starting transfers between devices  56.2 us (26%)
  waiting for transfers between devices  41.4 us (19%)
  local copies, waits for them, and re-layouts  8.94 us (4%)
  other arithmetic  4.52 us (2%)
    pallas_call x1, Pallas kernels, second_half(): pl.pallas_call(second_half_kernel, grid_spec=pltpu.PrefetchScalarGridSpec...  29 us
    ppermute x13, waiting for transfers between devices, swap_chips(): return lax.ppermute(block, 'dp', [(i, i ^ offset) for i in range(dp_count)])  22.5 us
    ppermute x12, starting transfers between devices, swap_shards(): lax.ppermute(value, 'shard', [(i, i ^ step) for i in range(shard_count)])  19 us
    pallas_call x1, Pallas kernels, first_half(): pl.pallas_call(first_half_kernel, grid_spec=pltpu.PrefetchScalarGridSpec(...  16.7 us
    pallas_call x1, Pallas kernels, attend_back(): pl.pallas_call(attend_back_kernel, grid=(width // 128,), in_specs=[half,...  15.3 us
    ppermute x13, starting transfers between devices, swap_chips(): return lax.ppermute(block, 'dp', [(i, i ^ offset) for i in range(dp_count)])  14.9 us
    pallas_call x1, Pallas kernels, attend(): pl.pallas_call(attend_kernel, grid=(pairs,), in_specs=[half, full, full,...  14 us
    ppermute x20, starting transfers between devices, swap_cores(): return lax.ppermute(value, 'dp', [(i, i ^ 1) for i in range(dp_count)])  12.2 us
  transfers between devices with their start and end apart: 53, of which 18 were waited for; matrix products, arithmetic and copies ran while one was open for 4% of the time, Pallas kernels for 30%

profile of v1, /device:TPU:0, one launch (start us, length us, event | category | flops | bytes accessed | tf_op | source)
XLA Modules:
  0.0 212.2 jit_solution(17601397392311707108)
XLA Ops:
  1.6 5.1 %collective-permute-start.2 = (bf16[48,1152]{1,0:T(8,128)(2,1)S(1)}, bf16[48,1152]{1,0:T(8,128)(2,1)S(1)}, u32[]{:S(2)}, u32[]{:S(2)}) collective-permute-start(bf16[48,1152]{1,0:T(8,128)(2,1)S(1)} %dynamic_slice.33), channel_id=1, source_target_pairs={{0,3},{1,2},{2,1},{3,0},{4,7},{5,6},{6,5},{7,4},{8,11},{9,10},{10,... | collective-permute-start | bytes 331784 | tf_op jit(solution)/shard_map/ppermute | solution.py:514
  16.5 2.4 %collective-permute-start.3 = (bf16[3,48,1152]{2,1,0:T(8,128)(2,1)S(1)}, bf16[3,48,1152]{2,1,0:T(8,128)(2,1)S(1)}, u32[]{:S(2)}, u32[]{:S(2)}) collective-permute-start(bf16[3,48,1152]{2,1,0:T(8,128)(2,1)S(1)} %pad_maximum_fusion.3.refs_5_.refs_1_), channel_id=1, source_target_pairs={{0,24},{4,28},{8,16},{12,20},{16,8},{20,12},{24,0},{28,4},{1,25},{... | collective-permute-start | bytes 995336 | tf_op jit(solution)/shard_map/ppermute | solution.py:523
  20.8 6.0 %collective-permute-done.3.refs_11_.refs_7_ = bf16[3,48,1152]{2,1,0:T(8,128)(2,1)S(1)} collective-permute-done((bf16[3,48,1152]{2,1,0:T(8,128)(2,1)S(1)}, bf16[3,48,1152]{2,1,0:T(8,128)(2,1)S(1)}, u32[]{:S(2)}, u32[]{:S(2)}) %collective-permute-start.3) | collective-permute-done | bytes 331808 | tf_op jit(solution)/shard_map/ppermute | solution.py:523
  26.7 2.8 %collective-permute-start.9 = (bf16[3,48,1152]{2,1,0:T(8,128)(2,1)S(1)}, bf16[3,48,1152]{2,1,0:T(8,128)(2,1)S(1)}, u32[]{:S(2)}, u32[]{:S(2)}) collective-permute-start(bf16[3,48,1152]{2,1,0:T(8,128)(2,1)S(1)} %pad_maximum_fusion.3.refs_5_.refs_1_), channel_id=1, source_target_pairs={{0,4},{4,0},{8,12},{12,8},{16,20},{20,16},{24,28},{28,24},{1,5},{5... | collective-permute-start | bytes 995336 | tf_op jit(solution)/shard_map/ppermute | solution.py:510
  30.7 4.4 %collective-permute-done.12.refs_9_.refs_5_ = bf16[3,48,1152]{2,1,0:T(8,128)(2,1)S(1)} collective-permute-done((bf16[3,48,1152]{2,1,0:T(8,128)(2,1)S(1)}, bf16[3,48,1152]{2,1,0:T(8,128)(2,1)S(1)}, u32[]{:S(2)}, u32[]{:S(2)}) %collective-permute-start.12) | collective-permute-done | bytes 331808 | tf_op jit(solution)/shard_map/ppermute | solution.py:523
  39.0 2.2 %collective-permute-start.15 = (bf16[240,384]{1,0:T(8,128)(2,1)S(1)}, bf16[240,384]{1,0:T(8,128)(2,1)S(1)}, u32[]{:S(2)}, u32[]{:S(2)}) collective-permute-start(bf16[240,384]{1,0:T(8,128)(2,1)S(1)} %pad_maximum_fusion.5), channel_id=1, source_target_pairs={{0,1},{1,0},{2,3},{3,2},{4,5},{5,4},{6,7},{7,6},{8,9},{9,8},{10,11... | collective-permute-start | bytes 552968 | tf_op jit(solution)/shard_map/ppermute | solution.py:514
  42.7 11.2 %project_qkv.1 = (bf16[512,768]{1,0:T(8,128)(2,1)}, bf16[1024,768]{1,0:T(8,128)(2,1)}, bf16[1024,768]{1,0:T(8,128)(2,1)}, bf16[1024,128]{1,0:T(8,128)(2,1)}, bf1...) custom-call(s32[2]{0:T(128)} %pad_add_fusion.meta, s32[6]{0:T(128)} %fusion.5.ids, ...), custom_call_target="tpu_custom_call" | custom-call | flops 1000000 | bytes 100000 | tf_op jit(solution)/shard_map/project_qkv/pallas_call | solution.py:705
  55.5 1.6 collective-permute-start.19
  57.1 1.5 collective-permute-start.18
  58.6 3.1 %collective-permute-start.21 = (bf16[192,384]{1,0:T(8,128)(2,1)S(1)}, bf16[192,384]{1,0:T(8,128)(2,1)S(1)}, u32[]{:S(2)}, u32[]{:S(2)}) collective-permute-start(bf16[192,384]{1,0:T(8,128)(2,1)S(1)} %copy-done.56), channel_id=1, source_target_pairs={{0,1},{1,0},{2,3},{3,2},{4,5},{5,4},{6,7},{7,6},{8,9},{9,8},{10,11... | collective-permute-start | bytes 442376 | tf_op jit(solution)/shard_map/ppermute | solution.py:514
  61.7 14.0 %attend.1 = (bf16[512,768]{1,0:T(8,128)(2,1)}, bf16[12,512,1024]{2,1,0:T(8,128)(2,1)}) custom-call(bf16[512,768]{1,0:T(8,128)(2,1)} %get-tuple-element.157.q_ref, bf16[1024,768]{1,0:T(8,128)(2,1)} %get-tuple-element.158.k_ref, bf16[1024,768]{1,0:T(8,128)(2,1)} %get-tuple-element.159.v_ref, bf16[1024,128]{1,0:T(8,128)(2,1)} %get-tuple-element.160.mask_ref, ...), custom_call_target="tpu_custom_call" | custom-call | flops 1000000 | bytes 100000 | tf_op jit(solution)/shard_map/attend/pallas_call | solution.py:775
  78.9 5.9 %collective-permute-done.27 = bf16[192,384]{1,0:T(8,128)(2,1)S(1)} collective-permute-done((bf16[192,384]{1,0:T(8,128)(2,1)S(1)}, bf16[192,384]{1,0:T(8,128)(2,1)S(1)}, u32[]{:S(2)}, u32[]{:S(2)}) %collective-permute-start.27) | collective-permute-done | bytes 147488 | tf_op jit(solution)/shard_map/ppermute | solution.py:514
  87.6 1.9 collective-permute-start.32
  92.9 16.7 %first_half.1 = (f32[512,768]{1,0:T(8,128)}, f32[512,128]{1,0:T(8,128)S(1)}, bf16[512,3072]{1,0:T(8,128)(2,1)}, bf16[512,3072]{1,0:T(8,128)(2,1)}) custom-call(s32[2]{0:T(128)S(1)} %copy-done.36, s32[6]{0:T(128)S(1)} %copy-done.38, bf16[192,768]{1,0:T(8,128)(2,1)S(1)} %copy-done.14, bf16[192,3072]{1,0:T(8,128)(2,1)} %refs_3_.1, ...), custom_call_target="tpu_custom_call" | custom-call | flops 1000000 | bytes 100000 | tf_op jit(solution)/shard_map/first_half/pallas_call | solution.py:923
  110.4 2.0 collective-permute-start.35
  116.6 29.0 %second_half.1 = (bf16[256,768]{1,0:T(8,128)(2,1)}, bf16[256,768]{1,0:T(8,128)(2,1)}, f32[512,768]{1,0:T(8,128)}, bf16[512,768]{1,0:T(8,128)(2,1)}, f32[4,24,768]{2,1,0:T(8,128)}, /*index=5*/bf16[4,24,768]{2,1,0:T(8,128)(2,1)}) custom-call(s32[2]{0:T(128)} %pad_add_fusion.meta, s32[6]{0:T(128)} %fusion.5.ids, bf16[256,768]{1,0:T(8,128)(2,1)} %copy-done.55, ...), custom_call_target="tpu_custom_call" | custom-call | flops 1000000 | bytes 100000 | tf_op jit(solution)/shard_map/second_half/pallas_call | solution.py:1061
  145.7 1.8 collective-permute-start.39
  147.5 2.0 collective-permute-start.40
  150.7 15.3 %attend_back.1 = (bf16[512,768]{1,0:T(8,128)(2,1)S(1)}, bf16[512,768]{1,0:T(8,128)(2,1)S(1)}, bf16[512,768]{1,0:T(8,128)(2,1)S(1)}, bf16[2,512,768]{2,1,0:T(8,128)(2,1)S(1)}) custom-call(bf16[512,768]{1,0:T(8,128)(2,1)S(1)} %copy-done.7, bf16[1024,768]{1,0:T(8,128)(2,1)S(1)} %copy-done.3, bf16[1024,768]{1,0:T(8,128)(2,1)} %get-tuple-element.159.v_ref, ...), custom_call_target="tpu_custom_call" | custom-call | flops 1000000 | bytes 100000 | tf_op jit(solution)/shard_map/attend_back/pallas_call | solution.py:827
  166.1 3.0 %collective-permute-start.41 = (bf16[2,512,768]{2,1,0:T(8,128)(2,1)S(1)}, bf16[2,512,768]{2,1,0:T(8,128)(2,1)S(1)}, u32[]{:S(2)}, u32[]{:S(2)}) collective-permute-start(bf16[2,512,768]{2,1,0:T(8,128)(2,1)S(1)} %get-tuple-element.226), channel_id=1, source_target_pairs={{0,4},{4,0},{8,12},{12,8},{16,20},{20,16},{24,28},{28,24},{1,5},{5... | collective-permute-start | bytes 4718600 | tf_op jit(solution)/shard_map/ppermute | solution.py:510
  169.1 3.0 %collective-permute-done.41.refs_4_ = bf16[2,512,768]{2,1,0:T(8,128)(2,1)S(1)} collective-permute-done((bf16[2,512,768]{2,1,0:T(8,128)(2,1)S(1)}, bf16[2,512,768]{2,1,0:T(8,128)(2,1)S(1)}, u32[]{:S(2)}, u32[]{:S(2)}) %collective-permute-start.41) | collective-permute-done | bytes 1572896 | tf_op jit(solution)/shard_map/ppermute | solution.py:510
  172.2 2.6 %first_grads.1 = (bf16[512,2304]{1,0:T(8,128)(2,1)S(1)}, bf16[512,48]{1,0:T(8,128)(2,1)S(1)}, f32[4,16,768]{2,1,0:T(8,128)S(1)}, bf16[4,16,768]{2,1,0:T(8,128)(2,1)S(1)}) custom-call(s32[2]{0:T(128)S(1)} %copy-done.37, s32[6]{0:T(128)S(1)} %copy-done.39, bf16[512,768]{1,0:T(8,128)(2,1)S(1)} %copy-done.8, bf16[512,768]{1,0:T(8,128)(2,1)S(1)} %get-tuple-element.223.refs_1_, ...), custom_call_target="tpu_custom_call" | custom-call | flops 1000000 | bytes 100000 | tf_op jit(solution)/shard_map/first_grads/pallas_call | solution.py:1152
  175.5 4.1 %project_back.1 = (bf16[256,768]{1,0:T(8,128)(2,1)S(1)}, bf16[256,768]{1,0:T(8,128)(2,1)S(1)}) custom-call(s32[2]{0:T(128)S(1)} %copy-done.37, s32[6]{0:T(128)S(1)} %copy-done.39, bf16[192,2304]{1,0:T(8,128)(2,1)S(1)} %copy-done.5, bf16[3,48,1152]{2,1,0:T(8,128)(2,1)S(1)} %copy-done.10, bf16[3,48,1152]{2,1,0:T(8,128)(2,1)S(1)} %copy-done.22, ...), custom_call_target="tpu_custom_call" | custom-call | flops 1000000 | bytes 100000 | tf_op jit(solution)/shard_map/project_back/pallas_call | solution.py:1195
  181.1 2.1 collective-permute-start.45
  183.2 1.5 collective-permute-start.46
  184.7 1.5 join_parts.2
  186.1 3.2 %collective-permute-done.45 = bf16[40,768]{1,0:T(8,128)(2,1)S(1)} collective-permute-done((bf16[40,768]{1,0:T(8,128)(2,1)S(1)}, bf16[40,768]{1,0:T(8,128)(2,1)S(1)}, u32[]{:S(2)}, u32[]{:S(2)}) %collective-permute-start.45) | collective-permute-done | bytes 61472 | tf_op jit(solution)/shard_map/ppermute | solution.py:514
  191.4 2.1 collective-permute-start.51
  194.8 4.9 %collective-permute-done.51 = bf16[4,40,768]{2,1,0:T(8,128)(2,1)S(1)} collective-permute-done((bf16[4,40,768]{2,1,0:T(8,128)(2,1)S(1)}, bf16[4,40,768]{2,1,0:T(8,128)(2,1)S(1)}, u32[]{:S(2)}, u32[]{:S(2)}) %collective-permute-start.51) | collective-permute-done | bytes 245792 | tf_op jit(solution)/shard_map/ppermute | solution.py:523
  199.7 6.5 %collective-permute-done.50 = bf16[4,40,768]{2,1,0:T(8,128)(2,1)S(1)} collective-permute-done((bf16[4,40,768]{2,1,0:T(8,128)(2,1)S(1)}, bf16[4,40,768]{2,1,0:T(8,128)(2,1)S(1)}, u32[]{:S(2)}, u32[]{:S(2)}) %collective-permute-start.50) | collective-permute-done | bytes 245792 | tf_op jit(solution)/shard_map/ppermute | solution.py:523
  207.4 1.8 join_parts.3
  209.4 2.7 %combine.1 = (f32[5,8,16,192]{3,2,1,0:T(8,128)}, f32[8,16,768]{2,1,0:T(8,128)}, f32[5,8,16,192]{3,2,1,0:T(8,128)}, f32[8,16,768]{2,1,0:T(8,128)}) custom-call(s32[96]{0:T(128)S(1)} %reshape.102.ids, s32[2]{0:T(128)S(1)} %copy-done.37, bf16[4,4,40,768]{3,2,1,0:T(8,128)(2,1)S(1)} %pad_maximum_fusion.own, bf16[4,4,40,768]{3,2,1,0:T(8,128)(2,1)S(1)} %collective-permute-done.52.other), custom_call_target="tpu_custom_call" | custom-call | flops 1000000 | bytes 100000 | tf_op jit(solution)/shard_map/combine/pallas_call | solution.py:1266
  (239 shorter events, 42.7 us)
Async XLA Ops:
  1.6 12.9 %collective-permute-start.2 = (bf16[48,1152]{1,0:T(8,128)(2,1)S(1)}, bf16[48,1152]{1,0:T(8,128)(2,1)S(1)}, u32[]{:S(2)}, u32[]{:S(2)}) collective-permute-start(bf16[48,1152]{1,0:T(8,128)(2,1)S(1)} %dynamic_slice.33), channel_id=1, source_target_pairs={{0,3},{1,2},{2,1},{3,0},{4,7},{5,6},{6,5},{7,4},{8,11},{9,10},{10,... | collective-permute-start | bytes 331784 | tf_op jit(solution)/shard_map/ppermute | solution.py:514
  6.7 9.8 %collective-permute-start.1 = (bf16[48,1152]{1,0:T(8,128)(2,1)S(1)}, bf16[48,1152]{1,0:T(8,128)(2,1)S(1)}, u32[]{:S(2)}, u32[]{:S(2)}) collective-permute-start(bf16[48,1152]{1,0:T(8,128)(2,1)S(1)} %dynamic_slice.33), channel_id=1, source_target_pairs={{0,2},{1,3},{2,0},{3,1},{4,6},{5,7},{6,4},{7,5},{8,10},{9,11},{10,... | collective-permute-start | bytes 331784 | tf_op jit(solution)/shard_map/ppermute | solution.py:514
  6.7 9.8 %collective-permute-start = (bf16[48,1152]{1,0:T(8,128)(2,1)S(1)}, bf16[48,1152]{1,0:T(8,128)(2,1)S(1)}, u32[]{:S(2)}, u32[]{:S(2)}) collective-permute-start(bf16[48,1152]{1,0:T(8,128)(2,1)S(1)} %dynamic_slice.33), channel_id=1, source_target_pairs={{0,1},{1,0},{2,3},{3,2},{4,5},{5,4},{6,7},{7,6},{8,9},{9,8},{10,11... | collective-permute-start | bytes 331784 | tf_op jit(solution)/shard_map/ppermute | solution.py:514
  7.3 12.7 %collective-permute-start.4 = (s32[2,6]{1,0:T(2,128)}, s32[2,6]{1,0:T(2,128)S(1)}, u32[]{:S(2)}, u32[]{:S(2)}) collective-permute-start(s32[2,6]{1,0:T(2,128)} %param.18), channel_id=1, source_target_pairs={{0,4},{4,0},{8,12},{12,8},{16,20},{20,16},{24,28},{28,24},{1,5},{5... | collective-permute-start | bytes 152 | tf_op jit(solution)/shard_map/ppermute | solution.py:510
  10.1 25.6 %collective-permute-start.6 = (bf16[272,768]{1,0:T(8,128)(2,1)}, bf16[272,768]{1,0:T(8,128)(2,1)}, u32[]{:S(2)}, u32[]{:S(2)}) collective-permute-start(bf16[272,768]{1,0:T(8,128)(2,1)} %get-tuple-element.272), channel_id=1, source_target_pairs={{0,1},{1,0},{2,5},{3,4},{4,3},{5,2},{6,7},{7,6},{8,9},{9,8},{10,13... | collective-permute-start | bytes 1253384 | tf_op jit(solution)/shard_map/ppermute | solution.py:558
  14.5 21.4 %collective-permute-start.5 = (bf16[272,768]{1,0:T(8,128)(2,1)S(1)}, bf16[272,768]{1,0:T(8,128)(2,1)}, u32[]{:S(2)}, u32[]{:S(2)}) collective-permute-start(bf16[272,768]{1,0:T(8,128)(2,1)S(1)} %get-tuple-element.273), channel_id=1, source_target_pairs={{0,0},{1,1},{2,4},{3,5},{4,2},{5,3},{6,6},{7,7},{8,8},{9,9},{10,12... | collective-permute-start | bytes 1253384 | tf_op jit(solution)/shard_map/ppermute | solution.py:558
  16.5 10.2 %collective-permute-start.3 = (bf16[3,48,1152]{2,1,0:T(8,128)(2,1)S(1)}, bf16[3,48,1152]{2,1,0:T(8,128)(2,1)S(1)}, u32[]{:S(2)}, u32[]{:S(2)}) collective-permute-start(bf16[3,48,1152]{2,1,0:T(8,128)(2,1)S(1)} %pad_maximum_fusion.3.refs_5_.refs_1_), channel_id=1, source_target_pairs={{0,24},{4,28},{8,16},{12,20},{16,8},{20,12},{24,0},{28,4},{1,25},{... | collective-permute-start | bytes 995336 | tf_op jit(solution)/shard_map/ppermute | solution.py:523
  19.5 15.6 %collective-permute-start.12 = (bf16[3,48,1152]{2,1,0:T(8,128)(2,1)S(1)}, bf16[3,48,1152]{2,1,0:T(8,128)(2,1)S(1)}, u32[]{:S(2)}, u32[]{:S(2)}) collective-permute-start(bf16[3,48,1152]{2,1,0:T(8,128)(2,1)S(1)} %pad_maximum_fusion.3.refs_5_.refs_1_), channel_id=1, source_target_pairs={{0,16},{4,20},{8,24},{12,28},{16,0},{20,4},{24,8},{28,12},{1,17},{... | collective-permute-start | bytes 995336 | tf_op jit(solution)/shard_map/ppermute | solution.py:523
  20.1 15.2 %collective-permute-start.10 = (bf16[3,48,1152]{2,1,0:T(8,128)(2,1)S(1)}, bf16[3,48,1152]{2,1,0:T(8,128)(2,1)S(1)}, u32[]{:S(2)}, u32[]{:S(2)}) collective-permute-start(bf16[3,48,1152]{2,1,0:T(8,128)(2,1)S(1)} %pad_maximum_fusion.3.refs_5_.refs_1_), channel_id=1, source_target_pairs={{0,8},{4,12},{8,0},{12,4},{16,24},{20,28},{24,16},{28,20},{1,9},{5... | collective-permute-start | bytes 995336 | tf_op jit(solution)/shard_map/ppermute | solution.py:523
  26.7 9.5 %collective-permute-start.9 = (bf16[3,48,1152]{2,1,0:T(8,128)(2,1)S(1)}, bf16[3,48,1152]{2,1,0:T(8,128)(2,1)S(1)}, u32[]{:S(2)}, u32[]{:S(2)}) collective-permute-start(bf16[3,48,1152]{2,1,0:T(8,128)(2,1)S(1)} %pad_maximum_fusion.3.refs_5_.refs_1_), channel_id=1, source_target_pairs={{0,4},{4,0},{8,12},{12,8},{16,20},{20,16},{24,28},{28,24},{1,5},{5... | collective-permute-start | bytes 995336 | tf_op jit(solution)/shard_map/ppermute | solution.py:510
  36.8 17.1 %collective-permute-start.17 = (bf16[240,384]{1,0:T(8,128)(2,1)S(1)}, bf16[240,384]{1,0:T(8,128)(2,1)S(1)}, u32[]{:S(2)}, u32[]{:S(2)}) collective-permute-start(bf16[240,384]{1,0:T(8,128)(2,1)S(1)} %pad_maximum_fusion.5), channel_id=1, source_target_pairs={{0,3},{1,2},{2,1},{3,0},{4,7},{5,6},{6,5},{7,4},{8,11},{9,10},{10,... | collective-permute-start | bytes 552968 | tf_op jit(solution)/shard_map/ppermute | solution.py:514
  38.2 17.1 %collective-permute-start.16 = (bf16[240,384]{1,0:T(8,128)(2,1)S(1)}, bf16[240,384]{1,0:T(8,128)(2,1)S(1)}, u32[]{:S(2)}, u32[]{:S(2)}) collective-permute-start(bf16[240,384]{1,0:T(8,128)(2,1)S(1)} %pad_maximum_fusion.5), channel_id=1, source_target_pairs={{0,2},{1,3},{2,0},{3,1},{4,6},{5,7},{6,4},{7,5},{8,10},{9,11},{10,... | collective-permute-start | bytes 552968 | tf_op jit(solution)/shard_map/ppermute | solution.py:514
  39.0 16.4 %collective-permute-start.15 = (bf16[240,384]{1,0:T(8,128)(2,1)S(1)}, bf16[240,384]{1,0:T(8,128)(2,1)S(1)}, u32[]{:S(2)}, u32[]{:S(2)}) collective-permute-start(bf16[240,384]{1,0:T(8,128)(2,1)S(1)} %pad_maximum_fusion.5), channel_id=1, source_target_pairs={{0,1},{1,0},{2,3},{3,2},{4,5},{5,4},{6,7},{7,6},{8,9},{9,8},{10,11... | collective-permute-start | bytes 552968 | tf_op jit(solution)/shard_map/ppermute | solution.py:514
  55.4 20.3 %collective-permute-start.20 = (bf16[3,240,384]{2,1,0:T(8,128)(2,1)S(1)}, bf16[3,240,384]{2,1,0:T(8,128)(2,1)S(1)}, u32[]{:S(2)}, u32[]{:S(2)}) collective-permute-start(bf16[3,240,384]{2,1,0:T(8,128)(2,1)S(1)} %pad_maximum_fusion.1.refs_2_.refs_5_), channel_id=1, source_target_pairs={{0,4},{4,0},{8,12},{12,8},{16,20},{20,16},{24,28},{28,24},{1,5},{5... | collective-permute-start | bytes 1658888 | tf_op jit(solution)/shard_map/ppermute | solution.py:510
  55.5 20.3 %collective-permute-start.19 = (bf16[3,240,384]{2,1,0:T(8,128)(2,1)S(1)}, bf16[3,240,384]{2,1,0:T(8,128)(2,1)S(1)}, u32[]{:S(2)}, u32[]{:S(2)}) collective-permute-start(bf16[3,240,384]{2,1,0:T(8,128)(2,1)S(1)} %pad_maximum_fusion.1.refs_2_.refs_5_), channel_id=1, source_target_pairs={{0,16},{4,20},{8,24},{12,28},{16,0},{20,4},{24,8},{28,12},{1,17},{... | collective-permute-start | bytes 1658888 | tf_op jit(solution)/shard_map/ppermute | solution.py:523
  57.1 18.7 %collective-permute-start.18 = (bf16[3,240,384]{2,1,0:T(8,128)(2,1)S(1)}, bf16[3,240,384]{2,1,0:T(8,128)(2,1)S(1)}, u32[]{:S(2)}, u32[]{:S(2)}) collective-permute-start(bf16[3,240,384]{2,1,0:T(8,128)(2,1)S(1)} %pad_maximum_fusion.1.refs_2_.refs_5_), channel_id=1, source_target_pairs={{0,8},{4,12},{8,0},{12,4},{16,24},{20,28},{24,16},{28,20},{1,9},{5... | collective-permute-start | bytes 1658888 | tf_op jit(solution)/shard_map/ppermute | solution.py:523
  58.6 17.2 %collective-permute-start.22 = (bf16[192,384]{1,0:T(8,128)(2,1)S(1)}, bf16[192,384]{1,0:T(8,128)(2,1)S(1)}, u32[]{:S(2)}, u32[]{:S(2)}) collective-permute-start(bf16[192,384]{1,0:T(8,128)(2,1)S(1)} %copy-done.56), channel_id=1, source_target_pairs={{0,2},{1,3},{2,0},{3,1},{4,6},{5,7},{6,4},{7,5},{8,10},{9,11},{10,... | collective-permute-start | bytes 442376 | tf_op jit(solution)/shard_map/ppermute | solution.py:514
  58.6 17.2 %collective-permute-start.21 = (bf16[192,384]{1,0:T(8,128)(2,1)S(1)}, bf16[192,384]{1,0:T(8,128)(2,1)S(1)}, u32[]{:S(2)}, u32[]{:S(2)}) collective-permute-start(bf16[192,384]{1,0:T(8,128)(2,1)S(1)} %copy-done.56), channel_id=1, source_target_pairs={{0,1},{1,0},{2,3},{3,2},{4,5},{5,4},{6,7},{7,6},{8,9},{9,8},{10,11... | collective-permute-start | bytes 442376 | tf_op jit(solution)/shard_map/ppermute | solution.py:514
  75.8 9.7 %collective-permute-start.25 = (bf16[3,240,384]{2,1,0:T(8,128)(2,1)S(1)}, bf16[3,240,384]{2,1,0:T(8,128)(2,1)S(1)}, u32[]{:S(2)}, u32[]{:S(2)}) collective-permute-start(bf16[3,240,384]{2,1,0:T(8,128)(2,1)S(1)} %collective-permute-done.18.refs_4_.refs_7_), channel_id=1, source_target_pairs={{0,4},{4,0},{8,12},{12,8},{16,20},{20,16},{24,28},{28,24},{1,5},{5... | collective-permute-start | bytes 1658888 | tf_op jit(solution)/shard_map/ppermute | solution.py:510
  75.9 9.6 %collective-permute-start.26 = (bf16[3,240,384]{2,1,0:T(8,128)(2,1)S(1)}, bf16[3,240,384]{2,1,0:T(8,128)(2,1)S(1)}, u32[]{:S(2)}, u32[]{:S(2)}) collective-permute-start(bf16[3,240,384]{2,1,0:T(8,128)(2,1)S(1)} %collective-permute-done.19.refs_6_.refs_9_), channel_id=1, source_target_pairs={{0,4},{4,0},{8,12},{12,8},{16,20},{20,16},{24,28},{28,24},{1,5},{5... | collective-permute-start | bytes 1658888 | tf_op jit(solution)/shard_map/ppermute | solution.py:510
  76.5 9.1 %collective-permute-start.23 = (bf16[3,128,384]{2,1,0:T(8,128)(2,1)S(1)}, bf16[3,128,384]{2,1,0:T(8,128)(2,1)S(1)}, u32[]{:S(2)}, u32[]{:S(2)}) collective-permute-start(bf16[3,128,384]{2,1,0:T(8,128)(2,1)S(1)} %slice.41), channel_id=1, source_target_pairs={{0,16},{4,20},{8,24},{12,28},{16,0},{20,4},{24,8},{28,12},{1,17},{... | collective-permute-start | bytes 884744 | tf_op jit(solution)/shard_map/ppermute | solution.py:523
  87.6 24.8 %collective-permute-start.32 = (bf16[3,192,384]{2,1,0:T(8,128)(2,1)S(1)}, bf16[3,192,384]{2,1,0:T(8,128)(2,1)S(1)}, u32[]{:S(2)}, u32[]{:S(2)}) collective-permute-start(bf16[3,192,384]{2,1,0:T(8,128)(2,1)S(1)} %pad_maximum_fusion.2.refs_15_), channel_id=1, source_target_pairs={{0,24},{4,28},{8,16},{12,20},{16,8},{20,12},{24,0},{28,4},{1,25},{... | collective-permute-start | bytes 1327112 | tf_op jit(solution)/shard_map/ppermute | solution.py:523
  89.5 22.9 %collective-permute-start.31 = (bf16[3,192,384]{2,1,0:T(8,128)(2,1)S(1)}, bf16[3,192,384]{2,1,0:T(8,128)(2,1)S(1)}, u32[]{:S(2)}, u32[]{:S(2)}) collective-permute-start(bf16[3,192,384]{2,1,0:T(8,128)(2,1)S(1)} %pad_maximum_fusion.2.refs_15_), channel_id=1, source_target_pairs={{0,16},{4,20},{8,24},{12,28},{16,0},{20,4},{24,8},{28,12},{1,17},{... | collective-permute-start | bytes 1327112 | tf_op jit(solution)/shard_map/ppermute | solution.py:523
  90.0 22.4 %collective-permute-start.30 = (bf16[3,192,384]{2,1,0:T(8,128)(2,1)S(1)}, bf16[3,192,384]{2,1,0:T(8,128)(2,1)S(1)}, u32[]{:S(2)}, u32[]{:S(2)}) collective-permute-start(bf16[3,192,384]{2,1,0:T(8,128)(2,1)S(1)} %pad_maximum_fusion.2.refs_15_), channel_id=1, source_target_pairs={{0,8},{4,12},{8,0},{12,4},{16,24},{20,28},{24,16},{28,20},{1,9},{5... | collective-permute-start | bytes 1327112 | tf_op jit(solution)/shard_map/ppermute | solution.py:523
  91.2 19.1 %collective-permute-start.34 = (bf16[256,768]{1,0:T(8,128)(2,1)S(1)}, bf16[256,768]{1,0:T(8,128)(2,1)S(1)}, u32[]{:S(2)}, u32[]{:S(2)}) collective-permute-start(bf16[256,768]{1,0:T(8,128)(2,1)S(1)} %get-tuple-element.274), channel_id=1, source_target_pairs={{0,1},{1,0},{2,5},{3,4},{4,3},{5,2},{6,7},{7,6},{8,9},{9,8},{10,13... | collective-permute-start | bytes 1179656 | tf_op jit(solution)/shard_map/ppermute | solution.py:558
  91.9 20.4 %collective-permute-start.33 = (bf16[256,768]{1,0:T(8,128)(2,1)S(1)}, bf16[256,768]{1,0:T(8,128)(2,1)S(1)}, u32[]{:S(2)}, u32[]{:S(2)}) collective-permute-start(bf16[256,768]{1,0:T(8,128)(2,1)S(1)} %get-tuple-element.275), channel_id=1, source_target_pairs={{0,0},{1,1},{2,4},{3,5},{4,2},{5,3},{6,6},{7,7},{8,8},{9,9},{10,12... | collective-permute-start | bytes 1179656 | tf_op jit(solution)/shard_map/ppermute | solution.py:558
  145.7 20.3 %collective-permute-start.39 = (bf16[256,768]{1,0:T(8,128)(2,1)}, bf16[256,768]{1,0:T(8,128)(2,1)S(1)}, u32[]{:S(2)}, u32[]{:S(2)}) collective-permute-start(bf16[256,768]{1,0:T(8,128)(2,1)} %get-tuple-element.217), channel_id=1, source_target_pairs={{0,0},{1,1},{2,4},{3,5},{4,2},{5,3},{6,6},{7,7},{8,8},{9,9},{10,12... | collective-permute-start | bytes 1179656 | tf_op jit(solution)/shard_map/ppermute | solution.py:1417
  147.5 18.5 %collective-permute-start.40 = (bf16[256,768]{1,0:T(8,128)(2,1)}, bf16[256,768]{1,0:T(8,128)(2,1)S(1)}, u32[]{:S(2)}, u32[]{:S(2)}) collective-permute-start(bf16[256,768]{1,0:T(8,128)(2,1)} %get-tuple-element.218), channel_id=1, source_target_pairs={{0,1},{1,0},{2,5},{3,4},{4,3},{5,2},{6,7},{7,6},{8,9},{9,8},{10,13... | collective-permute-start | bytes 1179656 | tf_op jit(solution)/shard_map/ppermute | solution.py:1417
  189.4 16.9 %collective-permute-start.47 = (bf16[256,768]{1,0:T(8,128)(2,1)S(1)}, bf16[256,768]{1,0:T(8,128)(2,1)S(1)}, u32[]{:S(2)}, u32[]{:S(2)}) collective-permute-start(bf16[256,768]{1,0:T(8,128)(2,1)S(1)} %get-tuple-element.254), channel_id=1, source_target_pairs={{0,0},{1,1},{2,4},{3,5},{4,2},{5,3},{6,6},{7,7},{8,8},{9,9},{10,12... | collective-permute-start | bytes 1179656 | tf_op jit(solution)/shard_map/ppermute | solution.py:1417
  190.1 16.2 %collective-permute-start.48 = (bf16[256,768]{1,0:T(8,128)(2,1)S(1)}, bf16[256,768]{1,0:T(8,128)(2,1)S(1)}, u32[]{:S(2)}, u32[]{:S(2)}) collective-permute-start(bf16[256,768]{1,0:T(8,128)(2,1)S(1)} %get-tuple-element.255), channel_id=1, source_target_pairs={{0,1},{1,0},{2,5},{3,4},{4,3},{5,2},{6,7},{7,6},{8,9},{9,8},{10,13... | collective-permute-start | bytes 1179656 | tf_op jit(solution)/shard_map/ppermute | solution.py:1417
  193.5 12.8 %collective-permute-start.50 = (bf16[4,40,768]{2,1,0:T(8,128)(2,1)S(1)}, bf16[4,40,768]{2,1,0:T(8,128)(2,1)S(1)}, u32[]{:S(2)}, u32[]{:S(2)}) collective-permute-start(bf16[4,40,768]{2,1,0:T(8,128)(2,1)S(1)} %get-tuple-element.256), channel_id=1, source_target_pairs={{0,16},{4,20},{8,24},{12,28},{16,0},{20,4},{24,8},{28,12},{1,17},{... | collective-permute-start | bytes 737288 | tf_op jit(solution)/shard_map/ppermute | solution.py:523
  194.0 12.3 %collective-permute-start.49 = (bf16[4,40,768]{2,1,0:T(8,128)(2,1)S(1)}, bf16[4,40,768]{2,1,0:T(8,128)(2,1)S(1)}, u32[]{:S(2)}, u32[]{:S(2)}) collective-permute-start(bf16[4,40,768]{2,1,0:T(8,128)(2,1)S(1)} %get-tuple-element.256), channel_id=1, source_target_pairs={{0,8},{4,12},{8,0},{12,4},{16,24},{20,28},{24,16},{28,20},{1,9},{5... | collective-permute-start | bytes 737288 | tf_op jit(solution)/shard_map/ppermute | solution.py:523
  (81 other events, 887.5 us)

commit v2 on v1

--- a/solution.py
+++ b/solution.py
@@ -735,7 +735,7 @@
             jax.ShapeDtypeStruct((512, 128), BF),
             jax.ShapeDtypeStruct((512, width), BF),
         ],
-        compiler_params=pltpu.CompilerParams(vmem_limit_bytes=56 * MEBI),
+        compiler_params=pltpu.CompilerParams(vmem_limit_bytes=48 * MEBI),
         cost_estimate=SMALL_COST,
         name="project_qkv",
     )(meta, ids, *messages, w_own, *pieces, *([table_in] * 3), *([table_out] * 3))
@@ -767,13 +767,17 @@
             o_ref[start : start + size] = jnp.where(low[0:size], mixed[0], mixed[1]).astype(BF)
 
 
-def attend(q, k, v, masks, hot, closed):
+def attend_more_kernel(q_ref, k_ref, v_ref, mask_ref, hot_ref, closed_ref, mixed, shares, o_ref, p_ref):
+    del mixed, shares
+    attend_kernel(q_ref, k_ref, v_ref, mask_ref, hot_ref, closed_ref, o_ref, p_ref)
+
+
+def attend(first, pairs, q, k, v, masks, hot, closed, *before):
     width = q.shape[1]
-    pairs = width // 128
-    half = pl.BlockSpec((512, 128), lambda g: (0, g))
-    full = pl.BlockSpec((1024, 128), lambda g: (0, g))
+    half = pl.BlockSpec((512, 128), lambda g: (0, g + first))
+    full = pl.BlockSpec((1024, 128), lambda g: (0, g + first))
     return pl.pallas_call(
-        attend_kernel,
+        attend_more_kernel if before else attend_kernel,
         grid=(pairs,),
         in_specs=[
             half,
@@ -781,17 +785,19 @@
             full,
             whole((1024, 128)),
             whole((512, 128)),
-            pl.BlockSpec((1, 8, 128), lambda g: (g, 0, 0)),
-        ],
-        out_specs=[half, pl.BlockSpec((2, 512, 1024), lambda g: (g, 0, 0))],
+            pl.BlockSpec((1, 8, 128), lambda g: (g + first, 0, 0)),
+        ]
+        + any_specs(len(before)),
+        out_specs=[half, pl.BlockSpec((2, 512, 1024), lambda g: (g + first, 0, 0))],
         out_shape=[
             jax.ShapeDtypeStruct((512, width), BF),
-            jax.ShapeDtypeStruct((2 * pairs, 512, 1024), BF),
+            jax.ShapeDtypeStruct((width // 64, 512, 1024), BF),
         ],
+        input_output_aliases={6 + n: n for n in range(len(before))},
         compiler_params=pltpu.CompilerParams(vmem_limit_bytes=56 * MEBI),
         cost_estimate=SMALL_COST,
         name="attend",
-    )(q, k, v, masks, hot, closed)
+    )(q, k, v, masks, hot, closed, *before)
 
 
 def attend_back_kernel(q_ref, k_ref, v_ref, p_ref, grad_ref, mixed_ref, dq_ref, dk_own, dv_own, other_ref):
@@ -835,7 +841,7 @@
             jax.ShapeDtypeStruct((512, width), BF),
             jax.ShapeDtypeStruct((2, 512, width), BF),
         ],
-        compiler_params=pltpu.CompilerParams(vmem_limit_bytes=45 * MEBI),
+        compiler_params=pltpu.CompilerParams(vmem_limit_bytes=40 * MEBI),
         cost_estimate=SMALL_COST,
         name="attend_back",
     )(q, k, v, shares, grad, mixed)
@@ -949,7 +955,7 @@
             jax.ShapeDtypeStruct((512, hidden), BF),
             jax.ShapeDtypeStruct((512, hidden), BF),
         ],
-        compiler_params=pltpu.CompilerParams(vmem_limit_bytes=50 * MEBI),
+        compiler_params=pltpu.CompilerParams(vmem_limit_bytes=44 * MEBI),
         cost_estimate=SMALL_COST,
         name="first_half",
     )(meta, ids, out_own, up_own, *up_pieces, x, mixed, gain1, table_in, table_in, table_out, table_out_hidden)
@@ -1371,22 +1377,24 @@
     (q, k, v, masks, hot, x), up_own = lax.optimization_barrier((work(*tokens, *qkv_pieces), up_own))
     up_own = jnp.stack(up_own)
     (mixed, shares), (up_x, up_y, up_there, down_1, down_2) = beside(
-        lambda *given: attend(*given, closed),
+        lambda *given: attend(0, 4, *given, closed),
         lambda block, part: (
             *chips(block, 2, 4), swap(block), swap_shards(part, shard_count, 1), swap_shards(part, shard_count, 2)
         ),
         (q, k, v, masks, hot),
         (up_own, down_piece),
     )
-    mixed, up_a, up_b, up_x_there, up_y_there, down_3 = lax.optimization_barrier(
-        (
-            mixed,
+    (mixed, shares), (up_a, up_b, up_x_there, up_y_there, down_3) = beside(
+        lambda *before: attend(4, H // 2 - 4, q, k, v, masks, hot, closed, *before),
+        lambda up_x, up_y, part: (
             *chips(up_x[:, 0:UP_SPLIT], 4),
             *chips(up_y[:, UP_SPLIT:], 2),
             swap(up_x),
             swap(up_y),
-            swap_shards(after(down_piece, mixed), shard_count, 3),
-        )
+            swap_shards(part, shard_count, 3),
+        ),
+        (mixed, shares),
+        (up_x, up_y, down_piece),
     )
     down_own = jnp.stack([down_1, down_2, down_3])
     up_pieces = (up_own, up_there, up_x, up_x_there, up_y, up_y_there, up_a, up_b, swap(up_a), swap(up_b))

time: 215 us -> 214 us (level)
  starting transfers between devices: 56.2 us -> 51.6 us
  waiting for transfers between devices: 41.4 us -> 44.1 us
    ppermute x13, waiting for transfers between devices: 22.5 us -> 26.2 us  [swap_chips(): return lax.ppermute(block, 'dp', [(i, i ^ offset) for i in range(dp_count)])]
    pallas_call x1 -> x2, Pallas kernels: 14 us -> 16.7 us  [attend(): pl.pallas_call(attend_more_kernel if before else attend_kernel, grid=(pai...]
    unnamed x121 -> x127, local copies, waits for them, and re-layouts: 4.41 us -> 5.09 us
  transfers between devices with their start and end apart: 53 -> 53, of which waited for: 18 -> 18; matrix products, arithmetic and copies ran while one was open for 4% -> 3% of each run, Pallas kernels for 30% -> 31%
where the time goes in v2:
time: 214 us; the launch traced here: 211 us
  Pallas kernels  100 us (47%)
  starting transfers between devices  51.6 us (24%)
  waiting for transfers between devices  44.1 us (21%)
  local copies, waits for them, and re-layouts  9.12 us (4%)
  other arithmetic  3.93 us (2%)
    pallas_call x1, Pallas kernels, second_half(): pl.pallas_call(second_half_kernel, grid_spec=pltpu.PrefetchScalarGridSpec...  29 us
    ppermute x13, waiting for transfers between devices, swap_chips(): return lax.ppermute(block, 'dp', [(i, i ^ offset) for i in range(dp_count)])  26.2 us
    ppermute x12, starting transfers between devices, swap_shards(): lax.ppermute(value, 'shard', [(i, i ^ step) for i in range(shard_count)])  17.2 us
    pallas_call x2, Pallas kernels, attend(): pl.pallas_call(attend_more_kernel if before else attend_kernel, grid=(pai...  16.7 us
    ppermute x13, starting transfers between devices, swap_chips(): return lax.ppermute(block, 'dp', [(i, i ^ offset) for i in range(dp_count)])  15.8 us
    pallas_call x1, Pallas kernels, first_half(): pl.pallas_call(first_half_kernel, grid_spec=pltpu.PrefetchScalarGridSpec(...  15.5 us
    pallas_call x1, Pallas kernels, attend_back(): pl.pallas_call(attend_back_kernel, grid=(width // 128,), in_specs=[half,...  15.4 us
    ppermute x20, starting transfers between devices, swap_cores(): return lax.ppermute(value, 'dp', [(i, i ^ 1) for i in range(dp_count)])  11.3 us
  transfers between devices with their start and end apart: 53, of which 18 were waited for; matrix products, arithmetic and copies ran while one was open for 3% of the time, Pallas kernels for 31%

profile of v2, /device:TPU:0, one launch (start us, length us, event | category | flops | bytes accessed | tf_op | source)
XLA Modules:
  0.0 210.9 jit_solution(9079173260708334524)
XLA Ops:
  1.6 5.1 %collective-permute-start.2 = (bf16[48,1152]{1,0:T(8,128)(2,1)S(1)}, bf16[48,1152]{1,0:T(8,128)(2,1)S(1)}, u32[]{:S(2)}, u32[]{:S(2)}) collective-permute-start(bf16[48,1152]{1,0:T(8,128)(2,1)S(1)} %dynamic_slice.33), channel_id=1, source_target_pairs={{0,3},{1,2},{2,1},{3,0},{4,7},{5,6},{6,5},{7,4},{8,11},{9,10},{10,... | collective-permute-start | bytes 331784 | tf_op jit(solution)/shard_map/ppermute | solution.py:514
  14.6 2.6 %collective-permute-done.1 = bf16[48,1152]{1,0:T(8,128)(2,1)S(1)} collective-permute-done((bf16[48,1152]{1,0:T(8,128)(2,1)S(1)}, bf16[48,1152]{1,0:T(8,128)(2,1)S(1)}, u32[]{:S(2)}, u32[]{:S(2)}) %collective-permute-start.1) | collective-permute-done | bytes 110624 | tf_op jit(solution)/shard_map/ppermute | solution.py:514
  17.3 2.4 %collective-permute-start.3 = (bf16[3,48,1152]{2,1,0:T(8,128)(2,1)S(1)}, bf16[3,48,1152]{2,1,0:T(8,128)(2,1)S(1)}, u32[]{:S(2)}, u32[]{:S(2)}) collective-permute-start(bf16[3,48,1152]{2,1,0:T(8,128)(2,1)S(1)} %pad_maximum_fusion.3.refs_5_.refs_1_), channel_id=1, source_target_pairs={{0,24},{4,28},{8,16},{12,20},{16,8},{20,12},{24,0},{28,4},{1,25},{... | collective-permute-start | bytes 995336 | tf_op jit(solution)/shard_map/ppermute | solution.py:523
  21.6 7.4 %collective-permute-done.3.refs_11_.refs_7_ = bf16[3,48,1152]{2,1,0:T(8,128)(2,1)S(1)} collective-permute-done((bf16[3,48,1152]{2,1,0:T(8,128)(2,1)S(1)}, bf16[3,48,1152]{2,1,0:T(8,128)(2,1)S(1)}, u32[]{:S(2)}, u32[]{:S(2)}) %collective-permute-start.3) | collective-permute-done | bytes 331808 | tf_op jit(solution)/shard_map/ppermute | solution.py:523
  29.7 6.4 %collective-permute-done.12.refs_9_.refs_5_ = bf16[3,48,1152]{2,1,0:T(8,128)(2,1)S(1)} collective-permute-done((bf16[3,48,1152]{2,1,0:T(8,128)(2,1)S(1)}, bf16[3,48,1152]{2,1,0:T(8,128)(2,1)S(1)}, u32[]{:S(2)}, u32[]{:S(2)}) %collective-permute-start.12) | collective-permute-done | bytes 331808 | tf_op jit(solution)/shard_map/ppermute | solution.py:523
  38.2 1.7 collective-permute-start.16
  39.9 2.3 %collective-permute-start.15 = (bf16[240,384]{1,0:T(8,128)(2,1)S(1)}, bf16[240,384]{1,0:T(8,128)(2,1)S(1)}, u32[]{:S(2)}, u32[]{:S(2)}) collective-permute-start(bf16[240,384]{1,0:T(8,128)(2,1)S(1)} %pad_maximum_fusion.5), channel_id=1, source_target_pairs={{0,1},{1,0},{2,3},{3,2},{4,5},{5,4},{6,7},{7,6},{8,9},{9,8},{10,11... | collective-permute-start | bytes 552968 | tf_op jit(solution)/shard_map/ppermute | solution.py:514
  42.1 10.6 %project_qkv.1 = (bf16[512,768]{1,0:T(8,128)(2,1)S(1)}, bf16[1024,768]{1,0:T(8,128)(2,1)}, bf16[1024,768]{1,0:T(8,128)(2,1)}, bf16[1024,128]{1,0:T(8,128)(2,1)S(...) custom-call(s32[2]{0:T(128)S(1)} %pad_add_fusion.meta, s32[6]{0:T(128)S(1)} %fusion.5.ids, ...), custom_call_target="tpu_custom_call" | custom-call | flops 1000000 | bytes 100000 | tf_op jit(solution)/shard_map/project_qkv/pallas_call | solution.py:705
  53.7 2.6 %collective-permute-done.16 = bf16[240,384]{1,0:T(8,128)(2,1)S(1)} collective-permute-done((bf16[240,384]{1,0:T(8,128)(2,1)S(1)}, bf16[240,384]{1,0:T(8,128)(2,1)S(1)}, u32[]{:S(2)}, u32[]{:S(2)}) %collective-permute-start.16) | collective-permute-done | bytes 184352 | tf_op jit(solution)/shard_map/ppermute | solution.py:514
  56.5 1.6 collective-permute-start.19
  58.1 1.5 collective-permute-start.18
  59.6 1.7 collective-permute-start.21
  61.4 10.2 %attend.2 = (bf16[512,768]{1,0:T(8,128)(2,1)}, bf16[12,512,1024]{2,1,0:T(8,128)(2,1)}) custom-call(bf16[512,768]{1,0:T(8,128)(2,1)} %copy-done.8, bf16[1024,768]{1,0:T(8,128)(2,1)} %get-tuple-element.166.k_ref, bf16[1024,768]{1,0:T(8,128)(2,1)} %get-tuple-element.167.v_ref, bf16[1024,128]{1,0:T(8,128)(2,1)} %copy-done.37, bf16[512,128]{1,0:T(8,128)(2,1)} %copy-done.41, ...), custom_call_target="tpu_custom_call" | custom-call | flops 1000000 | bytes 100000 | tf_op jit(solution)/shard_map/attend/pallas_call | solution.py:779
  73.9 1.6 collective-permute-start.24
  76.6 6.4 %attend.3 = (bf16[512,768]{1,0:T(8,128)(2,1)}, bf16[12,512,1024]{2,1,0:T(8,128)(2,1)}) custom-call(bf16[512,768]{1,0:T(8,128)(2,1)} %copy-done.8, bf16[1024,768]{1,0:T(8,128)(2,1)} %get-tuple-element.166.k_ref, bf16[1024,768]{1,0:T(8,128)(2,1)} %get-tuple-element.167.v_ref, ...), custom_call_target="tpu_custom_call", output_to_operand_aliasing={{0}: (6, {}), {1}: (7, {})} | custom-call | flops 1000000 | bytes 100000 | tf_op jit(solution)/shard_map/attend/pallas_call | solution.py:779
  85.2 2.0 collective-permute-start.32
  91.0 15.5 %first_half.1 = (f32[512,768]{1,0:T(8,128)}, f32[512,128]{1,0:T(8,128)S(1)}, bf16[512,3072]{1,0:T(8,128)(2,1)}, bf16[512,3072]{1,0:T(8,128)(2,1)}) custom-call(s32[2]{0:T(128)S(1)} %pad_add_fusion.meta, s32[6]{0:T(128)S(1)} %fusion.5.ids, bf16[192,768]{1,0:T(8,128)(2,1)S(1)} %copy-done.20, bf16[192,3072]{1,0:T(8,128)(2,1)} %refs_3_.1, ...), custom_call_target="tpu_custom_call" | custom-call | flops 1000000 | bytes 100000 | tf_op jit(solution)/shard_map/first_half/pallas_call | solution.py:929
  107.4 4.0 %collective-permute-start.35 = (bf16[3,192,384]{2,1,0:T(8,128)(2,1)S(1)}, bf16[3,192,384]{2,1,0:T(8,128)(2,1)S(1)}, u32[]{:S(2)}, u32[]{:S(2)}) collective-permute-start(bf16[3,192,384]{2,1,0:T(8,128)(2,1)S(1)} %pad_maximum_fusion.2.refs_15_), channel_id=1, source_target_pairs={{0,4},{4,0},{8,12},{12,8},{16,20},{20,16},{24,28},{28,24},{1,5},{5... | collective-permute-start | bytes 1327112 | tf_op jit(solution)/shard_map/ppermute | solution.py:510
  115.6 29.0 %second_half.1 = (bf16[256,768]{1,0:T(8,128)(2,1)}, bf16[256,768]{1,0:T(8,128)(2,1)}, f32[512,768]{1,0:T(8,128)}, bf16[512,768]{1,0:T(8,128)(2,1)}, f32[4,24,768]{2,1,0:T(8,128)}, /*index=5*/bf16[4,24,768]{2,1,0:T(8,128)(2,1)}) custom-call(s32[2]{0:T(128)} %copy-done.44, s32[6]{0:T(128)} %copy-done.46, bf16[256,768]{1,0:T(8,128)(2,1)} %copy-done.59, ...), custom_call_target="tpu_custom_call" | custom-call | flops 1000000 | bytes 100000 | tf_op jit(solution)/shard_map/second_half/pallas_call | solution.py:1067
  144.7 1.8 collective-permute-start.39
  148.2 15.4 %attend_back.1 = (bf16[512,768]{1,0:T(8,128)(2,1)S(1)}, bf16[512,768]{1,0:T(8,128)(2,1)S(1)}, bf16[512,768]{1,0:T(8,128)(2,1)S(1)}, bf16[2,512,768]{2,1,0:T(8,128)(2,1)S(1)}) custom-call(bf16[512,768]{1,0:T(8,128)(2,1)S(1)} %copy-done.9, bf16[1024,768]{1,0:T(8,128)(2,1)S(1)} %copy-done.4, bf16[1024,768]{1,0:T(8,128)(2,1)S(1)} %copy-done.5, ...), custom_call_target="tpu_custom_call" | custom-call | flops 1000000 | bytes 100000 | tf_op jit(solution)/shard_map/attend_back/pallas_call | solution.py:833
  163.8 2.8 %collective-permute-start.41 = (bf16[2,512,768]{2,1,0:T(8,128)(2,1)S(1)}, bf16[2,512,768]{2,1,0:T(8,128)(2,1)S(1)}, u32[]{:S(2)}, u32[]{:S(2)}) collective-permute-start(bf16[2,512,768]{2,1,0:T(8,128)(2,1)S(1)} %get-tuple-element.240), channel_id=1, source_target_pairs={{0,4},{4,0},{8,12},{12,8},{16,20},{20,16},{24,28},{28,24},{1,5},{5... | collective-permute-start | bytes 4718600 | tf_op jit(solution)/shard_map/ppermute | solution.py:510
  166.6 3.0 %collective-permute-done.41.refs_4_ = bf16[2,512,768]{2,1,0:T(8,128)(2,1)S(1)} collective-permute-done((bf16[2,512,768]{2,1,0:T(8,128)(2,1)S(1)}, bf16[2,512,768]{2,1,0:T(8,128)(2,1)S(1)}, u32[]{:S(2)}, u32[]{:S(2)}) %collective-permute-start.41) | collective-permute-done | bytes 1572896 | tf_op jit(solution)/shard_map/ppermute | solution.py:510
  169.7 2.6 %first_grads.1 = (bf16[512,2304]{1,0:T(8,128)(2,1)S(1)}, bf16[512,48]{1,0:T(8,128)(2,1)S(1)}, f32[4,16,768]{2,1,0:T(8,128)S(1)}, bf16[4,16,768]{2,1,0:T(8,128)(2,1)S(1)}) custom-call(s32[2]{0:T(128)S(1)} %copy-done.45, s32[6]{0:T(128)S(1)} %copy-done.47, bf16[512,768]{1,0:T(8,128)(2,1)S(1)} %copy-done.15, bf16[512,768]{1,0:T(8,128)(2,1)S(1)} %get-tuple-element.237.refs_1_, ...), custom_call_target="tpu_custom_call" | custom-call | flops 1000000 | bytes 100000 | tf_op jit(solution)/shard_map/first_grads/pallas_call | solution.py:1158
  173.0 4.1 %project_back.1 = (bf16[256,768]{1,0:T(8,128)(2,1)S(1)}, bf16[256,768]{1,0:T(8,128)(2,1)S(1)}) custom-call(s32[2]{0:T(128)S(1)} %copy-done.45, s32[6]{0:T(128)S(1)} %copy-done.47, bf16[192,2304]{1,0:T(8,128)(2,1)S(1)} %copy-done.11, bf16[3,48,1152]{2,1,0:T(8,128)(2,1)S(1)} %pad_maximum_fusion.3.refs_5_.refs_1_, bf16[3,48,1152]{2,1,0:T(8,128)(2,1)S(1)} %copy-done.28, ...), custom_call_target="tpu_custom_call" | custom-call | flops 1000000 | bytes 100000 | tf_op jit(solution)/shard_map/project_back/pallas_call | solution.py:1201
  177.7 2.2 %collective-permute-start.44 = (bf16[40,768]{1,0:T(8,128)(2,1)S(1)}, bf16[40,768]{1,0:T(8,128)(2,1)S(1)}, u32[]{:S(2)}, u32[]{:S(2)}) collective-permute-start(bf16[40,768]{1,0:T(8,128)(2,1)S(1)} %get-tuple-element.258), channel_id=1, source_target_pairs={{0,1},{1,0},{2,3},{3,2},{4,5},{5,4},{6,7},{7,6},{8,9},{9,8},{10,11... | collective-permute-start | bytes 184328 | tf_op jit(solution)/shard_map/ppermute | solution.py:514
  179.9 2.2 %collective-permute-start.45 = (bf16[40,768]{1,0:T(8,128)(2,1)S(1)}, bf16[40,768]{1,0:T(8,128)(2,1)S(1)}, u32[]{:S(2)}, u32[]{:S(2)}) collective-permute-start(bf16[40,768]{1,0:T(8,128)(2,1)S(1)} %get-tuple-element.259), channel_id=1, source_target_pairs={{0,2},{1,3},{2,0},{3,1},{4,6},{5,7},{6,4},{7,5},{8,10},{9,11},{10,... | collective-permute-start | bytes 184328 | tf_op jit(solution)/shard_map/ppermute | solution.py:514
  183.8 3.3 %collective-permute-done.45 = bf16[40,768]{1,0:T(8,128)(2,1)S(1)} collective-permute-done((bf16[40,768]{1,0:T(8,128)(2,1)S(1)}, bf16[40,768]{1,0:T(8,128)(2,1)S(1)}, u32[]{:S(2)}, u32[]{:S(2)}) %collective-permute-start.45) | collective-permute-done | bytes 61472 | tf_op jit(solution)/shard_map/ppermute | solution.py:514
  193.5 4.3 %collective-permute-done.51 = bf16[4,40,768]{2,1,0:T(8,128)(2,1)S(1)} collective-permute-done((bf16[4,40,768]{2,1,0:T(8,128)(2,1)S(1)}, bf16[4,40,768]{2,1,0:T(8,128)(2,1)S(1)}, u32[]{:S(2)}, u32[]{:S(2)}) %collective-permute-start.51) | collective-permute-done | bytes 245792 | tf_op jit(solution)/shard_map/ppermute | solution.py:523
  197.8 7.1 %collective-permute-done.50 = bf16[4,40,768]{2,1,0:T(8,128)(2,1)S(1)} collective-permute-done((bf16[4,40,768]{2,1,0:T(8,128)(2,1)S(1)}, bf16[4,40,768]{2,1,0:T(8,128)(2,1)S(1)}, u32[]{:S(2)}, u32[]{:S(2)}) %collective-permute-start.50) | collective-permute-done | bytes 245792 | tf_op jit(solution)/shard_map/ppermute | solution.py:523
  206.1 1.8 join_parts.3
  208.1 2.7 %combine.1 = (f32[5,8,16,192]{3,2,1,0:T(8,128)}, f32[8,16,768]{2,1,0:T(8,128)}, f32[5,8,16,192]{3,2,1,0:T(8,128)}, f32[8,16,768]{2,1,0:T(8,128)}) custom-call(s32[96]{0:T(128)S(1)} %reshape.102.ids, s32[2]{0:T(128)S(1)} %copy-done.45, bf16[4,4,40,768]{3,2,1,0:T(8,128)(2,1)S(1)} %pad_maximum_fusion.own, bf16[4,4,40,768]{3,2,1,0:T(8,128)(2,1)S(1)} %collective-permute-done.52.other), custom_call_target="tpu_custom_call" | custom-call | flops 1000000 | bytes 100000 | tf_op jit(solution)/shard_map/combine/pallas_call | solution.py:1272
  (246 shorter events, 41.1 us)
Async XLA Ops:
  1.6 12.4 %collective-permute-start.2 = (bf16[48,1152]{1,0:T(8,128)(2,1)S(1)}, bf16[48,1152]{1,0:T(8,128)(2,1)S(1)}, u32[]{:S(2)}, u32[]{:S(2)}) collective-permute-start(bf16[48,1152]{1,0:T(8,128)(2,1)S(1)} %dynamic_slice.33), channel_id=1, source_target_pairs={{0,3},{1,2},{2,1},{3,0},{4,7},{5,6},{6,5},{7,4},{8,11},{9,10},{10,... | collective-permute-start | bytes 331784 | tf_op jit(solution)/shard_map/ppermute | solution.py:514
  6.7 10.6 %collective-permute-start.1 = (bf16[48,1152]{1,0:T(8,128)(2,1)S(1)}, bf16[48,1152]{1,0:T(8,128)(2,1)S(1)}, u32[]{:S(2)}, u32[]{:S(2)}) collective-permute-start(bf16[48,1152]{1,0:T(8,128)(2,1)S(1)} %dynamic_slice.33), channel_id=1, source_target_pairs={{0,2},{1,3},{2,0},{3,1},{4,6},{5,7},{6,4},{7,5},{8,10},{9,11},{10,... | collective-permute-start | bytes 331784 | tf_op jit(solution)/shard_map/ppermute | solution.py:514
  6.7 10.6 %collective-permute-start = (bf16[48,1152]{1,0:T(8,128)(2,1)S(1)}, bf16[48,1152]{1,0:T(8,128)(2,1)S(1)}, u32[]{:S(2)}, u32[]{:S(2)}) collective-permute-start(bf16[48,1152]{1,0:T(8,128)(2,1)S(1)} %dynamic_slice.33), channel_id=1, source_target_pairs={{0,1},{1,0},{2,3},{3,2},{4,5},{5,4},{6,7},{7,6},{8,9},{9,8},{10,11... | collective-permute-start | bytes 331784 | tf_op jit(solution)/shard_map/ppermute | solution.py:514
  7.3 13.7 %collective-permute-start.4 = (s32[2,6]{1,0:T(2,128)}, s32[2,6]{1,0:T(2,128)S(1)}, u32[]{:S(2)}, u32[]{:S(2)}) collective-permute-start(s32[2,6]{1,0:T(2,128)} %param.18), channel_id=1, source_target_pairs={{0,4},{4,0},{8,12},{12,8},{16,20},{20,16},{24,28},{28,24},{1,5},{5... | collective-permute-start | bytes 152 | tf_op jit(solution)/shard_map/ppermute | solution.py:510
  9.3 27.3 %collective-permute-start.6 = (bf16[272,768]{1,0:T(8,128)(2,1)S(1)}, bf16[272,768]{1,0:T(8,128)(2,1)S(1)}, u32[]{:S(2)}, u32[]{:S(2)}) collective-permute-start(bf16[272,768]{1,0:T(8,128)(2,1)S(1)} %get-tuple-element.286), channel_id=1, source_target_pairs={{0,1},{1,0},{2,5},{3,4},{4,3},{5,2},{6,7},{7,6},{8,9},{9,8},{10,13... | collective-permute-start | bytes 1253384 | tf_op jit(solution)/shard_map/ppermute | solution.py:558
  14.0 22.8 %collective-permute-start.5 = (bf16[272,768]{1,0:T(8,128)(2,1)S(1)}, bf16[272,768]{1,0:T(8,128)(2,1)S(1)}, u32[]{:S(2)}, u32[]{:S(2)}) collective-permute-start(bf16[272,768]{1,0:T(8,128)(2,1)S(1)} %get-tuple-element.287), channel_id=1, source_target_pairs={{0,0},{1,1},{2,4},{3,5},{4,2},{5,3},{6,6},{7,7},{8,8},{9,9},{10,12... | collective-permute-start | bytes 1253384 | tf_op jit(solution)/shard_map/ppermute | solution.py:558
  17.3 11.6 %collective-permute-start.3 = (bf16[3,48,1152]{2,1,0:T(8,128)(2,1)S(1)}, bf16[3,48,1152]{2,1,0:T(8,128)(2,1)S(1)}, u32[]{:S(2)}, u32[]{:S(2)}) collective-permute-start(bf16[3,48,1152]{2,1,0:T(8,128)(2,1)S(1)} %pad_maximum_fusion.3.refs_5_.refs_1_), channel_id=1, source_target_pairs={{0,24},{4,28},{8,16},{12,20},{16,8},{20,12},{24,0},{28,4},{1,25},{... | collective-permute-start | bytes 995336 | tf_op jit(solution)/shard_map/ppermute | solution.py:523
  20.5 15.6 %collective-permute-start.12 = (bf16[3,48,1152]{2,1,0:T(8,128)(2,1)S(1)}, bf16[3,48,1152]{2,1,0:T(8,128)(2,1)S(1)}, u32[]{:S(2)}, u32[]{:S(2)}) collective-permute-start(bf16[3,48,1152]{2,1,0:T(8,128)(2,1)S(1)} %pad_maximum_fusion.3.refs_5_.refs_1_), channel_id=1, source_target_pairs={{0,16},{4,20},{8,24},{12,28},{16,0},{20,4},{24,8},{28,12},{1,17},{... | collective-permute-start | bytes 995336 | tf_op jit(solution)/shard_map/ppermute | solution.py:523
  21.0 15.2 %collective-permute-start.10 = (bf16[3,48,1152]{2,1,0:T(8,128)(2,1)S(1)}, bf16[3,48,1152]{2,1,0:T(8,128)(2,1)S(1)}, u32[]{:S(2)}, u32[]{:S(2)}) collective-permute-start(bf16[3,48,1152]{2,1,0:T(8,128)(2,1)S(1)} %pad_maximum_fusion.3.refs_5_.refs_1_), channel_id=1, source_target_pairs={{0,8},{4,12},{8,0},{12,4},{16,24},{20,28},{24,16},{28,20},{1,9},{5... | collective-permute-start | bytes 995336 | tf_op jit(solution)/shard_map/ppermute | solution.py:523
  37.7 16.0 %collective-permute-start.17 = (bf16[240,384]{1,0:T(8,128)(2,1)S(1)}, bf16[240,384]{1,0:T(8,128)(2,1)S(1)}, u32[]{:S(2)}, u32[]{:S(2)}) collective-permute-start(bf16[240,384]{1,0:T(8,128)(2,1)S(1)} %pad_maximum_fusion.5), channel_id=1, source_target_pairs={{0,3},{1,2},{2,1},{3,0},{4,7},{5,6},{6,5},{7,4},{8,11},{9,10},{10,... | collective-permute-start | bytes 552968 | tf_op jit(solution)/shard_map/ppermute | solution.py:514
  38.2 18.2 %collective-permute-start.16 = (bf16[240,384]{1,0:T(8,128)(2,1)S(1)}, bf16[240,384]{1,0:T(8,128)(2,1)S(1)}, u32[]{:S(2)}, u32[]{:S(2)}) collective-permute-start(bf16[240,384]{1,0:T(8,128)(2,1)S(1)} %pad_maximum_fusion.5), channel_id=1, source_target_pairs={{0,2},{1,3},{2,0},{3,1},{4,6},{5,7},{6,4},{7,5},{8,10},{9,11},{10,... | collective-permute-start | bytes 552968 | tf_op jit(solution)/shard_map/ppermute | solution.py:514
  39.9 16.5 %collective-permute-start.15 = (bf16[240,384]{1,0:T(8,128)(2,1)S(1)}, bf16[240,384]{1,0:T(8,128)(2,1)S(1)}, u32[]{:S(2)}, u32[]{:S(2)}) collective-permute-start(bf16[240,384]{1,0:T(8,128)(2,1)S(1)} %pad_maximum_fusion.5), channel_id=1, source_target_pairs={{0,1},{1,0},{2,3},{3,2},{4,5},{5,4},{6,7},{7,6},{8,9},{9,8},{10,11... | collective-permute-start | bytes 552968 | tf_op jit(solution)/shard_map/ppermute | solution.py:514
  56.5 15.2 %collective-permute-start.20 = (bf16[3,240,384]{2,1,0:T(8,128)(2,1)S(1)}, bf16[3,240,384]{2,1,0:T(8,128)(2,1)S(1)}, u32[]{:S(2)}, u32[]{:S(2)}) collective-permute-start(bf16[3,240,384]{2,1,0:T(8,128)(2,1)S(1)} %pad_maximum_fusion.1.refs_2_.refs_5_), channel_id=1, source_target_pairs={{0,4},{4,0},{8,12},{12,8},{16,20},{20,16},{24,28},{28,24},{1,5},{5... | collective-permute-start | bytes 1658888 | tf_op jit(solution)/shard_map/ppermute | solution.py:510
  56.5 15.1 %collective-permute-start.19 = (bf16[3,240,384]{2,1,0:T(8,128)(2,1)S(1)}, bf16[3,240,384]{2,1,0:T(8,128)(2,1)S(1)}, u32[]{:S(2)}, u32[]{:S(2)}) collective-permute-start(bf16[3,240,384]{2,1,0:T(8,128)(2,1)S(1)} %pad_maximum_fusion.1.refs_2_.refs_5_), channel_id=1, source_target_pairs={{0,16},{4,20},{8,24},{12,28},{16,0},{20,4},{24,8},{28,12},{1,17},{... | collective-permute-start | bytes 1658888 | tf_op jit(solution)/shard_map/ppermute | solution.py:523
  58.1 14.6 %collective-permute-start.18 = (bf16[3,240,384]{2,1,0:T(8,128)(2,1)S(1)}, bf16[3,240,384]{2,1,0:T(8,128)(2,1)S(1)}, u32[]{:S(2)}, u32[]{:S(2)}) collective-permute-start(bf16[3,240,384]{2,1,0:T(8,128)(2,1)S(1)} %pad_maximum_fusion.1.refs_2_.refs_5_), channel_id=1, source_target_pairs={{0,8},{4,12},{8,0},{12,4},{16,24},{20,28},{24,16},{28,20},{1,9},{5... | collective-permute-start | bytes 1658888 | tf_op jit(solution)/shard_map/ppermute | solution.py:523
  59.6 12.0 %collective-permute-start.22 = (bf16[192,384]{1,0:T(8,128)(2,1)}, bf16[192,384]{1,0:T(8,128)(2,1)S(1)}, u32[]{:S(2)}, u32[]{:S(2)}) collective-permute-start(bf16[192,384]{1,0:T(8,128)(2,1)} %pad_maximum_fusion.6), channel_id=1, source_target_pairs={{0,2},{1,3},{2,0},{3,1},{4,6},{5,7},{6,4},{7,5},{8,10},{9,11},{10,... | collective-permute-start | bytes 442376 | tf_op jit(solution)/shard_map/ppermute | solution.py:514
  59.6 12.0 %collective-permute-start.21 = (bf16[192,384]{1,0:T(8,128)(2,1)}, bf16[192,384]{1,0:T(8,128)(2,1)S(1)}, u32[]{:S(2)}, u32[]{:S(2)}) collective-permute-start(bf16[192,384]{1,0:T(8,128)(2,1)} %pad_maximum_fusion.6), channel_id=1, source_target_pairs={{0,1},{1,0},{2,3},{3,2},{4,5},{5,4},{6,7},{7,6},{8,9},{9,8},{10,11... | collective-permute-start | bytes 442376 | tf_op jit(solution)/shard_map/ppermute | solution.py:514
  72.7 10.4 %collective-permute-start.25 = (bf16[3,240,384]{2,1,0:T(8,128)(2,1)S(1)}, bf16[3,240,384]{2,1,0:T(8,128)(2,1)S(1)}, u32[]{:S(2)}, u32[]{:S(2)}) collective-permute-start(bf16[3,240,384]{2,1,0:T(8,128)(2,1)S(1)} %collective-permute-done.18.refs_4_.refs_7_), channel_id=1, source_target_pairs={{0,4},{4,0},{8,12},{12,8},{16,20},{20,16},{24,28},{28,24},{1,5},{5... | collective-permute-start | bytes 1658888 | tf_op jit(solution)/shard_map/ppermute | solution.py:510
  72.7 10.4 %collective-permute-start.26 = (bf16[3,240,384]{2,1,0:T(8,128)(2,1)S(1)}, bf16[3,240,384]{2,1,0:T(8,128)(2,1)S(1)}, u32[]{:S(2)}, u32[]{:S(2)}) collective-permute-start(bf16[3,240,384]{2,1,0:T(8,128)(2,1)S(1)} %collective-permute-done.19.refs_6_.refs_9_), channel_id=1, source_target_pairs={{0,4},{4,0},{8,12},{12,8},{16,20},{20,16},{24,28},{28,24},{1,5},{5... | collective-permute-start | bytes 1658888 | tf_op jit(solution)/shard_map/ppermute | solution.py:510
  73.3 9.9 %collective-permute-start.23 = (bf16[3,128,384]{2,1,0:T(8,128)(2,1)S(1)}, bf16[3,128,384]{2,1,0:T(8,128)(2,1)S(1)}, u32[]{:S(2)}, u32[]{:S(2)}) collective-permute-start(bf16[3,128,384]{2,1,0:T(8,128)(2,1)S(1)} %slice.41), channel_id=1, source_target_pairs={{0,16},{4,20},{8,24},{12,28},{16,0},{20,4},{24,8},{28,12},{1,17},{... | collective-permute-start | bytes 884744 | tf_op jit(solution)/shard_map/ppermute | solution.py:523
  73.9 9.2 %collective-permute-start.24 = (bf16[3,112,384]{2,1,0:T(8,128)(2,1)S(1)}, bf16[3,112,384]{2,1,0:T(8,128)(2,1)S(1)}, u32[]{:S(2)}, u32[]{:S(2)}) collective-permute-start(bf16[3,112,384]{2,1,0:T(8,128)(2,1)S(1)} %slice.42), channel_id=1, source_target_pairs={{0,8},{4,12},{8,0},{12,4},{16,24},{20,28},{24,16},{28,20},{1,9},{5... | collective-permute-start | bytes 774152 | tf_op jit(solution)/shard_map/ppermute | solution.py:523
  85.2 26.2 %collective-permute-start.32 = (bf16[3,192,384]{2,1,0:T(8,128)(2,1)S(1)}, bf16[3,192,384]{2,1,0:T(8,128)(2,1)S(1)}, u32[]{:S(2)}, u32[]{:S(2)}) collective-permute-start(bf16[3,192,384]{2,1,0:T(8,128)(2,1)S(1)} %pad_maximum_fusion.2.refs_15_), channel_id=1, source_target_pairs={{0,24},{4,28},{8,16},{12,20},{16,8},{20,12},{24,0},{28,4},{1,25},{... | collective-permute-start | bytes 1327112 | tf_op jit(solution)/shard_map/ppermute | solution.py:523
  87.3 24.2 %collective-permute-start.31 = (bf16[3,192,384]{2,1,0:T(8,128)(2,1)S(1)}, bf16[3,192,384]{2,1,0:T(8,128)(2,1)S(1)}, u32[]{:S(2)}, u32[]{:S(2)}) collective-permute-start(bf16[3,192,384]{2,1,0:T(8,128)(2,1)S(1)} %pad_maximum_fusion.2.refs_15_), channel_id=1, source_target_pairs={{0,16},{4,20},{8,24},{12,28},{16,0},{20,4},{24,8},{28,12},{1,17},{... | collective-permute-start | bytes 1327112 | tf_op jit(solution)/shard_map/ppermute | solution.py:523
  87.8 23.7 %collective-permute-start.30 = (bf16[3,192,384]{2,1,0:T(8,128)(2,1)S(1)}, bf16[3,192,384]{2,1,0:T(8,128)(2,1)S(1)}, u32[]{:S(2)}, u32[]{:S(2)}) collective-permute-start(bf16[3,192,384]{2,1,0:T(8,128)(2,1)S(1)} %pad_maximum_fusion.2.refs_15_), channel_id=1, source_target_pairs={{0,8},{4,12},{8,0},{12,4},{16,24},{20,28},{24,16},{28,20},{1,9},{5... | collective-permute-start | bytes 1327112 | tf_op jit(solution)/shard_map/ppermute | solution.py:523
  88.8 18.5 %collective-permute-start.34 = (bf16[256,768]{1,0:T(8,128)(2,1)S(1)}, bf16[256,768]{1,0:T(8,128)(2,1)S(1)}, u32[]{:S(2)}, u32[]{:S(2)}) collective-permute-start(bf16[256,768]{1,0:T(8,128)(2,1)S(1)} %get-tuple-element.288), channel_id=1, source_target_pairs={{0,1},{1,0},{2,5},{3,4},{4,3},{5,2},{6,7},{7,6},{8,9},{9,8},{10,13... | collective-permute-start | bytes 1179656 | tf_op jit(solution)/shard_map/ppermute | solution.py:558
  88.9 22.5 %collective-permute-start.33 = (bf16[256,768]{1,0:T(8,128)(2,1)S(1)}, bf16[256,768]{1,0:T(8,128)(2,1)S(1)}, u32[]{:S(2)}, u32[]{:S(2)}) collective-permute-start(bf16[256,768]{1,0:T(8,128)(2,1)S(1)} %get-tuple-element.289), channel_id=1, source_target_pairs={{0,0},{1,1},{2,4},{3,5},{4,2},{5,3},{6,6},{7,7},{8,8},{9,9},{10,12... | collective-permute-start | bytes 1179656 | tf_op jit(solution)/shard_map/ppermute | solution.py:558
  144.7 19.0 %collective-permute-start.39 = (bf16[256,768]{1,0:T(8,128)(2,1)}, bf16[256,768]{1,0:T(8,128)(2,1)S(1)}, u32[]{:S(2)}, u32[]{:S(2)}) collective-permute-start(bf16[256,768]{1,0:T(8,128)(2,1)} %get-tuple-element.231), channel_id=1, source_target_pairs={{0,0},{1,1},{2,4},{3,5},{4,2},{5,3},{6,6},{7,7},{8,8},{9,9},{10,12... | collective-permute-start | bytes 1179656 | tf_op jit(solution)/shard_map/ppermute | solution.py:1425
  146.5 17.2 %collective-permute-start.40 = (bf16[256,768]{1,0:T(8,128)(2,1)}, bf16[256,768]{1,0:T(8,128)(2,1)S(1)}, u32[]{:S(2)}, u32[]{:S(2)}) collective-permute-start(bf16[256,768]{1,0:T(8,128)(2,1)} %get-tuple-element.232), channel_id=1, source_target_pairs={{0,1},{1,0},{2,5},{3,4},{4,3},{5,2},{6,7},{7,6},{8,9},{9,8},{10,13... | collective-permute-start | bytes 1179656 | tf_op jit(solution)/shard_map/ppermute | solution.py:1425
  188.2 16.7 %collective-permute-start.47 = (bf16[256,768]{1,0:T(8,128)(2,1)S(1)}, bf16[256,768]{1,0:T(8,128)(2,1)S(1)}, u32[]{:S(2)}, u32[]{:S(2)}) collective-permute-start(bf16[256,768]{1,0:T(8,128)(2,1)S(1)} %get-tuple-element.268), channel_id=1, source_target_pairs={{0,0},{1,1},{2,4},{3,5},{4,2},{5,3},{6,6},{7,7},{8,8},{9,9},{10,12... | collective-permute-start | bytes 1179656 | tf_op jit(solution)/shard_map/ppermute | solution.py:1425
  188.9 16.0 %collective-permute-start.48 = (bf16[256,768]{1,0:T(8,128)(2,1)S(1)}, bf16[256,768]{1,0:T(8,128)(2,1)S(1)}, u32[]{:S(2)}, u32[]{:S(2)}) collective-permute-start(bf16[256,768]{1,0:T(8,128)(2,1)S(1)} %get-tuple-element.269), channel_id=1, source_target_pairs={{0,1},{1,0},{2,5},{3,4},{4,3},{5,2},{6,7},{7,6},{8,9},{9,8},{10,13... | collective-permute-start | bytes 1179656 | tf_op jit(solution)/shard_map/ppermute | solution.py:1425
  191.5 13.4 %collective-permute-start.50 = (bf16[4,40,768]{2,1,0:T(8,128)(2,1)S(1)}, bf16[4,40,768]{2,1,0:T(8,128)(2,1)S(1)}, u32[]{:S(2)}, u32[]{:S(2)}) collective-permute-start(bf16[4,40,768]{2,1,0:T(8,128)(2,1)S(1)} %get-tuple-element.270), channel_id=1, source_target_pairs={{0,16},{4,20},{8,24},{12,28},{16,0},{20,4},{24,8},{28,12},{1,17},{... | collective-permute-start | bytes 737288 | tf_op jit(solution)/shard_map/ppermute | solution.py:523
  192.0 12.9 %collective-permute-start.49 = (bf16[4,40,768]{2,1,0:T(8,128)(2,1)S(1)}, bf16[4,40,768]{2,1,0:T(8,128)(2,1)S(1)}, u32[]{:S(2)}, u32[]{:S(2)}) collective-permute-start(bf16[4,40,768]{2,1,0:T(8,128)(2,1)S(1)} %get-tuple-element.270), channel_id=1, source_target_pairs={{0,8},{4,12},{8,0},{12,4},{16,24},{20,28},{24,16},{28,20},{1,9},{5... | collective-permute-start | bytes 737288 | tf_op jit(solution)/shard_map/ppermute | solution.py:523
  (84 other events, 1053.6 us)

commit v3 on v2

--- a/solution.py
+++ b/solution.py
@@ -1189,11 +1189,10 @@
     for copy in copies:
         copy.wait()
     in_all = jnp.concatenate([ref[0, 0] for ref in ins], axis=0)
-    for r, ref in enumerate(parts):
-        rows = pl.ds(pl.multiple_of(256 * ((meta[0] & 1) ^ r), 256), 256)
-        ref[...] = (
-            branch_ref[rows, :] + mm_nt(grads_ref[rows, :], weight[...]) + mm(rank_grad_ref[rows, :], in_all)
-        ).astype(BF)
+    result = (branch_ref[...] + mm_nt(grads_ref[...], weight[...]) + mm(rank_grad_ref[...], in_all)).astype(BF)
+    even = (meta[0] & 1) == 0
+    parts[0][...] = jnp.where(even, result[0:256], result[256:512])
+    parts[1][...] = jnp.where(even, result[256:512], result[0:256])
 
 
 def project_back(meta, ids, w_own, pieces, branch, grads, rank_grad, table_in):

time: 214 us -> 214 us (level)
  no operation moved by 1% of the time
where the time goes in v3:
time: 214 us; the launch traced here: 211 us
  Pallas kernels  100 us (47%)
  starting transfers between devices  51.6 us (24%)
  waiting for transfers between devices  44.1 us (21%)
  local copies, waits for them, and re-layouts  9.12 us (4%)
  other arithmetic  3.93 us (2%)
    pallas_call x1, Pallas kernels, second_half(): pl.pallas_call(second_half_kernel, grid_spec=pltpu.PrefetchScalarGridSpec...  29 us
    ppermute x13, waiting for transfers between devices, swap_chips(): return lax.ppermute(block, 'dp', [(i, i ^ offset) for i in range(dp_count)])  26.2 us
    ppermute x12, starting transfers between devices, swap_shards(): lax.ppermute(value, 'shard', [(i, i ^ step) for i in range(shard_count)])  17.2 us
    pallas_call x2, Pallas kernels, attend(): pl.pallas_call(attend_more_kernel if before else attend_kernel, grid=(pai...  16.7 us
    ppermute x13, starting transfers between devices, swap_chips(): return lax.ppermute(block, 'dp', [(i, i ^ offset) for i in range(dp_count)])  15.8 us
    pallas_call x1, Pallas kernels, first_half(): pl.pallas_call(first_half_kernel, grid_spec=pltpu.PrefetchScalarGridSpec(...  15.5 us
    pallas_call x1, Pallas kernels, attend_back(): pl.pallas_call(attend_back_kernel, grid=(width // 128,), in_specs=[half,...  15.4 us
    ppermute x20, starting transfers between devices, swap_cores(): return lax.ppermute(value, 'dp', [(i, i ^ 1) for i in range(dp_count)])  11.3 us
  transfers between devices with their start and end apart: 53, of which 18 were waited for; matrix products, arithmetic and copies ran while one was open for 3% of the time, Pallas kernels for 31%

profile of v3, /device:TPU:0, one launch (start us, length us, event | category | flops | bytes accessed | tf_op | source)
XLA Modules:
  0.0 210.9 jit_solution(16947883790782748555)
XLA Ops:
  1.6 5.1 %collective-permute-start.2 = (bf16[48,1152]{1,0:T(8,128)(2,1)S(1)}, bf16[48,1152]{1,0:T(8,128)(2,1)S(1)}, u32[]{:S(2)}, u32[]{:S(2)}) collective-permute-start(bf16[48,1152]{1,0:T(8,128)(2,1)S(1)} %dynamic_slice.33), channel_id=1, source_target_pairs={{0,3},{1,2},{2,1},{3,0},{4,7},{5,6},{6,5},{7,4},{8,11},{9,10},{10,... | collective-permute-start | bytes 331784 | tf_op jit(solution)/shard_map/ppermute | solution.py:514
  14.6 2.6 %collective-permute-done.1 = bf16[48,1152]{1,0:T(8,128)(2,1)S(1)} collective-permute-done((bf16[48,1152]{1,0:T(8,128)(2,1)S(1)}, bf16[48,1152]{1,0:T(8,128)(2,1)S(1)}, u32[]{:S(2)}, u32[]{:S(2)}) %collective-permute-start.1) | collective-permute-done | bytes 110624 | tf_op jit(solution)/shard_map/ppermute | solution.py:514
  17.3 2.4 %collective-permute-start.3 = (bf16[3,48,1152]{2,1,0:T(8,128)(2,1)S(1)}, bf16[3,48,1152]{2,1,0:T(8,128)(2,1)S(1)}, u32[]{:S(2)}, u32[]{:S(2)}) collective-permute-start(bf16[3,48,1152]{2,1,0:T(8,128)(2,1)S(1)} %pad_maximum_fusion.3.refs_5_.refs_1_), channel_id=1, source_target_pairs={{0,24},{4,28},{8,16},{12,20},{16,8},{20,12},{24,0},{28,4},{1,25},{... | collective-permute-start | bytes 995336 | tf_op jit(solution)/shard_map/ppermute | solution.py:523
  21.6 7.4 %collective-permute-done.3.refs_11_.refs_7_ = bf16[3,48,1152]{2,1,0:T(8,128)(2,1)S(1)} collective-permute-done((bf16[3,48,1152]{2,1,0:T(8,128)(2,1)S(1)}, bf16[3,48,1152]{2,1,0:T(8,128)(2,1)S(1)}, u32[]{:S(2)}, u32[]{:S(2)}) %collective-permute-start.3) | collective-permute-done | bytes 331808 | tf_op jit(solution)/shard_map/ppermute | solution.py:523
  29.7 6.4 %collective-permute-done.12.refs_9_.refs_5_ = bf16[3,48,1152]{2,1,0:T(8,128)(2,1)S(1)} collective-permute-done((bf16[3,48,1152]{2,1,0:T(8,128)(2,1)S(1)}, bf16[3,48,1152]{2,1,0:T(8,128)(2,1)S(1)}, u32[]{:S(2)}, u32[]{:S(2)}) %collective-permute-start.12) | collective-permute-done | bytes 331808 | tf_op jit(solution)/shard_map/ppermute | solution.py:523
  38.2 1.7 collective-permute-start.16
  39.9 2.3 %collective-permute-start.15 = (bf16[240,384]{1,0:T(8,128)(2,1)S(1)}, bf16[240,384]{1,0:T(8,128)(2,1)S(1)}, u32[]{:S(2)}, u32[]{:S(2)}) collective-permute-start(bf16[240,384]{1,0:T(8,128)(2,1)S(1)} %pad_maximum_fusion.5), channel_id=1, source_target_pairs={{0,1},{1,0},{2,3},{3,2},{4,5},{5,4},{6,7},{7,6},{8,9},{9,8},{10,11... | collective-permute-start | bytes 552968 | tf_op jit(solution)/shard_map/ppermute | solution.py:514
  42.1 10.6 %project_qkv.1 = (bf16[512,768]{1,0:T(8,128)(2,1)S(1)}, bf16[1024,768]{1,0:T(8,128)(2,1)}, bf16[1024,768]{1,0:T(8,128)(2,1)}, bf16[1024,128]{1,0:T(8,128)(2,1)S(...) custom-call(s32[2]{0:T(128)S(1)} %pad_add_fusion.meta, s32[6]{0:T(128)S(1)} %fusion.5.ids, ...), custom_call_target="tpu_custom_call" | custom-call | flops 1000000 | bytes 100000 | tf_op jit(solution)/shard_map/project_qkv/pallas_call | solution.py:705
  53.7 2.6 %collective-permute-done.16 = bf16[240,384]{1,0:T(8,128)(2,1)S(1)} collective-permute-done((bf16[240,384]{1,0:T(8,128)(2,1)S(1)}, bf16[240,384]{1,0:T(8,128)(2,1)S(1)}, u32[]{:S(2)}, u32[]{:S(2)}) %collective-permute-start.16) | collective-permute-done | bytes 184352 | tf_op jit(solution)/shard_map/ppermute | solution.py:514
  56.5 1.6 collective-permute-start.19
  59.6 1.7 collective-permute-start.21
  61.4 10.2 %attend.2 = (bf16[512,768]{1,0:T(8,128)(2,1)}, bf16[12,512,1024]{2,1,0:T(8,128)(2,1)}) custom-call(bf16[512,768]{1,0:T(8,128)(2,1)} %copy-done.8, bf16[1024,768]{1,0:T(8,128)(2,1)} %get-tuple-element.166.k_ref, bf16[1024,768]{1,0:T(8,128)(2,1)} %get-tuple-element.167.v_ref, bf16[1024,128]{1,0:T(8,128)(2,1)} %copy-done.37, bf16[512,128]{1,0:T(8,128)(2,1)} %copy-done.41, ...), custom_call_target="tpu_custom_call" | custom-call | flops 1000000 | bytes 100000 | tf_op jit(solution)/shard_map/attend/pallas_call | solution.py:779
  73.9 1.6 collective-permute-start.24
  76.6 6.4 %attend.3 = (bf16[512,768]{1,0:T(8,128)(2,1)}, bf16[12,512,1024]{2,1,0:T(8,128)(2,1)}) custom-call(bf16[512,768]{1,0:T(8,128)(2,1)} %copy-done.8, bf16[1024,768]{1,0:T(8,128)(2,1)} %get-tuple-element.166.k_ref, bf16[1024,768]{1,0:T(8,128)(2,1)} %get-tuple-element.167.v_ref, ...), custom_call_target="tpu_custom_call", output_to_operand_aliasing={{0}: (6, {}), {1}: (7, {})} | custom-call | flops 1000000 | bytes 100000 | tf_op jit(solution)/shard_map/attend/pallas_call | solution.py:779
  85.2 2.0 collective-permute-start.32
  91.0 15.5 %first_half.1 = (f32[512,768]{1,0:T(8,128)}, f32[512,128]{1,0:T(8,128)S(1)}, bf16[512,3072]{1,0:T(8,128)(2,1)}, bf16[512,3072]{1,0:T(8,128)(2,1)}) custom-call(s32[2]{0:T(128)S(1)} %pad_add_fusion.meta, s32[6]{0:T(128)S(1)} %fusion.5.ids, bf16[192,768]{1,0:T(8,128)(2,1)S(1)} %copy-done.20, bf16[192,3072]{1,0:T(8,128)(2,1)} %refs_3_.1, ...), custom_call_target="tpu_custom_call" | custom-call | flops 1000000 | bytes 100000 | tf_op jit(solution)/shard_map/first_half/pallas_call | solution.py:929
  107.4 4.0 %collective-permute-start.35 = (bf16[3,192,384]{2,1,0:T(8,128)(2,1)S(1)}, bf16[3,192,384]{2,1,0:T(8,128)(2,1)S(1)}, u32[]{:S(2)}, u32[]{:S(2)}) collective-permute-start(bf16[3,192,384]{2,1,0:T(8,128)(2,1)S(1)} %pad_maximum_fusion.2.refs_15_), channel_id=1, source_target_pairs={{0,4},{4,0},{8,12},{12,8},{16,20},{20,16},{24,28},{28,24},{1,5},{5... | collective-permute-start | bytes 1327112 | tf_op jit(solution)/shard_map/ppermute | solution.py:510
  115.6 29.0 %second_half.1 = (bf16[256,768]{1,0:T(8,128)(2,1)}, bf16[256,768]{1,0:T(8,128)(2,1)}, f32[512,768]{1,0:T(8,128)}, bf16[512,768]{1,0:T(8,128)(2,1)}, f32[4,24,768]{2,1,0:T(8,128)}, /*index=5*/bf16[4,24,768]{2,1,0:T(8,128)(2,1)}) custom-call(s32[2]{0:T(128)} %copy-done.44, s32[6]{0:T(128)} %copy-done.46, bf16[256,768]{1,0:T(8,128)(2,1)} %copy-done.59, ...), custom_call_target="tpu_custom_call" | custom-call | flops 1000000 | bytes 100000 | tf_op jit(solution)/shard_map/second_half/pallas_call | solution.py:1067
  144.7 1.8 collective-permute-start.39
  148.2 15.4 %attend_back.1 = (bf16[512,768]{1,0:T(8,128)(2,1)S(1)}, bf16[512,768]{1,0:T(8,128)(2,1)S(1)}, bf16[512,768]{1,0:T(8,128)(2,1)S(1)}, bf16[2,512,768]{2,1,0:T(8,128)(2,1)S(1)}) custom-call(bf16[512,768]{1,0:T(8,128)(2,1)S(1)} %copy-done.9, bf16[1024,768]{1,0:T(8,128)(2,1)S(1)} %copy-done.4, bf16[1024,768]{1,0:T(8,128)(2,1)S(1)} %copy-done.5, ...), custom_call_target="tpu_custom_call" | custom-call | flops 1000000 | bytes 100000 | tf_op jit(solution)/shard_map/attend_back/pallas_call | solution.py:833
  163.8 2.8 %collective-permute-start.41 = (bf16[2,512,768]{2,1,0:T(8,128)(2,1)S(1)}, bf16[2,512,768]{2,1,0:T(8,128)(2,1)S(1)}, u32[]{:S(2)}, u32[]{:S(2)}) collective-permute-start(bf16[2,512,768]{2,1,0:T(8,128)(2,1)S(1)} %get-tuple-element.240), channel_id=1, source_target_pairs={{0,4},{4,0},{8,12},{12,8},{16,20},{20,16},{24,28},{28,24},{1,5},{5... | collective-permute-start | bytes 4718600 | tf_op jit(solution)/shard_map/ppermute | solution.py:510
  166.6 3.0 %collective-permute-done.41.refs_4_ = bf16[2,512,768]{2,1,0:T(8,128)(2,1)S(1)} collective-permute-done((bf16[2,512,768]{2,1,0:T(8,128)(2,1)S(1)}, bf16[2,512,768]{2,1,0:T(8,128)(2,1)S(1)}, u32[]{:S(2)}, u32[]{:S(2)}) %collective-permute-start.41) | collective-permute-done | bytes 1572896 | tf_op jit(solution)/shard_map/ppermute | solution.py:510
  169.7 2.6 %first_grads.1 = (bf16[512,2304]{1,0:T(8,128)(2,1)S(1)}, bf16[512,48]{1,0:T(8,128)(2,1)S(1)}, f32[4,16,768]{2,1,0:T(8,128)S(1)}, bf16[4,16,768]{2,1,0:T(8,128)(2,1)S(1)}) custom-call(s32[2]{0:T(128)S(1)} %copy-done.45, s32[6]{0:T(128)S(1)} %copy-done.47, bf16[512,768]{1,0:T(8,128)(2,1)S(1)} %copy-done.15, bf16[512,768]{1,0:T(8,128)(2,1)S(1)} %get-tuple-element.237.refs_1_, ...), custom_call_target="tpu_custom_call" | custom-call | flops 1000000 | bytes 100000 | tf_op jit(solution)/shard_map/first_grads/pallas_call | solution.py:1158
  173.0 4.1 %project_back.1 = (bf16[256,768]{1,0:T(8,128)(2,1)S(1)}, bf16[256,768]{1,0:T(8,128)(2,1)S(1)}) custom-call(s32[2]{0:T(128)S(1)} %copy-done.45, s32[6]{0:T(128)S(1)} %copy-done.47, bf16[192,2304]{1,0:T(8,128)(2,1)S(1)} %copy-done.11, bf16[3,48,1152]{2,1,0:T(8,128)(2,1)S(1)} %pad_maximum_fusion.3.refs_5_.refs_1_, bf16[3,48,1152]{2,1,0:T(8,128)(2,1)S(1)} %copy-done.28, ...), custom_call_target="tpu_custom_call" | custom-call | flops 1000000 | bytes 100000 | tf_op jit(solution)/shard_map/project_back/pallas_call | solution.py:1200
  177.7 2.2 %collective-permute-start.44 = (bf16[40,768]{1,0:T(8,128)(2,1)S(1)}, bf16[40,768]{1,0:T(8,128)(2,1)S(1)}, u32[]{:S(2)}, u32[]{:S(2)}) collective-permute-start(bf16[40,768]{1,0:T(8,128)(2,1)S(1)} %get-tuple-element.258), channel_id=1, source_target_pairs={{0,1},{1,0},{2,3},{3,2},{4,5},{5,4},{6,7},{7,6},{8,9},{9,8},{10,11... | collective-permute-start | bytes 184328 | tf_op jit(solution)/shard_map/ppermute | solution.py:514
  179.9 2.2 %collective-permute-start.45 = (bf16[40,768]{1,0:T(8,128)(2,1)S(1)}, bf16[40,768]{1,0:T(8,128)(2,1)S(1)}, u32[]{:S(2)}, u32[]{:S(2)}) collective-permute-start(bf16[40,768]{1,0:T(8,128)(2,1)S(1)} %get-tuple-element.259), channel_id=1, source_target_pairs={{0,2},{1,3},{2,0},{3,1},{4,6},{5,7},{6,4},{7,5},{8,10},{9,11},{10,... | collective-permute-start | bytes 184328 | tf_op jit(solution)/shard_map/ppermute | solution.py:514
  183.8 3.3 %collective-permute-done.45 = bf16[40,768]{1,0:T(8,128)(2,1)S(1)} collective-permute-done((bf16[40,768]{1,0:T(8,128)(2,1)S(1)}, bf16[40,768]{1,0:T(8,128)(2,1)S(1)}, u32[]{:S(2)}, u32[]{:S(2)}) %collective-permute-start.45) | collective-permute-done | bytes 61472 | tf_op jit(solution)/shard_map/ppermute | solution.py:514
  192.0 1.5 collective-permute-start.49
  193.5 4.3 %collective-permute-done.51 = bf16[4,40,768]{2,1,0:T(8,128)(2,1)S(1)} collective-permute-done((bf16[4,40,768]{2,1,0:T(8,128)(2,1)S(1)}, bf16[4,40,768]{2,1,0:T(8,128)(2,1)S(1)}, u32[]{:S(2)}, u32[]{:S(2)}) %collective-permute-start.51) | collective-permute-done | bytes 245792 | tf_op jit(solution)/shard_map/ppermute | solution.py:523
  197.8 7.1 %collective-permute-done.50 = bf16[4,40,768]{2,1,0:T(8,128)(2,1)S(1)} collective-permute-done((bf16[4,40,768]{2,1,0:T(8,128)(2,1)S(1)}, bf16[4,40,768]{2,1,0:T(8,128)(2,1)S(1)}, u32[]{:S(2)}, u32[]{:S(2)}) %collective-permute-start.50) | collective-permute-done | bytes 245792 | tf_op jit(solution)/shard_map/ppermute | solution.py:523
  206.1 1.8 join_parts.3
  208.1 2.7 %combine.1 = (f32[5,8,16,192]{3,2,1,0:T(8,128)}, f32[8,16,768]{2,1,0:T(8,128)}, f32[5,8,16,192]{3,2,1,0:T(8,128)}, f32[8,16,768]{2,1,0:T(8,128)}) custom-call(s32[96]{0:T(128)S(1)} %reshape.102.ids, s32[2]{0:T(128)S(1)} %copy-done.45, bf16[4,4,40,768]{3,2,1,0:T(8,128)(2,1)S(1)} %pad_maximum_fusion.own, bf16[4,4,40,768]{3,2,1,0:T(8,128)(2,1)S(1)} %collective-permute-done.52.other), custom_call_target="tpu_custom_call" | custom-call | flops 1000000 | bytes 100000 | tf_op jit(solution)/shard_map/combine/pallas_call | solution.py:1271
  (246 shorter events, 41.1 us)
Async XLA Ops:
  1.6 12.4 %collective-permute-start.2 = (bf16[48,1152]{1,0:T(8,128)(2,1)S(1)}, bf16[48,1152]{1,0:T(8,128)(2,1)S(1)}, u32[]{:S(2)}, u32[]{:S(2)}) collective-permute-start(bf16[48,1152]{1,0:T(8,128)(2,1)S(1)} %dynamic_slice.33), channel_id=1, source_target_pairs={{0,3},{1,2},{2,1},{3,0},{4,7},{5,6},{6,5},{7,4},{8,11},{9,10},{10,... | collective-permute-start | bytes 331784 | tf_op jit(solution)/shard_map/ppermute | solution.py:514
  6.7 10.6 %collective-permute-start.1 = (bf16[48,1152]{1,0:T(8,128)(2,1)S(1)}, bf16[48,1152]{1,0:T(8,128)(2,1)S(1)}, u32[]{:S(2)}, u32[]{:S(2)}) collective-permute-start(bf16[48,1152]{1,0:T(8,128)(2,1)S(1)} %dynamic_slice.33), channel_id=1, source_target_pairs={{0,2},{1,3},{2,0},{3,1},{4,6},{5,7},{6,4},{7,5},{8,10},{9,11},{10,... | collective-permute-start | bytes 331784 | tf_op jit(solution)/shard_map/ppermute | solution.py:514
  6.7 10.6 %collective-permute-start = (bf16[48,1152]{1,0:T(8,128)(2,1)S(1)}, bf16[48,1152]{1,0:T(8,128)(2,1)S(1)}, u32[]{:S(2)}, u32[]{:S(2)}) collective-permute-start(bf16[48,1152]{1,0:T(8,128)(2,1)S(1)} %dynamic_slice.33), channel_id=1, source_target_pairs={{0,1},{1,0},{2,3},{3,2},{4,5},{5,4},{6,7},{7,6},{8,9},{9,8},{10,11... | collective-permute-start | bytes 331784 | tf_op jit(solution)/shard_map/ppermute | solution.py:514
  7.3 13.7 %collective-permute-start.4 = (s32[2,6]{1,0:T(2,128)}, s32[2,6]{1,0:T(2,128)S(1)}, u32[]{:S(2)}, u32[]{:S(2)}) collective-permute-start(s32[2,6]{1,0:T(2,128)} %param.18), channel_id=1, source_target_pairs={{0,4},{4,0},{8,12},{12,8},{16,20},{20,16},{24,28},{28,24},{1,5},{5... | collective-permute-start | bytes 152 | tf_op jit(solution)/shard_map/ppermute | solution.py:510
  9.3 27.3 %collective-permute-start.6 = (bf16[272,768]{1,0:T(8,128)(2,1)S(1)}, bf16[272,768]{1,0:T(8,128)(2,1)S(1)}, u32[]{:S(2)}, u32[]{:S(2)}) collective-permute-start(bf16[272,768]{1,0:T(8,128)(2,1)S(1)} %get-tuple-element.286), channel_id=1, source_target_pairs={{0,1},{1,0},{2,5},{3,4},{4,3},{5,2},{6,7},{7,6},{8,9},{9,8},{10,13... | collective-permute-start | bytes 1253384 | tf_op jit(solution)/shard_map/ppermute | solution.py:558
  14.0 22.8 %collective-permute-start.5 = (bf16[272,768]{1,0:T(8,128)(2,1)S(1)}, bf16[272,768]{1,0:T(8,128)(2,1)S(1)}, u32[]{:S(2)}, u32[]{:S(2)}) collective-permute-start(bf16[272,768]{1,0:T(8,128)(2,1)S(1)} %get-tuple-element.287), channel_id=1, source_target_pairs={{0,0},{1,1},{2,4},{3,5},{4,2},{5,3},{6,6},{7,7},{8,8},{9,9},{10,12... | collective-permute-start | bytes 1253384 | tf_op jit(solution)/shard_map/ppermute | solution.py:558
  17.3 11.6 %collective-permute-start.3 = (bf16[3,48,1152]{2,1,0:T(8,128)(2,1)S(1)}, bf16[3,48,1152]{2,1,0:T(8,128)(2,1)S(1)}, u32[]{:S(2)}, u32[]{:S(2)}) collective-permute-start(bf16[3,48,1152]{2,1,0:T(8,128)(2,1)S(1)} %pad_maximum_fusion.3.refs_5_.refs_1_), channel_id=1, source_target_pairs={{0,24},{4,28},{8,16},{12,20},{16,8},{20,12},{24,0},{28,4},{1,25},{... | collective-permute-start | bytes 995336 | tf_op jit(solution)/shard_map/ppermute | solution.py:523
  20.5 15.6 %collective-permute-start.12 = (bf16[3,48,1152]{2,1,0:T(8,128)(2,1)S(1)}, bf16[3,48,1152]{2,1,0:T(8,128)(2,1)S(1)}, u32[]{:S(2)}, u32[]{:S(2)}) collective-permute-start(bf16[3,48,1152]{2,1,0:T(8,128)(2,1)S(1)} %pad_maximum_fusion.3.refs_5_.refs_1_), channel_id=1, source_target_pairs={{0,16},{4,20},{8,24},{12,28},{16,0},{20,4},{24,8},{28,12},{1,17},{... | collective-permute-start | bytes 995336 | tf_op jit(solution)/shard_map/ppermute | solution.py:523
  21.0 15.2 %collective-permute-start.10 = (bf16[3,48,1152]{2,1,0:T(8,128)(2,1)S(1)}, bf16[3,48,1152]{2,1,0:T(8,128)(2,1)S(1)}, u32[]{:S(2)}, u32[]{:S(2)}) collective-permute-start(bf16[3,48,1152]{2,1,0:T(8,128)(2,1)S(1)} %pad_maximum_fusion.3.refs_5_.refs_1_), channel_id=1, source_target_pairs={{0,8},{4,12},{8,0},{12,4},{16,24},{20,28},{24,16},{28,20},{1,9},{5... | collective-permute-start | bytes 995336 | tf_op jit(solution)/shard_map/ppermute | solution.py:523
  37.7 16.0 %collective-permute-start.17 = (bf16[240,384]{1,0:T(8,128)(2,1)S(1)}, bf16[240,384]{1,0:T(8,128)(2,1)S(1)}, u32[]{:S(2)}, u32[]{:S(2)}) collective-permute-start(bf16[240,384]{1,0:T(8,128)(2,1)S(1)} %pad_maximum_fusion.5), channel_id=1, source_target_pairs={{0,3},{1,2},{2,1},{3,0},{4,7},{5,6},{6,5},{7,4},{8,11},{9,10},{10,... | collective-permute-start | bytes 552968 | tf_op jit(solution)/shard_map/ppermute | solution.py:514
  38.2 18.2 %collective-permute-start.16 = (bf16[240,384]{1,0:T(8,128)(2,1)S(1)}, bf16[240,384]{1,0:T(8,128)(2,1)S(1)}, u32[]{:S(2)}, u32[]{:S(2)}) collective-permute-start(bf16[240,384]{1,0:T(8,128)(2,1)S(1)} %pad_maximum_fusion.5), channel_id=1, source_target_pairs={{0,2},{1,3},{2,0},{3,1},{4,6},{5,7},{6,4},{7,5},{8,10},{9,11},{10,... | collective-permute-start | bytes 552968 | tf_op jit(solution)/shard_map/ppermute | solution.py:514
  39.9 16.5 %collective-permute-start.15 = (bf16[240,384]{1,0:T(8,128)(2,1)S(1)}, bf16[240,384]{1,0:T(8,128)(2,1)S(1)}, u32[]{:S(2)}, u32[]{:S(2)}) collective-permute-start(bf16[240,384]{1,0:T(8,128)(2,1)S(1)} %pad_maximum_fusion.5), channel_id=1, source_target_pairs={{0,1},{1,0},{2,3},{3,2},{4,5},{5,4},{6,7},{7,6},{8,9},{9,8},{10,11... | collective-permute-start | bytes 552968 | tf_op jit(solution)/shard_map/ppermute | solution.py:514
  56.5 15.2 %collective-permute-start.20 = (bf16[3,240,384]{2,1,0:T(8,128)(2,1)S(1)}, bf16[3,240,384]{2,1,0:T(8,128)(2,1)S(1)}, u32[]{:S(2)}, u32[]{:S(2)}) collective-permute-start(bf16[3,240,384]{2,1,0:T(8,128)(2,1)S(1)} %pad_maximum_fusion.1.refs_2_.refs_5_), channel_id=1, source_target_pairs={{0,4},{4,0},{8,12},{12,8},{16,20},{20,16},{24,28},{28,24},{1,5},{5... | collective-permute-start | bytes 1658888 | tf_op jit(solution)/shard_map/ppermute | solution.py:510
  56.5 15.1 %collective-permute-start.19 = (bf16[3,240,384]{2,1,0:T(8,128)(2,1)S(1)}, bf16[3,240,384]{2,1,0:T(8,128)(2,1)S(1)}, u32[]{:S(2)}, u32[]{:S(2)}) collective-permute-start(bf16[3,240,384]{2,1,0:T(8,128)(2,1)S(1)} %pad_maximum_fusion.1.refs_2_.refs_5_), channel_id=1, source_target_pairs={{0,16},{4,20},{8,24},{12,28},{16,0},{20,4},{24,8},{28,12},{1,17},{... | collective-permute-start | bytes 1658888 | tf_op jit(solution)/shard_map/ppermute | solution.py:523
  58.1 14.6 %collective-permute-start.18 = (bf16[3,240,384]{2,1,0:T(8,128)(2,1)S(1)}, bf16[3,240,384]{2,1,0:T(8,128)(2,1)S(1)}, u32[]{:S(2)}, u32[]{:S(2)}) collective-permute-start(bf16[3,240,384]{2,1,0:T(8,128)(2,1)S(1)} %pad_maximum_fusion.1.refs_2_.refs_5_), channel_id=1, source_target_pairs={{0,8},{4,12},{8,0},{12,4},{16,24},{20,28},{24,16},{28,20},{1,9},{5... | collective-permute-start | bytes 1658888 | tf_op jit(solution)/shard_map/ppermute | solution.py:523
  59.6 12.0 %collective-permute-start.22 = (bf16[192,384]{1,0:T(8,128)(2,1)}, bf16[192,384]{1,0:T(8,128)(2,1)S(1)}, u32[]{:S(2)}, u32[]{:S(2)}) collective-permute-start(bf16[192,384]{1,0:T(8,128)(2,1)} %pad_maximum_fusion.6), channel_id=1, source_target_pairs={{0,2},{1,3},{2,0},{3,1},{4,6},{5,7},{6,4},{7,5},{8,10},{9,11},{10,... | collective-permute-start | bytes 442376 | tf_op jit(solution)/shard_map/ppermute | solution.py:514
  59.6 12.0 %collective-permute-start.21 = (bf16[192,384]{1,0:T(8,128)(2,1)}, bf16[192,384]{1,0:T(8,128)(2,1)S(1)}, u32[]{:S(2)}, u32[]{:S(2)}) collective-permute-start(bf16[192,384]{1,0:T(8,128)(2,1)} %pad_maximum_fusion.6), channel_id=1, source_target_pairs={{0,1},{1,0},{2,3},{3,2},{4,5},{5,4},{6,7},{7,6},{8,9},{9,8},{10,11... | collective-permute-start | bytes 442376 | tf_op jit(solution)/shard_map/ppermute | solution.py:514
  72.7 10.4 %collective-permute-start.25 = (bf16[3,240,384]{2,1,0:T(8,128)(2,1)S(1)}, bf16[3,240,384]{2,1,0:T(8,128)(2,1)S(1)}, u32[]{:S(2)}, u32[]{:S(2)}) collective-permute-start(bf16[3,240,384]{2,1,0:T(8,128)(2,1)S(1)} %collective-permute-done.18.refs_4_.refs_7_), channel_id=1, source_target_pairs={{0,4},{4,0},{8,12},{12,8},{16,20},{20,16},{24,28},{28,24},{1,5},{5... | collective-permute-start | bytes 1658888 | tf_op jit(solution)/shard_map/ppermute | solution.py:510
  72.7 10.4 %collective-permute-start.26 = (bf16[3,240,384]{2,1,0:T(8,128)(2,1)S(1)}, bf16[3,240,384]{2,1,0:T(8,128)(2,1)S(1)}, u32[]{:S(2)}, u32[]{:S(2)}) collective-permute-start(bf16[3,240,384]{2,1,0:T(8,128)(2,1)S(1)} %collective-permute-done.19.refs_6_.refs_9_), channel_id=1, source_target_pairs={{0,4},{4,0},{8,12},{12,8},{16,20},{20,16},{24,28},{28,24},{1,5},{5... | collective-permute-start | bytes 1658888 | tf_op jit(solution)/shard_map/ppermute | solution.py:510
  73.3 9.9 %collective-permute-start.23 = (bf16[3,128,384]{2,1,0:T(8,128)(2,1)S(1)}, bf16[3,128,384]{2,1,0:T(8,128)(2,1)S(1)}, u32[]{:S(2)}, u32[]{:S(2)}) collective-permute-start(bf16[3,128,384]{2,1,0:T(8,128)(2,1)S(1)} %slice.41), channel_id=1, source_target_pairs={{0,16},{4,20},{8,24},{12,28},{16,0},{20,4},{24,8},{28,12},{1,17},{... | collective-permute-start | bytes 884744 | tf_op jit(solution)/shard_map/ppermute | solution.py:523
  73.9 9.2 %collective-permute-start.24 = (bf16[3,112,384]{2,1,0:T(8,128)(2,1)S(1)}, bf16[3,112,384]{2,1,0:T(8,128)(2,1)S(1)}, u32[]{:S(2)}, u32[]{:S(2)}) collective-permute-start(bf16[3,112,384]{2,1,0:T(8,128)(2,1)S(1)} %slice.42), channel_id=1, source_target_pairs={{0,8},{4,12},{8,0},{12,4},{16,24},{20,28},{24,16},{28,20},{1,9},{5... | collective-permute-start | bytes 774152 | tf_op jit(solution)/shard_map/ppermute | solution.py:523
  85.2 26.2 %collective-permute-start.32 = (bf16[3,192,384]{2,1,0:T(8,128)(2,1)S(1)}, bf16[3,192,384]{2,1,0:T(8,128)(2,1)S(1)}, u32[]{:S(2)}, u32[]{:S(2)}) collective-permute-start(bf16[3,192,384]{2,1,0:T(8,128)(2,1)S(1)} %pad_maximum_fusion.2.refs_15_), channel_id=1, source_target_pairs={{0,24},{4,28},{8,16},{12,20},{16,8},{20,12},{24,0},{28,4},{1,25},{... | collective-permute-start | bytes 1327112 | tf_op jit(solution)/shard_map/ppermute | solution.py:523
  87.3 24.2 %collective-permute-start.31 = (bf16[3,192,384]{2,1,0:T(8,128)(2,1)S(1)}, bf16[3,192,384]{2,1,0:T(8,128)(2,1)S(1)}, u32[]{:S(2)}, u32[]{:S(2)}) collective-permute-start(bf16[3,192,384]{2,1,0:T(8,128)(2,1)S(1)} %pad_maximum_fusion.2.refs_15_), channel_id=1, source_target_pairs={{0,16},{4,20},{8,24},{12,28},{16,0},{20,4},{24,8},{28,12},{1,17},{... | collective-permute-start | bytes 1327112 | tf_op jit(solution)/shard_map/ppermute | solution.py:523
  87.8 23.7 %collective-permute-start.30 = (bf16[3,192,384]{2,1,0:T(8,128)(2,1)S(1)}, bf16[3,192,384]{2,1,0:T(8,128)(2,1)S(1)}, u32[]{:S(2)}, u32[]{:S(2)}) collective-permute-start(bf16[3,192,384]{2,1,0:T(8,128)(2,1)S(1)} %pad_maximum_fusion.2.refs_15_), channel_id=1, source_target_pairs={{0,8},{4,12},{8,0},{12,4},{16,24},{20,28},{24,16},{28,20},{1,9},{5... | collective-permute-start | bytes 1327112 | tf_op jit(solution)/shard_map/ppermute | solution.py:523
  88.8 18.5 %collective-permute-start.34 = (bf16[256,768]{1,0:T(8,128)(2,1)S(1)}, bf16[256,768]{1,0:T(8,128)(2,1)S(1)}, u32[]{:S(2)}, u32[]{:S(2)}) collective-permute-start(bf16[256,768]{1,0:T(8,128)(2,1)S(1)} %get-tuple-element.288), channel_id=1, source_target_pairs={{0,1},{1,0},{2,5},{3,4},{4,3},{5,2},{6,7},{7,6},{8,9},{9,8},{10,13... | collective-permute-start | bytes 1179656 | tf_op jit(solution)/shard_map/ppermute | solution.py:558
  88.9 22.5 %collective-permute-start.33 = (bf16[256,768]{1,0:T(8,128)(2,1)S(1)}, bf16[256,768]{1,0:T(8,128)(2,1)S(1)}, u32[]{:S(2)}, u32[]{:S(2)}) collective-permute-start(bf16[256,768]{1,0:T(8,128)(2,1)S(1)} %get-tuple-element.289), channel_id=1, source_target_pairs={{0,0},{1,1},{2,4},{3,5},{4,2},{5,3},{6,6},{7,7},{8,8},{9,9},{10,12... | collective-permute-start | bytes 1179656 | tf_op jit(solution)/shard_map/ppermute | solution.py:558
  144.7 19.0 %collective-permute-start.39 = (bf16[256,768]{1,0:T(8,128)(2,1)}, bf16[256,768]{1,0:T(8,128)(2,1)S(1)}, u32[]{:S(2)}, u32[]{:S(2)}) collective-permute-start(bf16[256,768]{1,0:T(8,128)(2,1)} %get-tuple-element.231), channel_id=1, source_target_pairs={{0,0},{1,1},{2,4},{3,5},{4,2},{5,3},{6,6},{7,7},{8,8},{9,9},{10,12... | collective-permute-start | bytes 1179656 | tf_op jit(solution)/shard_map/ppermute | solution.py:1424
  146.5 17.2 %collective-permute-start.40 = (bf16[256,768]{1,0:T(8,128)(2,1)}, bf16[256,768]{1,0:T(8,128)(2,1)S(1)}, u32[]{:S(2)}, u32[]{:S(2)}) collective-permute-start(bf16[256,768]{1,0:T(8,128)(2,1)} %get-tuple-element.232), channel_id=1, source_target_pairs={{0,1},{1,0},{2,5},{3,4},{4,3},{5,2},{6,7},{7,6},{8,9},{9,8},{10,13... | collective-permute-start | bytes 1179656 | tf_op jit(solution)/shard_map/ppermute | solution.py:1424
  188.2 16.7 %collective-permute-start.47 = (bf16[256,768]{1,0:T(8,128)(2,1)S(1)}, bf16[256,768]{1,0:T(8,128)(2,1)S(1)}, u32[]{:S(2)}, u32[]{:S(2)}) collective-permute-start(bf16[256,768]{1,0:T(8,128)(2,1)S(1)} %get-tuple-element.268), channel_id=1, source_target_pairs={{0,0},{1,1},{2,4},{3,5},{4,2},{5,3},{6,6},{7,7},{8,8},{9,9},{10,12... | collective-permute-start | bytes 1179656 | tf_op jit(solution)/shard_map/ppermute | solution.py:1424
  188.9 16.0 %collective-permute-start.48 = (bf16[256,768]{1,0:T(8,128)(2,1)S(1)}, bf16[256,768]{1,0:T(8,128)(2,1)S(1)}, u32[]{:S(2)}, u32[]{:S(2)}) collective-permute-start(bf16[256,768]{1,0:T(8,128)(2,1)S(1)} %get-tuple-element.269), channel_id=1, source_target_pairs={{0,1},{1,0},{2,5},{3,4},{4,3},{5,2},{6,7},{7,6},{8,9},{9,8},{10,13... | collective-permute-start | bytes 1179656 | tf_op jit(solution)/shard_map/ppermute | solution.py:1424
  191.5 13.4 %collective-permute-start.50 = (bf16[4,40,768]{2,1,0:T(8,128)(2,1)S(1)}, bf16[4,40,768]{2,1,0:T(8,128)(2,1)S(1)}, u32[]{:S(2)}, u32[]{:S(2)}) collective-permute-start(bf16[4,40,768]{2,1,0:T(8,128)(2,1)S(1)} %get-tuple-element.270), channel_id=1, source_target_pairs={{0,16},{4,20},{8,24},{12,28},{16,0},{20,4},{24,8},{28,12},{1,17},{... | collective-permute-start | bytes 737288 | tf_op jit(solution)/shard_map/ppermute | solution.py:523
  192.0 12.9 %collective-permute-start.49 = (bf16[4,40,768]{2,1,0:T(8,128)(2,1)S(1)}, bf16[4,40,768]{2,1,0:T(8,128)(2,1)S(1)}, u32[]{:S(2)}, u32[]{:S(2)}) collective-permute-start(bf16[4,40,768]{2,1,0:T(8,128)(2,1)S(1)} %get-tuple-element.270), channel_id=1, source_target_pairs={{0,8},{4,12},{8,0},{12,4},{16,24},{20,28},{24,16},{28,20},{1,9},{5... | collective-permute-start | bytes 737288 | tf_op jit(solution)/shard_map/ppermute | solution.py:523
  (84 other events, 1053.5 us)
